TPU v7x, 512 devices: a whole 4x8x8 slice. The times are simulated.
512 devices in a mesh: section: 32 (over y_lo, x, core), dp: 16 (over y_hi, z).
Axes of the slice: x: 4, y: 8 (y_hi: 2, y_lo: 4; y = y_hi * 4 + y_lo), z: 8, core: 2. Of those that a mesh axis runs over, the one named last changes fastest.
Arguments:
- down_in: bfloat16 [32, 512, 8192], P('section', None, 'dp'), may hold values from -8 to 8
- up_in: bfloat16 [32, 512, 8192], P('section', None, 'dp'), may hold values from -8 to 8
- down_cot: bfloat16 [32, 512, 8192], P('section', None, 'dp'), may hold values from -0.03125 to 0.03125
- up_cot: bfloat16 [32, 512, 8192], P('section', None, 'dp'), may hold values from -0.03125 to 0.03125
- adapt_a: bfloat16 [32, 8192, 32], P('section', 'dp'), may hold values from -0.0625 to 0.0625
- adapt_b: bfloat16 [32, 32, 8192], P('section', None, 'dp'), may hold values from -1 to 1
- head_gain: float32 [4, 8192], replicated, may hold values from 0.5 to 1.5
- cand: bfloat16 [32, 8192], replicated, may hold values from -3 to 3
- down_ids: int32 [512], replicated, may hold values from 0 to 31
- up_ids: int32 [512], replicated, may hold values from 0 to 31
- offsets: int32 [4], replicated, may hold values from 1 to 4
- loss_weights: int32 [4], replicated, may hold values from 1 to 4
Outputs:
- down_next: bfloat16 [32, 512, 8192], P('section', None, 'dp')
- up_next: bfloat16 [32, 512, 8192], P('section', None, 'dp')
- down_back: bfloat16 [32, 512, 8192], P('section', None, 'dp')
- up_back: bfloat16 [32, 512, 8192], P('section', None, 'dp')
- grad_a: float32 [32, 8192, 32], P('section', 'dp')
- grad_b: float32 [32, 32, 8192], P('section', None, 'dp')
- loss: float32 [1], replicated
All inputs are finite; a program needn't handle non-finite values.
Results may differ from a plain program's by a relative error of at most 0.005.
Values may be sent and summed in bfloat16 or wider, within the bound.
No kernel may reach another device: no remote copies, remote signals or barrier semaphores. Data moves between devices by JAX's collectives and lax.ppermute only.
A program may use at most 64 MiB of HBM per device.

v0:
```python
import jax
import jax.numpy as jnp
from jax import lax
from jax.sharding import PartitionSpec as P

EPS = 1e-05
HIGH = lax.Precision.HIGHEST


def swapped(block, axis, distance):
    count = lax.axis_size(axis)
    route = []
    for low in range(count):
        high = low | 1 << distance
        if high != low and high < count:
            route += [(low, high), (high, low)]
    return lax.ppermute(block, axis, route)


def from_behind(block, axis, distance):
    devices = range(lax.axis_size(axis))
    route = [(i - distance, i) for i in devices if i - distance in devices]
    return lax.ppermute(block, axis, route)


def logit_loss(logits, ids, offsets, loss_weights, groups):
    heads, tokens, classes_n = logits.shape
    rows = tokens // groups
    shaped = logits.reshape(heads, groups, rows, classes_n)
    id_rows = ids.reshape(groups, rows)
    classes = jnp.arange(classes_n, dtype=jnp.int32)
    places = jnp.arange(rows, dtype=jnp.int32)
    weight_sum = jnp.sum(loss_weights).astype(jnp.float32)
    total = jnp.float32(0.0)
    for head in range(heads):
        current = shaped[head]
        ahead = places + offsets[head]
        valid = ahead < rows
        target = jnp.take(id_rows, jnp.clip(ahead, 0, rows - 1), axis=1)
        picked = jnp.sum(jnp.where(target[..., None] == classes, current, 0.0), axis=-1)
        entropy = jax.nn.logsumexp(current, axis=-1) - picked
        count = (rows - offsets[head]).astype(jnp.float32)
        total = (
            total
            + loss_weights[head].astype(jnp.float32)
            / weight_sum
            * jnp.sum(jnp.where(valid[None, :], entropy, 0.0))
            / count
        )
    return total / groups


def mirror_weights(first, second, levels):
    for level in range(levels):
        first, second = swapped((first, second), "section", level)
    return (first, second)


def mirror_grads(first, second, levels):
    for level in range(levels):
        first, second = (
            swapped(first.astype(jnp.bfloat16), "section", level).astype(first.dtype),
            swapped(second.astype(jnp.bfloat16), "section", level).astype(second.dtype),
        )
    return (first, second)


def head_partial(outputs, gain_part, cand_part):
    squares = jnp.sum(outputs * outputs, axis=-1)
    scaled = outputs[None] * gain_part[:, None, :]
    partial_value = jnp.einsum("ktd,cd->ktc", scaled, cand_part, precision=HIGH)
    return (squares, partial_value)


def head_backward(outputs, squares, partial_value, grad_logits, gain_part, cand_part, width):
    scale = lax.rsqrt(squares / width + EPS)
    d_partial = grad_logits * scale[None, :, None]
    d_scale = jnp.sum(grad_logits * partial_value, axis=(0, 2))
    back = jnp.einsum("ktc,cd->ktd", d_partial, cand_part, precision=HIGH)
    d_out = jnp.sum(back * gain_part[:, None, :], axis=0)
    return d_out - (d_scale * scale * scale * scale / width)[:, None] * outputs


def section_backward(inputs, proj_a, cotan, scale, projected, pre, dg, width):
    sigma = jax.nn.sigmoid(pre)
    d_pre = dg * sigma * (1.0 + pre * (1.0 - sigma))
    d_scaled = d_pre * scale
    grad_a = jnp.dot(inputs.T, d_scaled, precision=HIGH)
    d_scale = jnp.sum(d_pre * projected, axis=-1, keepdims=True)
    d_in = (
        cotan
        + jnp.dot(d_scaled, proj_a.T, precision=HIGH)
        - d_scale * scale * scale * scale / width * inputs
    )
    return (d_in, grad_a)


def shards(
    down_in,
    up_in,
    down_cot,
    up_cot,
    adapt_a,
    adapt_b,
    head_gain,
    cand,
    down_ids,
    up_ids,
    offsets,
    loss_weights,
):
    sections = lax.axis_size("section")
    groups = lax.axis_size("dp")
    levels = sections.bit_length() - 1
    position = lax.axis_index("section")
    width = head_gain.shape[1]
    local_width = down_in.shape[2]
    first_col = lax.axis_index("dp") * local_width
    far_a, far_b = mirror_weights(adapt_a, adapt_b, levels)
    far_a = far_a[0]
    far_b = far_b[0]
    x_d = down_in[0].astype(jnp.float32)
    x_u = up_in[0].astype(jnp.float32)
    a_d = adapt_a[0].astype(jnp.float32)
    b_d = adapt_b[0].astype(jnp.float32)
    a_u = far_a.astype(jnp.float32)
    b_u = far_b.astype(jnp.float32)
    sq_d = jnp.sum(x_d * x_d, axis=-1, keepdims=True)
    sq_u = jnp.sum(x_u * x_u, axis=-1, keepdims=True)
    xa_d = jnp.dot(x_d, a_d, precision=HIGH)
    xa_u = jnp.dot(x_u, a_u, precision=HIGH)
    sq_d, xa_d, sq_u, xa_u = lax.psum((sq_d, xa_d, sq_u, xa_u), "dp")
    scale_d = lax.rsqrt(sq_d / width + EPS)
    scale_u = lax.rsqrt(sq_u / width + EPS)
    pre_d = scale_d * xa_d
    pre_u = scale_u * xa_u
    act_d = jax.nn.silu(pre_d)
    act_u = jax.nn.silu(pre_u)
    y_d = x_d + jnp.dot(act_d, b_d, precision=HIGH)
    y_u = x_u + jnp.dot(act_u, b_u, precision=HIGH)
    out_d = y_d.astype(jnp.bfloat16)[None]
    out_u = y_u.astype(jnp.bfloat16)[None]
    down_next = from_behind(out_d, "section", 1)
    up_next = from_behind(out_u, "section", -1)
    gain_part = lax.dynamic_slice_in_dim(head_gain, first_col, local_width, 1)
    cand_part = lax.dynamic_slice_in_dim(cand, first_col, local_width, 1).astype(jnp.float32)
    final_d = out_d[0].astype(jnp.float32)
    final_u = out_u[0].astype(jnp.float32)
    hsq_d, part_d = head_partial(final_d, gain_part, cand_part)
    hsq_u, part_u = head_partial(final_u, gain_part, cand_part)
    hsq_d, part_d, hsq_u, part_u = (
        lax.psum(hsq_d.astype(jnp.bfloat16), "dp").astype(jnp.float32),
        lax.psum(part_d.astype(jnp.bfloat16), "dp").astype(jnp.float32),
        lax.psum(hsq_u.astype(jnp.bfloat16), "dp").astype(jnp.float32),
        lax.psum(part_u.astype(jnp.bfloat16), "dp").astype(jnp.float32),
    )
    logits_d = part_d * lax.rsqrt(hsq_d / width + EPS)[None, :, None]
    logits_u = part_u * lax.rsqrt(hsq_u / width + EPS)[None, :, None]
    loss_d, dlog_d = jax.value_and_grad(logit_loss)(
        logits_d, down_ids, offsets, loss_weights, groups
    )
    loss_u, dlog_u = jax.value_and_grad(logit_loss)(logits_u, up_ids, offsets, loss_weights, groups)
    head_d = head_backward(final_d, hsq_d, part_d, dlog_d, gain_part, cand_part, width)
    head_u = head_backward(final_u, hsq_u, part_u, dlog_u, gain_part, cand_part, width)
    is_last = position == sections - 1
    is_first = position == 0
    cot_d = jnp.where(is_last, head_d, down_cot[0].astype(jnp.float32))
    cot_u = jnp.where(is_first, head_u, up_cot[0].astype(jnp.float32))
    gb_d = jnp.dot(act_d.T, cot_d, precision=HIGH)
    gb_u = jnp.dot(act_u.T, cot_u, precision=HIGH)
    dg_d = jnp.dot(cot_d, b_d.T, precision=HIGH)
    dg_u = jnp.dot(cot_u, b_u.T, precision=HIGH)
    dg_d, dg_u = lax.psum((dg_d, dg_u), "dp")
    dx_d, ga_d = section_backward(x_d, a_d, cot_d, scale_d, xa_d, pre_d, dg_d, width)
    dx_u, ga_u = section_backward(x_u, a_u, cot_u, scale_u, xa_u, pre_u, dg_u, width)
    back_d = dx_d.astype(jnp.bfloat16)[None]
    back_u = dx_u.astype(jnp.bfloat16)[None]
    down_back = from_behind(back_d, "section", -1)
    up_back = from_behind(back_u, "section", 1)
    partial_value = jnp.where(is_last, loss_d, 0.0) + jnp.where(is_first, loss_u, 0.0)
    loss = lax.psum(partial_value, "section").reshape(1)
    mate_a, mate_b = mirror_grads(ga_u, gb_u, levels)
    grad_a = ga_d + mate_a
    grad_b = gb_d + mate_b
    return (down_next, up_next, down_back, up_back, grad_a[None], grad_b[None], loss)


def solution(mesh):
    in_specs = (
        P("section", None, "dp"),
        P("section", None, "dp"),
        P("section", None, "dp"),
        P("section", None, "dp"),
        P("section", "dp", None),
        P("section", None, "dp"),
        P(),
        P(),
        P(),
        P(),
        P(),
        P(),
    )
    out_specs = (
        P("section", None, "dp"),
        P("section", None, "dp"),
        P("section", None, "dp"),
        P("section", None, "dp"),
        P("section", "dp", None),
        P("section", None, "dp"),
        P(),
    )
    return jax.shard_map(shards, mesh=mesh, in_specs=in_specs, out_specs=out_specs, check_vma=False)
```

profile of v0, /device:TPU:1, one launch (start us, length us, event | category | flops | bytes accessed | tf_op | source)
XLA Modules:
  0.0 811.4 jit_solution(13147709343666225645)
XLA Ops:
  7.3 8.9 %collective-permute-start.1 = (bf16[1,512,32]{1,2,0:T(8,128)(2,1)}, bf16[1,512,32]{1,2,0:T(8,128)(2,1)S(1)}, u32[]{:S(2)}, u32[]{:S(2)}) collective-permute-start(bf16[1,512,32]{1,2,0:T(8,128)(2,1)} %param.18), channel_id=1, source_target_pairs={{0,16},{16,0},{32,48},{48,32},{64,80},{80,64},{96,112},{112,96},{1... | collective-permute-start | bytes 98312 | tf_op jit(solution)/shard_map/ppermute | solution.py:17
  16.2 1.9 collective-permute-start.6
  22.2 1.3 compare_and_fusion
  37.7 47.9 %all-reduce.8 = (f32[512,1]{0,1:T(1,128)S(1)}, f32[512,1]{0,1:T(1,128)S(1)}) all-reduce(f32[512,1]{0,1:T(1,128)S(1)} %bitcast.146, f32[512,1]{0,1:T(1,128)S(1)} %bitcast.147), channel_id=1, replica_groups=mesh['section'=32,'dp'=16] {'dp'}, use_global_device_ids=true, to_apply=%region_1.0 | all-reduce | flops 1024 | bytes 8192 | tf_op jit(solution)/shard_map/psum | solution.py:132
  89.3 3.1 collective-permute-start.2
  95.1 4.4 collective-permute-start.3
  100.7 1.9 collective-permute-start.7
  102.6 2.3 collective-permute-start.4
  106.2 3.3 collective-permute-start.8
  109.4 2.4 collective-permute-start.5
  113.0 3.1 collective-permute-start.9
  118.3 3.8 collective-permute-start.10
  126.7 176.0 %all-reduce.19.cloned.1.call-done = (f32[512,32]{0,1:T(8,128)}, f32[512,32]{0,1:T(8,128)}) async-done(((f32[512,32]{0,1:T(8,128)}, f32[512,32]{0,1:T(8,128)}), (f32[512,32]{0,1:T(8,128)}, f32[512,32]{0,1:T(8,128)})) %all-reduce.19.cloned.1.call-update) | async-done | bytes 131088 | tf_op jit(solution)/shard_map/psum | solution.py:132
  302.7 2.3 multiply_reduce_fusion.2
  306.4 1.5 multiply_reduce_fusion.3
  309.1 3.0 fusion.19
  312.1 3.0 fusion.16
  315.2 46.3 %all-reduce.11 = (bf16[512]{0:T(512)(128)(2,1)S(1)}, bf16[512]{0:T(512)(128)(2,1)S(1)}) all-reduce(bf16[512]{0:T(512)(128)(2,1)S(1)} %get-tuple-element.127, bf16[512]{0:T(512)(128)(2,1)S(1)} %get-tuple-element.129), channel_id=1, replica_groups=mesh['section'=32,'dp'=16] {'dp'}, use_global_device_ids=true, to_apply=%region_8.9 | all-reduce | flops 1024 | bytes 4096 | tf_op jit(solution)/shard_map/psum | solution.py:152
  361.5 20.0 %collective-permute-start.11 = (bf16[1,512,512]{1,2,0:T(8,128)(2,1)}, bf16[1,512,512]{1,2,0:T(8,128)(2,1)}, u32[]{:S(2)}, u32[]{:S(2)}) collective-permute-start(bf16[1,512,512]{1,2,0:T(8,128)(2,1)} %bitcast.11), channel_id=1, source_target_pairs={{16,0},{32,16},{48,32},{64,48},{80,64},{96,80},{112,96},{128,112},... | collective-permute-start | bytes 1572872 | tf_op jit(solution)/shard_map/ppermute | solution.py:23
  381.5 3.2 collective-permute-start
  384.7 123.4 %all-reduce.21.cloned.1.call-done = (bf16[4,512,32]{1,2,0:T(8,128)(2,1)}, bf16[4,512,32]{1,2,0:T(8,128)(2,1)}) async-done(((bf16[4,512,32]{1,2,0:T(8,128)(2,1)}, bf16[4,512,32]{1,2,0:T(8,128)(2,1)}), (bf16[4,512,32]{1,2,0:T(8,128)(2,1)}, bf16[4,512,32]{1,2,0:T(8,128)(2,1)})) %all-reduce.21.cloned.1.call-update) | async-done | bytes 262160 | tf_op jit(solution)/shard_map/psum | solution.py:153
  533.0 1.6 select_add_fusion.3
  534.6 1.5 select_reduce_fusion.9
  536.2 1.6 select_add_fusion.2
  542.1 2.0 multiply_reduce_fusion
  545.5 3.7 multiply_reduce_fusion.1
  549.6 1.4 convert_select_fusion
  552.2 13.3 %collective-permute-start.19 = (bf16[32,512]{1,0:T(8,128)(2,1)S(1)}, bf16[32,512]{1,0:T(8,128)(2,1)S(1)}, u32[]{:S(2)}, u32[]{:S(2)}) collective-permute-start(bf16[32,512]{1,0:T(8,128)(2,1)S(1)} %convolution_convert_fusion), channel_id=1, source_target_pairs={{0,16},{16,0},{32,48},{48,32},{64,80},{80,64},{96,112},{112,96},{1... | collective-permute-start | bytes 98312 | tf_op jit(solution)/shard_map/ppermute | solution.py:17
  566.8 1.7 convert_select_fusion.1
  569.7 3.1 collective-permute-start.20
  574.3 4.6 collective-permute-start.21
  585.3 69.7 %psum.87 = f32[1]{0:T(128)} all-reduce(f32[1]{0:T(128)} %bitcast.41), channel_id=1, replica_groups=mesh['section'=32,'dp'=16] {'section'}, use_global_device_ids=true, to_apply=%region_53.55 | all-reduce | flops 1 | bytes 8 | tf_op jit(solution)/shard_map/psum | solution.py:181
  655.0 1.9 collective-permute-start.22
  656.9 97.7 %all-reduce.17.cloned.1.call-done = (f32[512,32]{0,1:T(8,128)}, f32[512,32]{0,1:T(8,128)}) async-done(((f32[512,32]{0,1:T(8,128)}, f32[512,32]{0,1:T(8,128)}), (f32[512,32]{0,1:T(8,128)}, f32[512,32]{0,1:T(8,128)})) %all-reduce.17.cloned.1.call-update) | async-done | bytes 131088 | tf_op jit(solution)/shard_map/psum | solution.py:173
  754.6 1.5 fusion.22
  757.0 13.4 %collective-permute-start.14 = (bf16[512,32]{0,1:T(8,128)(2,1)S(1)}, bf16[512,32]{0,1:T(8,128)(2,1)S(1)}, u32[]{:S(2)}, u32[]{:S(2)}) collective-permute-start(bf16[512,32]{0,1:T(8,128)(2,1)S(1)} %fusion.22), channel_id=1, source_target_pairs={{0,16},{16,0},{32,48},{48,32},{64,80},{80,64},{96,112},{112,96},{1... | collective-permute-start | bytes 98312 | tf_op jit(solution)/shard_map/ppermute | solution.py:17
  770.5 2.3 fusion.14
  772.9 3.0 collective-permute-start.13
  775.9 3.1 collective-permute-start.15
  779.1 2.2 collective-permute-start.23
  781.3 1.5 collective-permute-done.15
  782.9 4.3 collective-permute-start.16
  787.9 1.9 collective-permute-start.12
  789.8 2.2 collective-permute-start.17
  792.4 2.2 collective-permute-done.17
  794.6 2.9 collective-permute-start.18
  798.1 2.0 copy.110
  800.2 2.0 copy.109
  (361 shorter events, 73.0 us)
Async XLA Ops:
  7.2 301.9 %copy-start = (bf16[32,8192]{1,0:T(8,128)(2,1)S(1)}, bf16[32,8192]{1,0:T(8,128)(2,1)}, u32[]{:S(2)}) copy-start(bf16[32,8192]{1,0:T(8,128)(2,1)} %param.21) | copy-start | bytes 1572868
  7.2 12.2 %copy-start.18 = (bf16[1,512,32]{1,2,0:T(8,128)(2,1)S(1)}, bf16[1,512,32]{1,2,0:T(8,128)(2,1)}, u32[]{:S(2)}) copy-start(bf16[1,512,32]{1,2,0:T(8,128)(2,1)} %param.18) | copy-start | bytes 98308
  7.2 13.1 %copy-start.69 = (s32[4]{0:T(128)S(1)}, s32[4]{0:T(128)}, u32[]{:S(2)}) copy-start(s32[4]{0:T(128)} %param.24) | copy-start | bytes 52
  7.2 16.3 %copy-start.80 = (s32[512]{0:T(512)S(1)}, s32[512]{0:T(512)}, u32[]{:S(2)}) copy-start(s32[512]{0:T(512)} %param.22) | copy-start | bytes 6148
  7.2 16.5 %copy-start.81 = (s32[512]{0:T(512)S(1)}, s32[512]{0:T(512)}, u32[]{:S(2)}) copy-start(s32[512]{0:T(512)} %param.23) | copy-start | bytes 6148
  7.2 295.5 %all-reduce.19.cloned.1.call-start = ((), (), s32[]{:S(2)}) async-start(), calls=%async_computation.1 | async-start | bytes 262144 | tf_op jit(solution)/shard_map/psum | solution.py:132
  7.3 82.0 %collective-permute-start.1 = (bf16[1,512,32]{1,2,0:T(8,128)(2,1)}, bf16[1,512,32]{1,2,0:T(8,128)(2,1)S(1)}, u32[]{:S(2)}, u32[]{:S(2)}) collective-permute-start(bf16[1,512,32]{1,2,0:T(8,128)(2,1)} %param.18), channel_id=1, source_target_pairs={{0,16},{16,0},{32,48},{48,32},{64,80},{80,64},{96,112},{112,96},{1... | collective-permute-start | bytes 98312 | tf_op jit(solution)/shard_map/ppermute | solution.py:17
  16.2 84.5 %collective-permute-start.6 = (bf16[1,32,512]{2,1,0:T(8,128)(2,1)}, bf16[1,32,512]{2,1,0:T(8,128)(2,1)S(1)}, u32[]{:S(2)}, u32[]{:S(2)}) collective-permute-start(bf16[1,32,512]{2,1,0:T(8,128)(2,1)} %param.19), channel_id=1, source_target_pairs={{0,16},{16,0},{32,48},{48,32},{64,80},{80,64},{96,112},{112,96},{1... | collective-permute-start | bytes 98312 | tf_op jit(solution)/shard_map/ppermute | solution.py:17
  19.4 13.2 %copy-start.3 = (bf16[1,512,512]{2,1,0:T(8,128)(2,1)S(1)}, bf16[1,512,512]{2,1,0:T(8,128)(2,1)}, u32[]{:S(2)}) copy-start(bf16[1,512,512]{2,1,0:T(8,128)(2,1)} %param.15) | copy-start | bytes 1572868
  32.8 269.9 %copy-start.1 = (bf16[1,512,512]{1,2,0:T(8,128)(2,1)}, bf16[1,512,512]{1,2,0:T(8,128)(2,1)S(1)}, u32[]{:S(2)}) copy-start(bf16[1,512,512]{1,2,0:T(8,128)(2,1)S(1)} %copy.76) | copy-start | bytes 1572868
  32.8 91.9 %copy-start.16 = (bf16[1,512,512]{2,1,0:T(8,128)(2,1)S(1)}, bf16[1,512,512]{2,1,0:T(8,128)(2,1)}, u32[]{:S(2)}) copy-start(bf16[1,512,512]{2,1,0:T(8,128)(2,1)} %param.17) | copy-start | bytes 1572868
  85.7 217.1 %copy-start.29 = (f32[512,1]{0,1:T(1,128)}, f32[512,1]{0,1:T(1,128)S(1)}, u32[]{:S(2)}) copy-start(f32[512,1]{0,1:T(1,128)S(1)} %get-tuple-element.131) | copy-start | bytes 6148
  85.7 220.7 %copy-start.27 = (f32[512,1]{0,1:T(1,128)}, f32[512,1]{0,1:T(1,128)S(1)}, u32[]{:S(2)}) copy-start(f32[512,1]{0,1:T(1,128)S(1)} %get-tuple-element.132) | copy-start | bytes 6148
  86.4 225.7 %copy-start.63 = (f32[4,512]{1,0:T(4,128)}, f32[4,512]{1,0:T(4,128)S(1)}, u32[]{:S(2)}) copy-start(f32[4,512]{1,0:T(4,128)S(1)} %constant_dynamic-slice_fusion) | copy-start | bytes 24580
  89.3 5.8 collective-permute-start.2
  95.1 7.5 collective-permute-start.3
  100.7 5.5 collective-permute-start.7
  102.6 6.8 collective-permute-start.4
  106.2 6.9 collective-permute-start.8
  109.4 6.7 collective-permute-start.5
  113.0 12.7 %copy-start.17 = (bf16[1,512,512]{2,1,0:T(8,128)(2,1)S(1)}, bf16[1,512,512]{2,1,0:T(8,128)(2,1)}, u32[]{:S(2)}) copy-start(bf16[1,512,512]{2,1,0:T(8,128)(2,1)} %param.16) | copy-start | bytes 1572868
  113.0 5.3 collective-permute-start.9
  117.1 391.1 %all-reduce.21.cloned.1.call-start = ((), (), s32[]{:S(2)}) async-start(), calls=%async_computation.2 | async-start | bytes 524288 | tf_op jit(solution)/shard_map/psum | solution.py:153
  118.3 8.4 %collective-permute-start.10 = (bf16[1,32,512]{2,1,0:T(8,128)(2,1)S(1)}, bf16[1,32,512]{2,1,0:T(8,128)(2,1)S(1)}, u32[]{:S(2)}, u32[]{:S(2)}) collective-permute-start(bf16[1,32,512]{2,1,0:T(8,128)(2,1)S(1)} %collective-permute-done.9), channel_id=1, source_target_pairs={{0,256},{256,0},{16,272},{272,16},{32,288},{288,32},{48,304},{304,... | collective-permute-start | bytes 98312 | tf_op jit(solution)/shard_map/ppermute | solution.py:17
  126.7 176.0 %copy-start.33 = (bf16[1,32,512]{2,1,0:T(8,128)(2,1)}, bf16[1,32,512]{2,1,0:T(8,128)(2,1)S(1)}, u32[]{:S(2)}) copy-start(bf16[1,32,512]{2,1,0:T(8,128)(2,1)S(1)} %collective-permute-done.10) | copy-start | bytes 98308
  315.1 439.5 %all-reduce.17.cloned.1.call-start = ((), (), s32[]{:S(2)}) async-start(), calls=%async_computation | async-start | bytes 262144 | tf_op jit(solution)/shard_map/psum | solution.py:173
  361.5 147.9 %copy-start.71 = (bf16[512]{0:T(512)(128)(2,1)}, bf16[512]{0:T(512)(128)(2,1)S(1)}, u32[]{:S(2)}) copy-start(bf16[512]{0:T(512)(128)(2,1)S(1)} %get-tuple-element.67) | copy-start | bytes 3076
  361.5 147.9 %copy-start.73 = (bf16[512]{0:T(512)(128)(2,1)}, bf16[512]{0:T(512)(128)(2,1)S(1)}, u32[]{:S(2)}) copy-start(bf16[512]{0:T(512)(128)(2,1)S(1)} %get-tuple-element.68) | copy-start | bytes 3076
  361.5 147.9 %copy-start.53 = (f32[512]{0:T(512)}, f32[512]{0:T(512)S(1)}, u32[]{:S(2)}) copy-start(f32[512]{0:T(512)S(1)} %add_rsqrt_fusion.1) | copy-start | bytes 6148
  361.5 436.6 %collective-permute-start.11 = (bf16[1,512,512]{1,2,0:T(8,128)(2,1)}, bf16[1,512,512]{1,2,0:T(8,128)(2,1)}, u32[]{:S(2)}, u32[]{:S(2)}) collective-permute-start(bf16[1,512,512]{1,2,0:T(8,128)(2,1)} %bitcast.11), channel_id=1, source_target_pairs={{16,0},{32,16},{48,32},{64,48},{80,64},{96,80},{112,96},{128,112},... | collective-permute-start | bytes 1572872 | tf_op jit(solution)/shard_map/ppermute | solution.py:23
  381.5 418.6 %collective-permute-start = (bf16[1,512,512]{1,2,0:T(8,128)(2,1)}, bf16[1,512,512]{1,2,0:T(8,128)(2,1)}, u32[]{:S(2)}, u32[]{:S(2)}) collective-permute-start(bf16[1,512,512]{1,2,0:T(8,128)(2,1)} %bitcast.5), channel_id=1, source_target_pairs={{0,16},{16,32},{32,48},{48,64},{64,80},{80,96},{96,112},{112,128},... | collective-permute-start | bytes 1572872 | tf_op jit(solution)/shard_map/ppermute | solution.py:23
  384.7 124.7 %copy-start.55 = (f32[512]{0:T(512)}, f32[512]{0:T(512)S(1)}, u32[]{:S(2)}) copy-start(f32[512]{0:T(512)S(1)} %add_rsqrt_fusion) | copy-start | bytes 6148
  551.1 14.3 %copy-start.72 = (bf16[512]{0:T(512)(128)(2,1)S(1)}, bf16[512]{0:T(512)(128)(2,1)}, u32[]{:S(2)}) copy-start(bf16[512]{0:T(512)(128)(2,1)} %copy-done.71) | copy-start | bytes 3076
  551.1 14.4 %copy-start.6 = (f32[512,512]{1,0:T(8,128)S(1)}, f32[512,512]{1,0:T(8,128)}, u32[]{:S(2)}) copy-start(f32[512,512]{1,0:T(8,128)} %multiply_reduce_fusion.1) | copy-start | bytes 3145732
  552.2 17.5 %collective-permute-start.19 = (bf16[32,512]{1,0:T(8,128)(2,1)S(1)}, bf16[32,512]{1,0:T(8,128)(2,1)S(1)}, u32[]{:S(2)}, u32[]{:S(2)}) collective-permute-start(bf16[32,512]{1,0:T(8,128)(2,1)S(1)} %convolution_convert_fusion), channel_id=1, source_target_pairs={{0,16},{16,0},{32,48},{48,32},{64,80},{80,64},{96,112},{112,96},{1... | collective-permute-start | bytes 98312 | tf_op jit(solution)/shard_map/ppermute | solution.py:17
  569.7 4.6 collective-permute-start.20
  573.9 196.6 %copy-start.68 = (f32[512,1]{0,1:T(1,128)S(1)}, f32[512,1]{0,1:T(1,128)}, u32[]{:S(2)}) copy-start(f32[512,1]{0,1:T(1,128)} %copy-done.67) | copy-start | bytes 6148
  574.3 80.7 %collective-permute-start.21 = (bf16[32,512]{1,0:T(8,128)(2,1)S(1)}, bf16[32,512]{1,0:T(8,128)(2,1)}, u32[]{:S(2)}, u32[]{:S(2)}) collective-permute-start(bf16[32,512]{1,0:T(8,128)(2,1)S(1)} %collective-permute-done.20), channel_id=1, source_target_pairs={{0,64},{64,0},{16,80},{80,16},{32,96},{96,32},{48,112},{112,48},{1... | collective-permute-start | bytes 98312 | tf_op jit(solution)/shard_map/ppermute | solution.py:17
  655.0 124.1 %collective-permute-start.22 = (bf16[32,512]{1,0:T(8,128)(2,1)}, bf16[32,512]{1,0:T(8,128)(2,1)}, u32[]{:S(2)}, u32[]{:S(2)}) collective-permute-start(bf16[32,512]{1,0:T(8,128)(2,1)} %collective-permute-done.21), channel_id=1, source_target_pairs={{0,128},{128,0},{16,144},{144,16},{32,160},{160,32},{48,176},{176,... | collective-permute-start | bytes 98312 | tf_op jit(solution)/shard_map/ppermute | solution.py:17
  754.6 15.9 %copy-start.2 = (bf16[1,512,512]{1,2,0:T(8,128)(2,1)S(1)}, bf16[1,512,512]{1,2,0:T(8,128)(2,1)}, u32[]{:S(2)}) copy-start(bf16[1,512,512]{1,2,0:T(8,128)(2,1)} %copy-done.1) | copy-start | bytes 1572868
  757.0 18.9 %collective-permute-start.14 = (bf16[512,32]{0,1:T(8,128)(2,1)S(1)}, bf16[512,32]{0,1:T(8,128)(2,1)S(1)}, u32[]{:S(2)}, u32[]{:S(2)}) collective-permute-start(bf16[512,32]{0,1:T(8,128)(2,1)S(1)} %fusion.22), channel_id=1, source_target_pairs={{0,16},{16,0},{32,48},{48,32},{64,80},{80,64},{96,112},{112,96},{1... | collective-permute-start | bytes 98312 | tf_op jit(solution)/shard_map/ppermute | solution.py:17
  772.9 30.0 %collective-permute-start.13 = (bf16[1,512,512]{1,2,0:T(8,128)(2,1)}, bf16[1,512,512]{1,2,0:T(8,128)(2,1)S(1)}, u32[]{:S(2)}, u32[]{:S(2)}) collective-permute-start(bf16[1,512,512]{1,2,0:T(8,128)(2,1)} %fusion.14), channel_id=1, source_target_pairs={{0,16},{16,32},{32,48},{48,64},{64,80},{80,96},{96,112},{112,128},... | collective-permute-start | bytes 1572872 | tf_op jit(solution)/shard_map/ppermute | solution.py:23
  775.9 6.9 collective-permute-start.15
  779.1 8.8 %collective-permute-start.23 = (bf16[32,512]{1,0:T(8,128)(2,1)}, bf16[32,512]{1,0:T(8,128)(2,1)S(1)}, u32[]{:S(2)}, u32[]{:S(2)}) collective-permute-start(bf16[32,512]{1,0:T(8,128)(2,1)} %collective-permute-done.22), channel_id=1, source_target_pairs={{0,256},{256,0},{16,272},{272,16},{32,288},{288,32},{48,304},{304,... | collective-permute-start | bytes 98312 | tf_op jit(solution)/shard_map/ppermute | solution.py:17
  782.9 6.9 collective-permute-start.16
  787.9 16.0 %collective-permute-start.12 = (bf16[1,512,512]{1,2,0:T(8,128)(2,1)S(1)}, bf16[1,512,512]{1,2,0:T(8,128)(2,1)S(1)}, u32[]{:S(2)}, u32[]{:S(2)}) collective-permute-start(bf16[1,512,512]{1,2,0:T(8,128)(2,1)S(1)} %fusion.15), channel_id=1, source_target_pairs={{16,0},{32,16},{48,32},{64,48},{80,64},{96,80},{112,96},{128,112},... | collective-permute-start | bytes 1572872 | tf_op jit(solution)/shard_map/ppermute | solution.py:23
  789.8 4.8 collective-permute-start.17
  794.6 7.7 collective-permute-start.18
  (64 other events, 193.9 us)
Sparse Core Ops, SparseCore 0:
  117.2 185.4 all-reduce.18
  315.2 192.8 all-reduce.20
  574.0 180.5 all-reduce.16
where the time goes:
time: 818 us; the launch traced here: 811 us
  waiting for transfers between devices  401 us (49%)
  blocking collectives  164 us (20%)
  starting transfers between devices  114 us (14%)
  local copies, waits for them, and re-layouts  46.1 us (6%)
  other arithmetic  32.5 us (4%)
  between operations  26.8 us (3%)
  matrix products  26.3 us (3%)
    psum x1, waiting for transfers between devices, shards(): sq_d, xa_d, sq_u, xa_u = lax.psum((sq_d, xa_d, sq_u, xa_u), 'dp')  176 us
    psum x1, waiting for transfers between devices, shards(): lax.psum(part_d.astype(jnp.bfloat16), 'dp').astype(jnp.float32)  123 us
    psum x1, waiting for transfers between devices, shards(): dg_d, dg_u = lax.psum((dg_d, dg_u), 'dp')  97.7 us
    ppermute x20, starting transfers between devices, swapped(): return lax.ppermute(block, axis, route)  86.1 us
    psum x1, blocking collectives, shards(): loss = lax.psum(partial_value, 'section').reshape(1)  69.7 us
    psum x1, blocking collectives, shards(): sq_d, xa_d, sq_u, xa_u = lax.psum((sq_d, xa_d, sq_u, xa_u), 'dp')  47.9 us
    psum x1, blocking collectives, shards(): lax.psum(hsq_d.astype(jnp.bfloat16), 'dp').astype(jnp.float32)  46.3 us
    ppermute x4, starting transfers between devices, from_behind(): return lax.ppermute(block, axis, route)  28.1 us
  transfers between devices with their start and end apart: 27, of which 6 were waited for; matrix products, arithmetic and copies ran while one was open for 11% of the time, Pallas kernels for 0%

commit v1 on v0

v1 whole, which is shorter than its diff:
```python
import jax
import jax.numpy as jnp
from jax import lax
from jax.experimental import pallas as pl
from jax.experimental.pallas import tpu as pltpu
from jax.sharding import PartitionSpec as P

EPS = 1e-05
F32 = jnp.float32
BF16 = jnp.bfloat16
HIGH = lax.Precision.HIGHEST
ROWS = 112
BACK_ROWS = 80
R = 32
LANES = 128


def nt(a, b, precision=None):
    return lax.dot_general(a, b, (((1,), (1,)), ((), ())), precision=precision, preferred_element_type=F32)


def nn(a, b, precision=None):
    return lax.dot_general(a, b, (((1,), (0,)), ((), ())), precision=precision, preferred_element_type=F32)


def tn(a, b):
    return lax.dot_general(a, b, (((0,), (0,)), ((), ())), preferred_element_type=F32)


def halves(value):
    high = value.astype(BF16)
    return high, (value - high.astype(F32)).astype(BF16)


def columns_of(gain_ref, cand_ref):
    cand = cand_ref[...].astype(F32)
    return jnp.concatenate([gain_ref[k : k + 1, :] * cand for k in range(gain_ref.shape[0])], axis=0)


def squares_row(block):
    wide = block.astype(F32)
    ones = jnp.ones((8, wide.shape[1]), BF16)
    high, low = halves(wide * wide)
    return (nt(ones, high) + nt(ones, low))[0:1, :]


def gated(weights, flag):
    return jnp.where(flag, weights.astype(F32), 0.0).astype(BF16)


def first_partial(meta, x_d, x_u, c_d, a_d, b_d, gain, cand, out):
    sections = meta[2]
    is_first = meta[1] == 0
    is_last = meta[1] == sections - 1
    chunks = out.shape[0]
    width = x_d.shape[1]
    zero = jnp.zeros((R, width), BF16)
    wx = jnp.concatenate([a_d[...], zero, gated(b_d[...], is_last), zero], axis=0)
    wc = jnp.concatenate([zero, zero, gated(b_d[...], jnp.logical_not(is_last)), zero], axis=0)
    main = nt(x_d[...], wx) + nt(c_d[...], wc)
    out[:, 0:R, :] = main.astype(BF16).reshape(chunks, R, LANES)
    rows = []
    for block in (x_d[...], x_u[...]):
        row = squares_row(block)
        high = row.astype(BF16).astype(F32)
        rows += [high, row - high]
    per = LANES // R
    pad = jnp.zeros((8, LANES), F32)
    for j in range(chunks):
        start = (j // per) * LANES
        piece = [row[:, start : start + LANES] for row in rows]
        tail = jnp.concatenate([pad] + piece + [pad[0:4]], axis=0)
        out[j, 96:ROWS, :] = tail.astype(BF16)
    out[:, 64:96, :] = jnp.zeros((chunks, R, LANES), BF16)

    def logits_of(block):
        high, low = halves(columns_of(gain, cand))
        value = nt(block, high) + nt(block, low)
        out[:, 32:64, :] = value.astype(BF16).reshape(chunks, R, LANES)

    @pl.when(is_last)
    def _():
        logits_of(x_d[...])

    @pl.when(is_first)
    def _():
        logits_of(x_u[...])

    @pl.when(jnp.logical_not(jnp.logical_or(is_first, is_last)))
    def _():
        out[:, 32:64, :] = jnp.zeros((chunks, R, LANES), BF16)


def second_partial(meta, partial, x_u, c_u, a_u, b_u, b_d, gain, cand, out):
    is_first = meta[1] == 0
    is_last = meta[1] == meta[2] - 1
    chunks = out.shape[0]
    width = x_u.shape[1]
    zero = jnp.zeros((R, width), BF16)
    wx = jnp.concatenate([zero, a_u[...], zero, gated(b_u[...], is_first)], axis=0)
    wc = jnp.concatenate([zero, zero, zero, gated(b_u[...], jnp.logical_not(is_first))], axis=0)
    main = nt(x_u[...], wx) + nt(c_u[...], wc)
    main = main.reshape(chunks, R, LANES) + partial[:, 0:R, :].astype(F32)
    out[:, 0:R, :] = main.astype(BF16)
    out[:, R:ROWS, :] = partial[:, R:ROWS, :]

    @pl.when(jnp.logical_or(is_first, is_last))
    def _():
        b_e = jnp.where(is_last, b_d[...].astype(F32), b_u[...].astype(F32)).astype(BF16)
        high, low = halves(columns_of(gain, cand))
        cross = nt(b_e, high) + nt(b_e, low)
        own = nt(b_e, b_e)
        packed = jnp.concatenate([own[8 * r : 8 * r + 8] for r in range(4)], axis=1)
        tail = jnp.concatenate([packed, jnp.zeros((8, LANES), F32)], axis=0)
        out[:, 64:96, :] = jnp.broadcast_to(cross.astype(BF16)[None], (chunks, R, LANES))
        held = partial[:, 96:ROWS, :].astype(F32) + tail[None]
        out[:, 96:ROWS, :] = held.astype(BF16)


def middle(meta, offsets, loss_weights, received, down_ids, up_ids, out):
    place = meta[0]
    is_first = meta[1] == 0
    is_last = meta[1] == meta[2] - 1
    is_end = jnp.logical_or(is_first, is_last)
    chunks = received.shape[0]
    inverse = 1.0 / meta[3].astype(F32)
    heads = LANES // R
    total = jnp.sum(received[...].astype(F32), axis=0)
    main, base_logits, cross = total[0:32], total[32:64], total[64:96]
    packed, square_rows = total[96:104], total[104:108]
    lane = lax.broadcasted_iota(jnp.int32, (R, LANES), 1)
    token = lax.broadcasted_iota(jnp.int32, (R, LANES), 0)
    base = R * lax.rem(place, LANES // R)

    def column(row):
        return jnp.sum(jnp.where(lane == base + token, row, 0.0), axis=1, keepdims=True)

    square_d = column(square_rows[0:1] + square_rows[1:2])
    square_u = column(square_rows[2:3] + square_rows[3:4])
    scale_d = lax.rsqrt(square_d * inverse + EPS)
    scale_u = lax.rsqrt(square_u * inverse + EPS)
    down_lane = lane < R
    up_lane = jnp.logical_and(lane >= R, lane < 2 * R)
    low_lane = lane < 2 * R
    scale = jnp.where(down_lane, scale_d, scale_u)
    projected = jnp.where(low_lane, main, 0.0)
    pre = projected * scale
    sigma = jax.nn.sigmoid(pre)
    act = pre * sigma

    act_e = jnp.where(is_first, act[:, R : 2 * R], act[:, 0:R])
    cot_e = jnp.where(is_first, main[:, 3 * R :], main[:, 2 * R : 3 * R])
    own = jnp.concatenate([packed[:, R * r : R * r + R] for r in range(4)], axis=0)
    act_own = nn(act_e, own, HIGH)
    out_b = cot_e + act_own
    square_e = jnp.where(is_first, square_u, square_d)
    square_e = square_e + jnp.sum(act_e * (cot_e + out_b), axis=1, keepdims=True)
    scale_e = lax.rsqrt(jnp.maximum(square_e, 0.0) * inverse + EPS)
    raw = base_logits + nn(act_e, cross, HIGH)
    logits = raw * scale_e
    block = lax.div(place, LANES // R)
    ids_d = down_ids[pl.ds(block, 1), :]
    ids_u = up_ids[pl.ds(block, 1), :]
    ids = jnp.where(is_first, ids_u, ids_d).astype(F32)
    group = lax.div(lane, R)
    within = lax.rem(lane, R)
    weight_sum = jnp.float32(0.0)
    for k in range(heads):
        weight_sum = weight_sum + loss_weights[k].astype(F32)
    top = jnp.zeros((R, LANES), F32)
    target = jnp.zeros((R, LANES), F32)
    weight = jnp.zeros((R, LANES), F32)
    for k in range(heads):
        mine = group == k
        shift = offsets[k]
        largest = jnp.max(jnp.where(mine, logits, -jnp.inf), axis=1, keepdims=True)
        wanted = jnp.sum(jnp.where(lane == base + token + shift, ids, 0.0), axis=1, keepdims=True)
        factor = loss_weights[k].astype(F32) / weight_sum / ((R - shift) * chunks).astype(F32)
        valid = jnp.where(token + shift < R, factor, 0.0)
        top = jnp.where(mine, largest, top)
        target = jnp.where(mine, wanted, target)
        weight = jnp.where(mine, valid, weight)
    power = jnp.exp(logits - top)
    below = jnp.ones((R, LANES), F32)
    for k in range(heads):
        mine = group == k
        below = jnp.where(mine, jnp.sum(jnp.where(mine, power, 0.0), axis=1, keepdims=True), below)
    hit = jnp.where(within == target.astype(jnp.int32), 1.0, 0.0)
    per_lane = hit * (top + jnp.log(below) - logits) * weight
    loss = jnp.sum(jnp.sum(per_lane, axis=1, keepdims=True), axis=0, keepdims=True)
    grad = weight * (power / below - hit)
    grad_cols = grad * scale_e
    coef_e = jnp.sum(grad * raw, axis=1, keepdims=True) * scale_e * scale_e * scale_e * inverse
    dg_e = nt(grad_cols, cross, HIGH) - coef_e * out_b

    dg = pltpu.roll(main, 2 * R, axis=1)
    dg_wide = jnp.concatenate([dg_e] * 4, axis=1)
    replace = jnp.logical_or(jnp.logical_and(is_last, down_lane), jnp.logical_and(is_first, up_lane))
    dg = jnp.where(replace, dg_wide, dg)
    d_pre = jnp.where(low_lane, dg * sigma * (1.0 + pre * (1.0 - sigma)), 0.0)
    d_scaled = d_pre * scale
    moved = d_pre * projected
    coef_d = jnp.sum(jnp.where(down_lane, moved, 0.0), axis=1, keepdims=True)
    coef_u = jnp.sum(jnp.where(up_lane, moved, 0.0), axis=1, keepdims=True)
    coef_d = coef_d * scale_d * scale_d * scale_d * inverse
    coef_u = coef_u * scale_u * scale_u * scale_u * inverse
    both = jnp.where(low_lane, act, pltpu.roll(d_scaled, 2 * R, axis=1))
    head = jnp.where(is_end, grad_cols, 0.0)

    def parts_of(row):
        high = row.astype(BF16).astype(F32)
        low = (row - high).astype(BF16).astype(F32)
        return [high, low, row - high - low]

    rows = []
    for col in (coef_d, coef_u, coef_e):
        row = jnp.sum(jnp.where(lane == token, col, 0.0), axis=0, keepdims=True)
        rows += parts_of(row)[0:2]
    rows += parts_of(jnp.broadcast_to(jnp.where(is_end, loss, 0.0), (1, LANES)))
    rows += [jnp.zeros((7, LANES), F32)]
    chunk = jnp.concatenate([both, head, jnp.concatenate(rows, axis=0)], axis=0)
    out[...] = jnp.broadcast_to(chunk.astype(BF16)[None], out.shape)


def tokens_of(received, first):
    chunks = received.shape[0]
    return received[:, first : first + R, :].reshape(chunks * R, LANES)


def coefficient(received, row):
    chunks = received.shape[0]
    lane = lax.broadcasted_iota(jnp.int32, (R, LANES), 1)
    token = lax.broadcasted_iota(jnp.int32, (R, LANES), 0)
    cols = []
    for j in range(chunks):
        rows = received[j, 64:BACK_ROWS, :].astype(F32)
        both = rows[row : row + 1] + rows[row + 1 : row + 2]
        cols.append(jnp.sum(jnp.where(lane == token, both, 0.0), axis=1, keepdims=True))
    return jnp.concatenate(cols, axis=0)


def at_rows(weights, group):
    zero = jnp.zeros_like(weights)
    return jnp.concatenate([weights if k == group else zero for k in range(LANES // R)], axis=0)


def outputs(received, x_d, x_u, b_d, b_u, y_d, y_u, loss):
    act = tokens_of(received, 0)
    y_d[...] = (x_d[...].astype(F32) + nn(act, at_rows(b_d[...], 0))).astype(BF16)
    y_u[...] = (x_u[...].astype(F32) + nn(act, at_rows(b_u[...], 1))).astype(BF16)
    rows = jnp.sum(received[:, 64:BACK_ROWS, :].astype(F32), axis=0)
    total = rows[6:7] + rows[7:8] + rows[8:9]
    loss[...] = jnp.broadcast_to(total, loss.shape)


def backward(meta, received, x_d, x_u, c_d, c_u, a_d, b_d, a_u, b_u, gain, cand, dx_d, dx_u, g_d, g_u, cot):
    is_first = meta[1] == 0
    is_last = meta[1] == meta[2] - 1
    act = tokens_of(received, 0)
    work = (
        (1, x_u, c_u, a_u, b_u, dx_u, g_u, is_first),
        (0, x_d, c_d, a_d, b_d, dx_d, g_d, is_last),
    )
    for side, x, c, a, b, dx, g, end in work:
        cot[...] = c[...].astype(F32)

        @pl.when(end)
        def _():
            high, low = halves(columns_of(gain, cand))
            grad = tokens_of(received, 32)
            final = x[...].astype(F32) + nn(act, at_rows(b[...], side))
            cot[...] = nn(grad, high) + nn(grad, low) - coefficient(received, 4) * final

        held = cot[...]
        wide = x[...].astype(F32)
        back = held + nn(act, at_rows(a[...], 2 + side)) - coefficient(received, 2 * side) * wide
        dx[...] = back.astype(BF16)
        by_cot = tn(act, held.astype(BF16))
        by_x = tn(act, x[...])
        grads = jnp.concatenate(
            [by_x[64 + R * side : 64 + R * side + R], by_cot[R * side : R * side + R]], axis=0
        )
        g[...] = grads.astype(g.dtype)


def finish(g_d, mate, losses, grad_a, grad_b, loss):
    total = g_d[...] + mate[...].astype(F32)
    grad_a[...] = total[0:R]
    grad_b[...] = total[R : 2 * R]
    loss[0] = jnp.sum(losses[:, 0:1])


def shards(
    down_in,
    up_in,
    down_cot,
    up_cot,
    adapt_a,
    adapt_b,
    head_gain,
    cand,
    down_ids,
    up_ids,
    offsets,
    loss_weights,
):
    sections = lax.axis_size("section")
    groups = lax.axis_size("dp")
    position = lax.axis_index("section")
    place = lax.axis_index("dp")
    x_d, x_u, c_d, c_u = down_in[0], up_in[0], down_cot[0], up_cot[0]
    tokens, local_width = x_d.shape
    a_d = adapt_a[0].T
    b_d = adapt_b[0]
    mirror = [(i, sections - 1 - i) for i in range(sections)]
    a_u = lax.ppermute(a_d, "section", mirror)
    b_u = lax.ppermute(b_d, "section", mirror)
    whole = jnp.int32(sections), jnp.int32(head_gain.shape[1])
    meta = jnp.stack([place.astype(jnp.int32), position.astype(jnp.int32), *whole])
    gain_part = lax.dynamic_slice_in_dim(head_gain, place * local_width, local_width, 1)
    cand_part = lax.dynamic_slice_in_dim(cand, place * local_width, local_width, 1)
    smem = pl.BlockSpec(memory_space=pltpu.SMEM)
    vmem = pl.BlockSpec(memory_space=pltpu.VMEM)
    params = pltpu.CompilerParams(vmem_limit_bytes=48 << 20)

    send = jax.ShapeDtypeStruct((groups, ROWS, LANES), BF16)
    partial = pl.pallas_call(
        first_partial,
        out_shape=send,
        in_specs=[smem] + [vmem] * 7,
        out_specs=vmem,
        compiler_params=params,
    )(meta, x_d, x_u, c_d, a_d, b_d, gain_part, cand_part)
    partial = pl.pallas_call(
        second_partial,
        out_shape=send,
        in_specs=[smem] + [vmem] * 8,
        out_specs=vmem,
        compiler_params=params,
    )(meta, partial, x_u, c_u, a_u, b_u, b_d, gain_part, cand_part)
    received = lax.all_to_all(partial, "dp", 0, 0)

    back = pl.pallas_call(
        middle,
        out_shape=jax.ShapeDtypeStruct((groups, BACK_ROWS, LANES), BF16),
        in_specs=[smem] * 3 + [vmem] * 3,
        out_specs=vmem,
        compiler_params=params,
    )(
        meta,
        offsets,
        loss_weights,
        received,
        down_ids.reshape(tokens // LANES, LANES),
        up_ids.reshape(tokens // LANES, LANES),
    )
    gathered = lax.all_to_all(back, "dp", 0, 0)

    wide = jax.ShapeDtypeStruct((tokens, local_width), BF16)
    y_d, y_u, loss_rows = pl.pallas_call(
        outputs,
        out_shape=(wide, wide, jax.ShapeDtypeStruct((sections, LANES), F32)),
        in_specs=[vmem] * 5,
        out_specs=(vmem,) * 3,
        compiler_params=params,
    )(gathered, x_d, x_u, b_d, b_u)
    ahead = [(i, i + 1) for i in range(sections - 1)]
    behind = [(i + 1, i) for i in range(sections - 1)]
    down_next = lax.ppermute(y_d, "section", ahead)
    up_next = lax.ppermute(y_u, "section", behind)

    dx_d, dx_u, g_d, g_u = pl.pallas_call(
        backward,
        out_shape=(
            wide,
            wide,
            jax.ShapeDtypeStruct((2 * R, local_width), F32),
            jax.ShapeDtypeStruct((2 * R, local_width), BF16),
        ),
        in_specs=[smem] + [vmem] * 11,
        out_specs=(vmem,) * 4,
        scratch_shapes=[pltpu.VMEM((tokens, local_width), F32)],
        compiler_params=params,
    )(meta, gathered, x_d, x_u, c_d, c_u, a_d, b_d, a_u, b_u, gain_part, cand_part)
    mate = lax.ppermute(g_u, "section", mirror)
    down_back = lax.ppermute(dx_d, "section", behind)
    up_back = lax.ppermute(dx_u, "section", ahead)
    losses = lax.all_to_all(loss_rows, "section", 0, 0, tiled=True)
    grad_a, grad_b, loss = pl.pallas_call(
        finish,
        out_shape=(
            jax.ShapeDtypeStruct((R, local_width), F32),
            jax.ShapeDtypeStruct((R, local_width), F32),
            jax.ShapeDtypeStruct((1,), F32),
        ),
        in_specs=[vmem] * 3,
        out_specs=(vmem, vmem, smem),
        compiler_params=params,
    )(g_d, mate, losses)
    return (
        down_next[None],
        up_next[None],
        down_back[None],
        up_back[None],
        grad_a.T[None],
        grad_b[None],
        loss,
    )


def solution(mesh):
    in_specs = (
        P("section", None, "dp"),
        P("section", None, "dp"),
        P("section", None, "dp"),
        P("section", None, "dp"),
        P("section", "dp", None),
        P("section", None, "dp"),
        P(),
        P(),
        P(),
        P(),
        P(),
        P(),
    )
    out_specs = (
        P("section", None, "dp"),
        P("section", None, "dp"),
        P("section", None, "dp"),
        P("section", None, "dp"),
        P("section", "dp", None),
        P("section", None, "dp"),
        P(),
    )
    return jax.shard_map(shards, mesh=mesh, in_specs=in_specs, out_specs=out_specs, check_vma=False)
```

time: 818 us -> 108 us (0.13)
  waiting for transfers between devices: 401 us -> 1.3 us
  blocking collectives: 164 us -> 59.3 us
  starting transfers between devices: 114 us -> 30.4 us
  local copies, waits for them, and re-layouts: 46.1 us -> 8.4 us
  other arithmetic: 32.5 us -> 0.08 us
  matrix products: 26.3 us -> 0 us
  between operations: 26.8 us -> 0.83 us
    psum x3 -> x0, waiting for transfers between devices: 397 us -> none  [the longest x1 176 us: shards(): sq_d, xa_d, sq_u, xa_u = lax.psum((sq_d, xa_d, sq_u, xa_u), 'dp')]
    psum x3 -> x0, blocking collectives: 164 us -> none  [the longest x1 69.7 us: shards(): loss = lax.psum(partial_value, 'section').reshape(1)]
    ppermute x24 -> x7, starting transfers between devices: 114 us -> 30.4 us  [the longest x1 8.95 us: shards(): a_u = lax.ppermute(a_d, 'section', mirror)]
    all_to_all x0 -> x3, blocking collectives: none -> 59.3 us  [the longest x1 28 us: shards(): received = lax.all_to_all(partial, 'dp', 0, 0)]
    dot_general x16 -> x0, matrix products: 26.3 us -> none  [the longest x2 5.98 us: head_partial(): partial_value = jnp.einsum('ktd,cd->ktc', scaled, cand_part, precision=HIGH)]
  transfers between devices with their start and end apart: 27 -> 7, of which waited for: 6 -> 1; matrix products, arithmetic and copies ran while one was open for 11% -> 1% of each run, Pallas kernels for 0% -> 4%
where the time goes in v1:
time: 108 us
  blocking collectives  59.3 us (55%)
  starting transfers between devices  30.4 us (28%)
  local copies, waits for them, and re-layouts  8.4 us (8%)
  Pallas kernels  7.17 us (7%)
  waiting for transfers between devices  1.3 us (1%)
    all_to_all x1, blocking collectives, shards(): received = lax.all_to_all(partial, 'dp', 0, 0)  28 us
    all_to_all x1, blocking collectives, shards(): gathered = lax.all_to_all(back, 'dp', 0, 0)  19.3 us
    all_to_all x1, blocking collectives, shards(): losses = lax.all_to_all(loss_rows, 'section', 0, 0, tiled=True)  12.1 us
    ppermute x1, starting transfers between devices, shards(): a_u = lax.ppermute(a_d, 'section', mirror)  8.95 us
    unnamed x32, local copies, waits for them, and re-layouts  7.69 us
    ppermute x1, starting transfers between devices, shards(): mate = lax.ppermute(g_u, 'section', mirror)  6.74 us
    ppermute x1, starting transfers between devices, shards(): down_next = lax.ppermute(y_d, 'section', ahead)  5.34 us
    ppermute x1, starting transfers between devices, shards(): up_back = lax.ppermute(dx_u, 'section', ahead)  3.64 us
  transfers between devices with their start and end apart: 7, of which 1 were waited for; matrix products, arithmetic and copies ran while one was open for 1% of the time, Pallas kernels for 4%

profile of v1, /device:TPU:1, one launch (start us, length us, event | category | flops | bytes accessed | tf_op | source)
XLA Modules:
  0.0 107.5 jit_solution(17590112776574708366)
XLA Ops:
  0.6 0.0 copy-start
  0.6 8.9 %collective-permute-start = (bf16[32,512]{1,0:T(8,128)(2,1)}, bf16[32,512]{1,0:T(8,128)(2,1)S(1)}, u32[]{:S(2)}, u32[]{:S(2)}) collective-permute-start(bf16[32,512]{1,0:T(8,128)(2,1)} %bitcast.40), channel_id=1, source_target_pairs={{0,496},{16,480},{32,464},{48,448},{64,432},{80,416},{96,400},{112... | collective-permute-start | bytes 98312 | tf_op jit(solution)/shard_map/ppermute | solution.py:316
  9.6 1.9 %collective-permute-start.1 = (bf16[32,512]{1,0:T(8,128)(2,1)}, bf16[32,512]{1,0:T(8,128)(2,1)S(1)}, u32[]{:S(2)}, u32[]{:S(2)}) collective-permute-start(bf16[32,512]{1,0:T(8,128)(2,1)} %bitcast.35), channel_id=1, source_target_pairs={{0,496},{16,480},{32,464},{48,448},{64,432},{80,416},{96,400},{112... | collective-permute-start | bytes 98312 | tf_op jit(solution)/shard_map/ppermute | solution.py:317
  11.5 0.7 constant_dynamic-slice_fusion.1.gain
  12.2 0.0 copy-done
  12.2 0.0 copy-start.8
  12.2 0.0 copy-start.9
  12.3 0.1 pad_add_fusion.meta
  12.3 0.7 copy-done.8
  13.0 0.0 copy-done.9
  13.0 1.0 copy-done.1
  14.1 1.0 copy-done.3
  15.1 1.0 copy-done.5
  16.1 1.5 %shard_map.171.partial = bf16[16,112,128]{2,1,0:T(8,128)(2,1)S(1)} custom-call(s32[4]{0:T(128)S(1)} %pad_add_fusion.meta, bf16[512,512]{1,0:T(8,128)(2,1)S(1)} %bitcast.28, bf16[512,512]{1,0:T(8,128)(2,1)S(1)} %bitcast.24, bf16[512,512]{1,0:T(8,128)(2,1)S(1)} %bitcast.31, bf16[32,512]{1,0:T(8,128)(2,1)S(1)} %bitcast.41, bf16[32,512]{1,0:T(8,128)(2,1)S(1)} %bitcast.36, ...), custom_call_target="tpu_custom_call" | custom-call | tf_op jit(solution)/shard_map/pallas_call | solution.py:327
  17.7 0.0 collective-permute-done.a_u
  17.7 1.3 %collective-permute-done.1.b_u = bf16[32,512]{1,0:T(8,128)(2,1)S(1)} collective-permute-done((bf16[32,512]{1,0:T(8,128)(2,1)}, bf16[32,512]{1,0:T(8,128)(2,1)S(1)}, u32[]{:S(2)}, u32[]{:S(2)}) %collective-permute-start.1) | collective-permute-done | bytes 32800 | tf_op jit(solution)/shard_map/ppermute | solution.py:317
  19.0 0.0 copy-done.2
  19.0 0.0 copy-done.7
  19.0 1.0 shard_map.172
  19.9 0.0 copy-start.11
  20.0 28.0 %all_to_all.21.received = bf16[16,112,128]{2,1,0:T(8,128)(2,1)S(1)} all-to-all(bf16[16,112,128]{2,1,0:T(8,128)(2,1)S(1)} %shard_map.172), channel_id=1, replica_groups=mesh['section'=32,'dp'=16] {'dp'}, dimensions={0} | all-to-all | bytes 917504 | tf_op jit(solution)/shard_map/all_to_all | solution.py:341
  48.0 0.0 copy-done.11
  48.0 0.7 copy-done.10
  48.6 0.0 copy-done.12
  48.6 0.0 copy-done.13
  48.7 1.8 %shard_map.173 = bf16[16,80,128]{2,1,0:T(8,128)(2,1)S(1)} custom-call(s32[4]{0:T(128)S(1)} %pad_add_fusion.meta, s32[4]{0:T(128)S(1)} %copy-done.12, s32[4]{0:T(128)S(1)} %copy-done.13, bf16[16,112,128]{2,1,0:T(8,128)(2,1)S(1)} %all_to_all.21.received, s32[4,128]{1,0:T(4,128)S(1)} %bitcast.45, s32[4,128]{1,0:T(4,128)S(1)} %bitcast.46), custom_call_target="tpu_custom_call" | custom-call | tf_op jit(solution)/shard_map/pallas_call | solution.py:343
  50.4 0.0 copy-start.4
  50.4 19.3 %all_to_all.22.received = bf16[16,80,128]{2,1,0:T(8,128)(2,1)S(1)} all-to-all(bf16[16,80,128]{2,1,0:T(8,128)(2,1)S(1)} %shard_map.173), channel_id=1, replica_groups=mesh['section'=32,'dp'=16] {'dp'}, dimensions={0} | all-to-all | bytes 655360 | tf_op jit(solution)/shard_map/all_to_all | solution.py:357
  69.7 0.0 copy-done.4
  69.7 0.4 shard_map.174
  70.1 5.3 %collective-permute-start.2 = (bf16[512,512]{1,0:T(8,128)(2,1)S(1)}, bf16[512,512]{1,0:T(8,128)(2,1)S(1)}, u32[]{:S(2)}, u32[]{:S(2)}) collective-permute-start(bf16[512,512]{1,0:T(8,128)(2,1)S(1)} %get-tuple-element.17), channel_id=1, source_target_pairs={{0,16},{16,32},{32,48},{48,64},{64,80},{80,96},{96,112},{112,128},... | collective-permute-start | bytes 1572872 | tf_op jit(solution)/shard_map/ppermute | solution.py:369
  75.5 1.9 %collective-permute-start.3 = (bf16[512,512]{1,0:T(8,128)(2,1)S(1)}, bf16[512,512]{1,0:T(8,128)(2,1)S(1)}, u32[]{:S(2)}, u32[]{:S(2)}) collective-permute-start(bf16[512,512]{1,0:T(8,128)(2,1)S(1)} %get-tuple-element.18), channel_id=1, source_target_pairs={{16,0},{32,16},{48,32},{64,48},{80,64},{96,80},{112,96},{128,112},... | collective-permute-start | bytes 1572872 | tf_op jit(solution)/shard_map/ppermute | solution.py:370
  77.4 0.0 copy-done.6
  77.4 1.8 %shard_map.175 = (bf16[512,512]{1,0:T(8,128)(2,1)S(1)}, bf16[512,512]{1,0:T(8,128)(2,1)S(1)}, f32[64,512]{1,0:T(8,128)S(1)}, bf16[64,512]{1,0:T(8,128)(2,1)S(1)}) custom-call(s32[4]{0:T(128)S(1)} %pad_add_fusion.meta, bf16[16,80,128]{2,1,0:T(8,128)(2,1)S(1)} %all_to_all.22.received, bf16[512,512]{1,0:T(8,128)(2,1)S(1)} %bitcast.30, ...), custom_call_target="tpu_custom_call" | custom-call | tf_op jit(solution)/shard_map/pallas_call | solution.py:372
  79.3 1.9 %collective-permute-start.4 = (bf16[512,512]{1,0:T(8,128)(2,1)S(1)}, bf16[512,512]{1,0:T(8,128)(2,1)S(1)}, u32[]{:S(2)}, u32[]{:S(2)}) collective-permute-start(bf16[512,512]{1,0:T(8,128)(2,1)S(1)} %get-tuple-element.19), channel_id=1, source_target_pairs={{16,0},{32,16},{48,32},{64,48},{80,64},{96,80},{112,96},{128,112},... | collective-permute-start | bytes 1572872 | tf_op jit(solution)/shard_map/ppermute | solution.py:386
  81.2 3.6 %collective-permute-start.5 = (bf16[512,512]{1,0:T(8,128)(2,1)S(1)}, bf16[512,512]{1,0:T(8,128)(2,1)S(1)}, u32[]{:S(2)}, u32[]{:S(2)}) collective-permute-start(bf16[512,512]{1,0:T(8,128)(2,1)S(1)} %get-tuple-element.20), channel_id=1, source_target_pairs={{0,16},{16,32},{32,48},{48,64},{64,80},{80,96},{96,112},{112,128},... | collective-permute-start | bytes 1572872 | tf_op jit(solution)/shard_map/ppermute | solution.py:387
  84.8 6.7 %collective-permute-start.6 = (bf16[64,512]{1,0:T(8,128)(2,1)S(1)}, bf16[64,512]{1,0:T(8,128)(2,1)S(1)}, u32[]{:S(2)}, u32[]{:S(2)}) collective-permute-start(bf16[64,512]{1,0:T(8,128)(2,1)S(1)} %get-tuple-element.22), channel_id=1, source_target_pairs={{0,496},{16,480},{32,464},{48,448},{64,432},{80,416},{96,400},{112... | collective-permute-start | bytes 196616 | tf_op jit(solution)/shard_map/ppermute | solution.py:385
  91.6 12.1 %all_to_all.23 = f32[32,1,128]{2,1,0:T(1,128)S(1)} all-to-all(f32[32,1,128]{2,1,0:T(1,128)S(1)} %bitcast.44), channel_id=1, replica_groups=mesh['section'=32,'dp'=16] {'section'}, dimensions={0} | all-to-all | bytes 32768 | tf_op jit(solution)/shard_map/all_to_all | solution.py:388
  103.6 0.0 collective-permute-done.6.mate
  103.6 0.7 shard_map.176
  104.3 0.0 collective-permute-done.2
  104.3 0.0 collective-permute-done.3
  104.3 0.0 collective-permute-done.4
  104.4 0.0 collective-permute-done.5
  104.4 0.8 copy.24
  105.2 0.8 copy.25
  106.0 0.8 copy.26
  106.7 0.8 copy.27
  (10 shorter events, 0.0 us)
Async XLA Ops:
  0.6 11.6 %copy-start = (bf16[32,8192]{1,0:T(8,128)(2,1)S(1)}, bf16[32,8192]{1,0:T(8,128)(2,1)}, u32[]{:S(2)}) copy-start(bf16[32,8192]{1,0:T(8,128)(2,1)} %param.19) | copy-start | bytes 1572868
  0.6 17.0 %collective-permute-start = (bf16[32,512]{1,0:T(8,128)(2,1)}, bf16[32,512]{1,0:T(8,128)(2,1)S(1)}, u32[]{:S(2)}, u32[]{:S(2)}) collective-permute-start(bf16[32,512]{1,0:T(8,128)(2,1)} %bitcast.40), channel_id=1, source_target_pairs={{0,496},{16,480},{32,464},{48,448},{64,432},{80,416},{96,400},{112... | collective-permute-start | bytes 98312 | tf_op jit(solution)/shard_map/ppermute | solution.py:316
  9.6 9.4 %collective-permute-start.1 = (bf16[32,512]{1,0:T(8,128)(2,1)}, bf16[32,512]{1,0:T(8,128)(2,1)S(1)}, u32[]{:S(2)}, u32[]{:S(2)}) collective-permute-start(bf16[32,512]{1,0:T(8,128)(2,1)} %bitcast.35), channel_id=1, source_target_pairs={{0,496},{16,480},{32,464},{48,448},{64,432},{80,416},{96,400},{112... | collective-permute-start | bytes 98312 | tf_op jit(solution)/shard_map/ppermute | solution.py:317
  12.2 0.8 copy-start.8
  12.2 0.8 copy-start.9
  13.0 1.0 copy-start.1
  14.1 1.0 copy-start.3
  15.1 1.0 copy-start.5
  16.1 2.8 %copy-start.2 = (bf16[1,512,512]{2,1,0:T(8,128)(2,1)S(1)}, bf16[1,512,512]{2,1,0:T(8,128)(2,1)}, u32[]{:S(2)}) copy-start(bf16[1,512,512]{2,1,0:T(8,128)(2,1)} %param.13) | copy-start | bytes 1572868
  16.1 2.8 %copy-start.7 = (bf16[1,512,512]{2,1,0:T(8,128)(2,1)S(1)}, bf16[1,512,512]{2,1,0:T(8,128)(2,1)}, u32[]{:S(2)}) copy-start(bf16[1,512,512]{2,1,0:T(8,128)(2,1)} %param.15) | copy-start | bytes 1572868
  19.9 28.0 %copy-start.11 = (s32[512]{0:T(512)S(1)}, s32[512]{0:T(512)}, u32[]{:S(2)}) copy-start(s32[512]{0:T(512)} %param.21) | copy-start | bytes 6148
  48.0 0.7 copy-start.10
  48.0 0.7 copy-start.12
  48.0 0.7 copy-start.13
  50.4 19.3 %copy-start.4 = (bf16[1,512,512]{2,1,0:T(8,128)(2,1)S(1)}, bf16[1,512,512]{2,1,0:T(8,128)(2,1)}, u32[]{:S(2)}) copy-start(bf16[1,512,512]{2,1,0:T(8,128)(2,1)} %param.12) | copy-start | bytes 1572868
  69.7 7.7 %copy-start.6 = (bf16[1,512,512]{2,1,0:T(8,128)(2,1)S(1)}, bf16[1,512,512]{2,1,0:T(8,128)(2,1)}, u32[]{:S(2)}) copy-start(bf16[1,512,512]{2,1,0:T(8,128)(2,1)} %param.14) | copy-start | bytes 1572868
  70.1 34.2 %collective-permute-start.2 = (bf16[512,512]{1,0:T(8,128)(2,1)S(1)}, bf16[512,512]{1,0:T(8,128)(2,1)S(1)}, u32[]{:S(2)}, u32[]{:S(2)}) collective-permute-start(bf16[512,512]{1,0:T(8,128)(2,1)S(1)} %get-tuple-element.17), channel_id=1, source_target_pairs={{0,16},{16,32},{32,48},{48,64},{64,80},{80,96},{96,112},{112,128},... | collective-permute-start | bytes 1572872 | tf_op jit(solution)/shard_map/ppermute | solution.py:369
  75.5 28.9 %collective-permute-start.3 = (bf16[512,512]{1,0:T(8,128)(2,1)S(1)}, bf16[512,512]{1,0:T(8,128)(2,1)S(1)}, u32[]{:S(2)}, u32[]{:S(2)}) collective-permute-start(bf16[512,512]{1,0:T(8,128)(2,1)S(1)} %get-tuple-element.18), channel_id=1, source_target_pairs={{16,0},{32,16},{48,32},{64,48},{80,64},{96,80},{112,96},{128,112},... | collective-permute-start | bytes 1572872 | tf_op jit(solution)/shard_map/ppermute | solution.py:370
  79.3 25.1 %collective-permute-start.4 = (bf16[512,512]{1,0:T(8,128)(2,1)S(1)}, bf16[512,512]{1,0:T(8,128)(2,1)S(1)}, u32[]{:S(2)}, u32[]{:S(2)}) collective-permute-start(bf16[512,512]{1,0:T(8,128)(2,1)S(1)} %get-tuple-element.19), channel_id=1, source_target_pairs={{16,0},{32,16},{48,32},{64,48},{80,64},{96,80},{112,96},{128,112},... | collective-permute-start | bytes 1572872 | tf_op jit(solution)/shard_map/ppermute | solution.py:386
  81.2 23.2 %collective-permute-start.5 = (bf16[512,512]{1,0:T(8,128)(2,1)S(1)}, bf16[512,512]{1,0:T(8,128)(2,1)S(1)}, u32[]{:S(2)}, u32[]{:S(2)}) collective-permute-start(bf16[512,512]{1,0:T(8,128)(2,1)S(1)} %get-tuple-element.20), channel_id=1, source_target_pairs={{0,16},{16,32},{32,48},{48,64},{64,80},{80,96},{96,112},{112,128},... | collective-permute-start | bytes 1572872 | tf_op jit(solution)/shard_map/ppermute | solution.py:387
  84.8 18.8 %collective-permute-start.6 = (bf16[64,512]{1,0:T(8,128)(2,1)S(1)}, bf16[64,512]{1,0:T(8,128)(2,1)S(1)}, u32[]{:S(2)}, u32[]{:S(2)}) collective-permute-start(bf16[64,512]{1,0:T(8,128)(2,1)S(1)} %get-tuple-element.22), channel_id=1, source_target_pairs={{0,496},{16,480},{32,464},{48,448},{64,432},{80,416},{96,400},{112... | collective-permute-start | bytes 196616 | tf_op jit(solution)/shard_map/ppermute | solution.py:385

commit v2 on v1

--- a/solution.py
+++ b/solution.py
@@ -48,17 +48,69 @@
     return jnp.where(flag, weights.astype(F32), 0.0).astype(BF16)
 
 
-def first_partial(meta, x_d, x_u, c_d, a_d, b_d, gain, cand, out):
+def in_hbm(value):
+    return pltpu.with_memory_space_constraint(value, pltpu.HBM)
+
+
+def packed(a_hbm, b_hbm, w, sems):
+    copies = [
+        pltpu.make_async_copy(a_hbm, w.at[0:R], sems.at[0]),
+        pltpu.make_async_copy(b_hbm, w.at[R : 2 * R], sems.at[1]),
+    ]
+    for copy in copies:
+        copy.start()
+    for copy in copies:
+        copy.wait()
+
+
+def first_partial(
+    meta,
+    x_d_hbm,
+    x_u_hbm,
+    c_d_hbm,
+    c_u_hbm,
+    gain_hbm,
+    cand_hbm,
+    ids_d_hbm,
+    ids_u_hbm,
+    w_d,
+    out,
+    x_d,
+    x_u,
+    c_d,
+    c_u,
+    gain,
+    cand,
+    ids_d,
+    ids_u,
+    sems,
+):
     sections = meta[2]
     is_first = meta[1] == 0
     is_last = meta[1] == sections - 1
     chunks = out.shape[0]
     width = x_d.shape[1]
+    here = pl.ds(pl.multiple_of(meta[0] * width, width), width)
+    get_x_d = pltpu.make_async_copy(x_d_hbm, x_d, sems.at[0])
+    get_c_d = pltpu.make_async_copy(c_d_hbm, c_d, sems.at[1])
+    get_x_u = pltpu.make_async_copy(x_u_hbm, x_u, sems.at[2])
+    get_c_u = pltpu.make_async_copy(c_u_hbm, c_u, sems.at[3])
+    get_gain = pltpu.make_async_copy(gain_hbm.at[:, here], gain, sems.at[4])
+    get_cand = pltpu.make_async_copy(cand_hbm.at[:, here], cand, sems.at[5])
+    get_ids_d = pltpu.make_async_copy(ids_d_hbm, ids_d, sems.at[6])
+    get_ids_u = pltpu.make_async_copy(ids_u_hbm, ids_u, sems.at[7])
+    for copy in (get_x_d, get_c_d, get_x_u, get_gain, get_cand, get_c_u, get_ids_d, get_ids_u):
+        copy.start()
+    a_d, b_d = w_d[0:R], w_d[R : 2 * R]
     zero = jnp.zeros((R, width), BF16)
-    wx = jnp.concatenate([a_d[...], zero, gated(b_d[...], is_last), zero], axis=0)
-    wc = jnp.concatenate([zero, zero, gated(b_d[...], jnp.logical_not(is_last)), zero], axis=0)
+    wx = jnp.concatenate([a_d, zero, gated(b_d, is_last), zero], axis=0)
+    wc = jnp.concatenate([zero, zero, gated(b_d, jnp.logical_not(is_last)), zero], axis=0)
+    out[:, 64:96, :] = jnp.zeros((chunks, R, LANES), BF16)
+    get_x_d.wait()
+    get_c_d.wait()
     main = nt(x_d[...], wx) + nt(c_d[...], wc)
     out[:, 0:R, :] = main.astype(BF16).reshape(chunks, R, LANES)
+    get_x_u.wait()
     rows = []
     for block in (x_d[...], x_u[...]):
         row = squares_row(block)
@@ -71,7 +123,8 @@
         piece = [row[:, start : start + LANES] for row in rows]
         tail = jnp.concatenate([pad] + piece + [pad[0:4]], axis=0)
         out[j, 96:ROWS, :] = tail.astype(BF16)
-    out[:, 64:96, :] = jnp.zeros((chunks, R, LANES), BF16)
+    get_gain.wait()
+    get_cand.wait()
 
     def logits_of(block):
         high, low = halves(columns_of(gain, cand))
@@ -90,15 +143,20 @@
     def _():
         out[:, 32:64, :] = jnp.zeros((chunks, R, LANES), BF16)
 
-
-def second_partial(meta, partial, x_u, c_u, a_u, b_u, b_d, gain, cand, out):
+    get_c_u.wait()
+    get_ids_d.wait()
+    get_ids_u.wait()
+
+
+def second_partial(meta, partial, x_u, c_u, w_u, w_d, gain, cand, out):
     is_first = meta[1] == 0
     is_last = meta[1] == meta[2] - 1
     chunks = out.shape[0]
     width = x_u.shape[1]
+    a_u, b_u = w_u[0:R], w_u[R : 2 * R]
     zero = jnp.zeros((R, width), BF16)
-    wx = jnp.concatenate([zero, a_u[...], zero, gated(b_u[...], is_first)], axis=0)
-    wc = jnp.concatenate([zero, zero, zero, gated(b_u[...], jnp.logical_not(is_first))], axis=0)
+    wx = jnp.concatenate([zero, a_u, zero, gated(b_u, is_first)], axis=0)
+    wc = jnp.concatenate([zero, zero, zero, gated(b_u, jnp.logical_not(is_first))], axis=0)
     main = nt(x_u[...], wx) + nt(c_u[...], wc)
     main = main.reshape(chunks, R, LANES) + partial[:, 0:R, :].astype(F32)
     out[:, 0:R, :] = main.astype(BF16)
@@ -106,18 +164,19 @@
 
     @pl.when(jnp.logical_or(is_first, is_last))
     def _():
-        b_e = jnp.where(is_last, b_d[...].astype(F32), b_u[...].astype(F32)).astype(BF16)
+        b_d = w_d[R : 2 * R]
+        b_e = jnp.where(is_last, b_d.astype(F32), b_u.astype(F32)).astype(BF16)
         high, low = halves(columns_of(gain, cand))
         cross = nt(b_e, high) + nt(b_e, low)
         own = nt(b_e, b_e)
-        packed = jnp.concatenate([own[8 * r : 8 * r + 8] for r in range(4)], axis=1)
-        tail = jnp.concatenate([packed, jnp.zeros((8, LANES), F32)], axis=0)
+        folded = jnp.concatenate([own[8 * r : 8 * r + 8] for r in range(4)], axis=1)
+        tail = jnp.concatenate([folded, jnp.zeros((8, LANES), F32)], axis=0)
         out[:, 64:96, :] = jnp.broadcast_to(cross.astype(BF16)[None], (chunks, R, LANES))
         held = partial[:, 96:ROWS, :].astype(F32) + tail[None]
         out[:, 96:ROWS, :] = held.astype(BF16)
 
 
-def middle(meta, offsets, loss_weights, received, down_ids, up_ids, out):
+def middle(meta, received, down_ids, up_ids, out):
     place = meta[0]
     is_first = meta[1] == 0
     is_last = meta[1] == meta[2] - 1
@@ -125,9 +184,11 @@
     chunks = received.shape[0]
     inverse = 1.0 / meta[3].astype(F32)
     heads = LANES // R
+    offsets = [meta[4 + k] for k in range(heads)]
+    loss_weights = [meta[4 + heads + k] for k in range(heads)]
     total = jnp.sum(received[...].astype(F32), axis=0)
     main, base_logits, cross = total[0:32], total[32:64], total[64:96]
-    packed, square_rows = total[96:104], total[104:108]
+    folded, square_rows = total[96:104], total[104:108]
     lane = lax.broadcasted_iota(jnp.int32, (R, LANES), 1)
     token = lax.broadcasted_iota(jnp.int32, (R, LANES), 0)
     base = R * lax.rem(place, LANES // R)
@@ -150,7 +211,7 @@
 
     act_e = jnp.where(is_first, act[:, R : 2 * R], act[:, 0:R])
     cot_e = jnp.where(is_first, main[:, 3 * R :], main[:, 2 * R : 3 * R])
-    own = jnp.concatenate([packed[:, R * r : R * r + R] for r in range(4)], axis=0)
+    own = jnp.concatenate([folded[:, R * r : R * r + R] for r in range(4)], axis=0)
     act_own = nn(act_e, own, HIGH)
     out_b = cot_e + act_own
     square_e = jnp.where(is_first, square_u, square_d)
@@ -244,36 +305,29 @@
     return jnp.concatenate([weights if k == group else zero for k in range(LANES // R)], axis=0)
 
 
-def outputs(received, x_d, x_u, b_d, b_u, y_d, y_u, loss):
-    act = tokens_of(received, 0)
-    y_d[...] = (x_d[...].astype(F32) + nn(act, at_rows(b_d[...], 0))).astype(BF16)
-    y_u[...] = (x_u[...].astype(F32) + nn(act, at_rows(b_u[...], 1))).astype(BF16)
-    rows = jnp.sum(received[:, 64:BACK_ROWS, :].astype(F32), axis=0)
-    total = rows[6:7] + rows[7:8] + rows[8:9]
-    loss[...] = jnp.broadcast_to(total, loss.shape)
-
-
-def backward(meta, received, x_d, x_u, c_d, c_u, a_d, b_d, a_u, b_u, gain, cand, dx_d, dx_u, g_d, g_u, cot):
+def backward(meta, received, x_d, x_u, c_d, c_u, w_d, w_u, gain, cand, ahead, behind, g_d, g_u, loss, cot):
     is_first = meta[1] == 0
     is_last = meta[1] == meta[2] - 1
     act = tokens_of(received, 0)
     work = (
-        (1, x_u, c_u, a_u, b_u, dx_u, g_u, is_first),
-        (0, x_d, c_d, a_d, b_d, dx_d, g_d, is_last),
+        (1, x_u, c_u, w_u, behind.at[0], ahead.at[1], g_u, is_first),
+        (0, x_d, c_d, w_d, ahead.at[0], behind.at[1], g_d, is_last),
     )
-    for side, x, c, a, b, dx, g, end in work:
+    for side, x, c, w, y, dx, g, end in work:
+        final = x[...].astype(F32) + nn(act, at_rows(w[R : 2 * R], side))
+        y[...] = final.astype(BF16)
         cot[...] = c[...].astype(F32)
 
         @pl.when(end)
         def _():
             high, low = halves(columns_of(gain, cand))
             grad = tokens_of(received, 32)
-            final = x[...].astype(F32) + nn(act, at_rows(b[...], side))
-            cot[...] = nn(grad, high) + nn(grad, low) - coefficient(received, 4) * final
+            again = x[...].astype(F32) + nn(act, at_rows(w[R : 2 * R], side))
+            cot[...] = nn(grad, high) + nn(grad, low) - coefficient(received, 4) * again
 
         held = cot[...]
         wide = x[...].astype(F32)
-        back = held + nn(act, at_rows(a[...], 2 + side)) - coefficient(received, 2 * side) * wide
+        back = held + nn(act, at_rows(w[0:R], 2 + side)) - coefficient(received, 2 * side) * wide
         dx[...] = back.astype(BF16)
         by_cot = tn(act, held.astype(BF16))
         by_x = tn(act, x[...])
@@ -281,13 +335,26 @@
             [by_x[64 + R * side : 64 + R * side + R], by_cot[R * side : R * side + R]], axis=0
         )
         g[...] = grads.astype(g.dtype)
-
-
-def finish(g_d, mate, losses, grad_a, grad_b, loss):
+    rows = jnp.sum(received[:, 64:BACK_ROWS, :].astype(F32), axis=0)
+    total = rows[6:7] + rows[7:8] + rows[8:9]
+    loss[...] = jnp.broadcast_to(total, loss.shape)
+
+
+def finish(ahead, behind, g_d, mate, losses, down_next, up_next, down_back, up_back, grad_a, grad_b, loss, sems):
+    copies = [
+        pltpu.make_async_copy(ahead.at[0], down_next, sems.at[0]),
+        pltpu.make_async_copy(behind.at[0], up_next, sems.at[1]),
+        pltpu.make_async_copy(behind.at[1], down_back, sems.at[2]),
+        pltpu.make_async_copy(ahead.at[1], up_back, sems.at[3]),
+    ]
+    for copy in copies:
+        copy.start()
     total = g_d[...] + mate[...].astype(F32)
     grad_a[...] = total[0:R]
     grad_b[...] = total[R : 2 * R]
     loss[0] = jnp.sum(losses[:, 0:1])
+    for copy in copies:
+        copy.wait()
 
 
 def shards(
@@ -308,95 +375,106 @@
     groups = lax.axis_size("dp")
     position = lax.axis_index("section")
     place = lax.axis_index("dp")
-    x_d, x_u, c_d, c_u = down_in[0], up_in[0], down_cot[0], up_cot[0]
-    tokens, local_width = x_d.shape
-    a_d = adapt_a[0].T
-    b_d = adapt_b[0]
+    tokens, local_width = down_in.shape[1:]
+    heads, candidates = head_gain.shape[0], cand.shape[0]
     mirror = [(i, sections - 1 - i) for i in range(sections)]
-    a_u = lax.ppermute(a_d, "section", mirror)
-    b_u = lax.ppermute(b_d, "section", mirror)
-    whole = jnp.int32(sections), jnp.int32(head_gain.shape[1])
-    meta = jnp.stack([place.astype(jnp.int32), position.astype(jnp.int32), *whole])
-    gain_part = lax.dynamic_slice_in_dim(head_gain, place * local_width, local_width, 1)
-    cand_part = lax.dynamic_slice_in_dim(cand, place * local_width, local_width, 1)
+    further = [(i, i + 1) for i in range(sections - 1)]
+    nearer = [(i + 1, i) for i in range(sections - 1)]
     smem = pl.BlockSpec(memory_space=pltpu.SMEM)
     vmem = pl.BlockSpec(memory_space=pltpu.VMEM)
+    hbm = pl.BlockSpec(memory_space=pltpu.HBM)
     params = pltpu.CompilerParams(vmem_limit_bytes=48 << 20)
-
-    send = jax.ShapeDtypeStruct((groups, ROWS, LANES), BF16)
+    shape = jax.ShapeDtypeStruct
+    wide = shape((tokens, local_width), BF16)
+    both = shape((2, tokens, local_width), BF16)
+
+    w_d = pl.pallas_call(
+        packed,
+        out_shape=shape((2 * R, local_width), BF16),
+        in_specs=[hbm] * 2,
+        out_specs=vmem,
+        scratch_shapes=[pltpu.SemaphoreType.DMA((2,))],
+        compiler_params=params,
+    )(in_hbm(adapt_a[0].T), in_hbm(adapt_b[0]))
+    w_u = lax.ppermute(w_d, "section", mirror)
+    sizes = jnp.int32(sections), jnp.int32(head_gain.shape[1])
+    meta = jnp.stack([place.astype(jnp.int32), position.astype(jnp.int32), *sizes])
+    meta = jnp.concatenate([meta, offsets, loss_weights])
+    id_rows = (tokens // LANES, LANES)
+    ids = down_ids.reshape(id_rows), up_ids.reshape(id_rows)
+    fetched = (down_in[0], up_in[0], down_cot[0], up_cot[0], head_gain, cand, *ids)
+
+    send = shape((groups, ROWS, LANES), BF16)
+    partial, x_d, x_u, c_d, c_u, gain_part, cand_part, ids_d, ids_u = pl.pallas_call(
+        first_partial,
+        out_shape=(
+            send,
+            wide,
+            wide,
+            wide,
+            wide,
+            shape((heads, local_width), F32),
+            shape((candidates, local_width), BF16),
+            shape(id_rows, jnp.int32),
+            shape(id_rows, jnp.int32),
+        ),
+        in_specs=[smem] + [hbm] * 8 + [vmem],
+        out_specs=(vmem,) * 9,
+        scratch_shapes=[pltpu.SemaphoreType.DMA((8,))],
+        compiler_params=params,
+    )(meta, *(in_hbm(held) for held in fetched), w_d)
     partial = pl.pallas_call(
-        first_partial,
+        second_partial,
         out_shape=send,
         in_specs=[smem] + [vmem] * 7,
         out_specs=vmem,
         compiler_params=params,
-    )(meta, x_d, x_u, c_d, a_d, b_d, gain_part, cand_part)
-    partial = pl.pallas_call(
-        second_partial,
-        out_shape=send,
-        in_specs=[smem] + [vmem] * 8,
+    )(meta, partial, x_u, c_u, w_u, w_d, gain_part, cand_part)
+    received = lax.all_to_all(partial, "dp", 0, 0)
+
+    back = pl.pallas_call(
+        middle,
+        out_shape=shape((groups, BACK_ROWS, LANES), BF16),
+        in_specs=[smem] + [vmem] * 3,
         out_specs=vmem,
         compiler_params=params,
-    )(meta, partial, x_u, c_u, a_u, b_u, b_d, gain_part, cand_part)
-    received = lax.all_to_all(partial, "dp", 0, 0)
-
-    back = pl.pallas_call(
-        middle,
-        out_shape=jax.ShapeDtypeStruct((groups, BACK_ROWS, LANES), BF16),
-        in_specs=[smem] * 3 + [vmem] * 3,
-        out_specs=vmem,
-        compiler_params=params,
-    )(
-        meta,
-        offsets,
-        loss_weights,
-        received,
-        down_ids.reshape(tokens // LANES, LANES),
-        up_ids.reshape(tokens // LANES, LANES),
-    )
+    )(meta, received, ids_d, ids_u)
     gathered = lax.all_to_all(back, "dp", 0, 0)
 
-    wide = jax.ShapeDtypeStruct((tokens, local_width), BF16)
-    y_d, y_u, loss_rows = pl.pallas_call(
-        outputs,
-        out_shape=(wide, wide, jax.ShapeDtypeStruct((sections, LANES), F32)),
-        in_specs=[vmem] * 5,
-        out_specs=(vmem,) * 3,
-        compiler_params=params,
-    )(gathered, x_d, x_u, b_d, b_u)
-    ahead = [(i, i + 1) for i in range(sections - 1)]
-    behind = [(i + 1, i) for i in range(sections - 1)]
-    down_next = lax.ppermute(y_d, "section", ahead)
-    up_next = lax.ppermute(y_u, "section", behind)
-
-    dx_d, dx_u, g_d, g_u = pl.pallas_call(
+    ahead, behind, g_d, g_u, loss_rows = pl.pallas_call(
         backward,
         out_shape=(
-            wide,
-            wide,
-            jax.ShapeDtypeStruct((2 * R, local_width), F32),
-            jax.ShapeDtypeStruct((2 * R, local_width), BF16),
+            both,
+            both,
+            shape((2 * R, local_width), F32),
+            shape((2 * R, local_width), BF16),
+            shape((sections, LANES), F32),
         ),
-        in_specs=[smem] + [vmem] * 11,
-        out_specs=(vmem,) * 4,
+        in_specs=[smem] + [vmem] * 9,
+        out_specs=(vmem,) * 5,
         scratch_shapes=[pltpu.VMEM((tokens, local_width), F32)],
         compiler_params=params,
-    )(meta, gathered, x_d, x_u, c_d, c_u, a_d, b_d, a_u, b_u, gain_part, cand_part)
+    )(meta, gathered, x_d, x_u, c_d, c_u, w_d, w_u, gain_part, cand_part)
+    ahead = lax.ppermute(ahead, "section", further)
+    behind = lax.ppermute(behind, "section", nearer)
     mate = lax.ppermute(g_u, "section", mirror)
-    down_back = lax.ppermute(dx_d, "section", behind)
-    up_back = lax.ppermute(dx_u, "section", ahead)
     losses = lax.all_to_all(loss_rows, "section", 0, 0, tiled=True)
-    grad_a, grad_b, loss = pl.pallas_call(
+    down_next, up_next, down_back, up_back, grad_a, grad_b, loss = pl.pallas_call(
         finish,
         out_shape=(
-            jax.ShapeDtypeStruct((R, local_width), F32),
-            jax.ShapeDtypeStruct((R, local_width), F32),
-            jax.ShapeDtypeStruct((1,), F32),
+            wide,
+            wide,
+            wide,
+            wide,
+            shape((R, local_width), F32),
+            shape((R, local_width), F32),
+            shape((1,), F32),
         ),
-        in_specs=[vmem] * 3,
-        out_specs=(vmem, vmem, smem),
+        in_specs=[vmem] * 5,
+        out_specs=(hbm,) * 4 + (vmem, vmem, smem),
+        scratch_shapes=[pltpu.SemaphoreType.DMA((4,))],
         compiler_params=params,
-    )(g_d, mate, losses)
+    )(ahead, behind, g_d, mate, losses)
     return (
         down_next[None],
         up_next[None],

time: 108 us -> 98.5 us (0.912)
  starting transfers between devices: 30.4 us -> 22.2 us
  local copies, waits for them, and re-layouts: 8.4 us -> 0.74 us
  Pallas kernels: 7.17 us -> 11.2 us
  blocking collectives: 59.3 us -> 63.3 us
  waiting for transfers between devices: 1.3 us -> 0.01 us
    ppermute x6 -> x3, starting transfers between devices: 23.7 us -> 15.8 us  [the longest x1 8.81 us: shards(): w_u = lax.ppermute(w_d, 'section', mirror)]
    unnamed x32 -> x4, local copies, waits for them, and re-layouts: 7.69 us -> 0.66 us
    pallas_call x5, Pallas kernels: 6.2 us -> 10.2 us  [the longest x1 3.47 us: shards(): pl.pallas_call(first_partial, out_shape=(send, wide, wide, wide, wide, sh...]
    all_to_all x1, blocking collectives: 12.1 us -> 14.9 us  [shards(): losses = lax.all_to_all(loss_rows, 'section', 0, 0, tiled=True)]
    ppermute x6 -> x3, waiting for transfers between devices: 1.3 us -> 0.01 us  [the longest x1 0.01 us: shards(): w_u = lax.ppermute(w_d, 'section', mirror)]
  transfers between devices with their start and end apart: 7 -> 4, of which waited for: 1 -> 0; matrix products, arithmetic and copies ran while one was open for 1% -> 0% of each run, Pallas kernels for 4% -> 4%
where the time goes in v2:
time: 98.5 us; the launch traced here: 98.1 us
  blocking collectives  63.3 us (64%)
  starting transfers between devices  22.2 us (23%)
  Pallas kernels  11.2 us (11%)
    all_to_all x1, blocking collectives, shards(): received = lax.all_to_all(partial, 'dp', 0, 0)  28.7 us
    all_to_all x1, blocking collectives, shards(): gathered = lax.all_to_all(back, 'dp', 0, 0)  19.6 us
    all_to_all x1, blocking collectives, shards(): losses = lax.all_to_all(loss_rows, 'section', 0, 0, tiled=True)  14.9 us
    ppermute x1, starting transfers between devices, shards(): w_u = lax.ppermute(w_d, 'section', mirror)  8.81 us
    ppermute x1, starting transfers between devices, shards(): mate = lax.ppermute(g_u, 'section', mirror)  6.41 us
    ppermute x1, starting transfers between devices, shards(): ahead = lax.ppermute(ahead, 'section', further)  4.92 us
    pallas_call x1, Pallas kernels, shards(): pl.pallas_call(first_partial, out_shape=(send, wide, wide, wide, wide, sh...  3.47 us
    pallas_call x1, Pallas kernels, shards(): pl.pallas_call(backward, out_shape=(both, both, shape((2 * R, local_width...  2.16 us
  transfers between devices with their start and end apart: 4, of which 0 were waited for; matrix products, arithmetic and copies ran while one was open for 0% of the time, Pallas kernels for 4%

profile of v2, /device:TPU:1, one launch (start us, length us, event | category | flops | bytes accessed | tf_op | source)
XLA Modules:
  0.0 98.1 jit_solution(16250937159871616751)
XLA Ops:
  0.6 0.8 shard_map.171.w_d
  1.4 8.8 %collective-permute-start = (bf16[64,512]{1,0:T(8,128)(2,1)S(1)}, bf16[64,512]{1,0:T(8,128)(2,1)S(1)}, u32[]{:S(2)}, u32[]{:S(2)}) collective-permute-start(bf16[64,512]{1,0:T(8,128)(2,1)S(1)} %shard_map.171.w_d), channel_id=1, source_target_pairs={{0,496},{16,480},{32,464},{48,448},{64,432},{80,416},{96,400},{112... | collective-permute-start | bytes 196616 | tf_op jit(solution)/shard_map/ppermute | solution.py:399
  10.3 0.0 copy-start
  10.3 0.0 copy-start.1
  10.3 0.6 copy-done
  10.9 0.0 copy-done.1
  10.9 0.1 concatenate.3.meta
  11.0 3.5 %shard_map.172 = (bf16[16,112,128]{2,1,0:T(8,128)(2,1)S(1)}, bf16[512,512]{1,0:T(8,128)(2,1)S(1)}, bf16[512,512]{1,0:T(8,128)(2,1)S(1)}, bf16[512,512]{1,0:T(8,1...) custom-call(s32[12]{0:T(128)S(1)} %concatenate.3.meta, ...), custom_call_target="tpu_custom_call" | custom-call | tf_op jit(solution)/shard_map/pallas_call | solution.py:408
  14.5 0.0 collective-permute-done.w_u
  14.5 1.0 shard_map.173
  15.5 28.7 %all_to_all.21.received = bf16[16,112,128]{2,1,0:T(8,128)(2,1)S(1)} all-to-all(bf16[16,112,128]{2,1,0:T(8,128)(2,1)S(1)} %shard_map.173), channel_id=1, replica_groups=mesh['section'=32,'dp'=16] {'dp'}, dimensions={0} | all-to-all | bytes 917504 | tf_op jit(solution)/shard_map/all_to_all | solution.py:433
  44.2 1.8 %shard_map.174 = bf16[16,80,128]{2,1,0:T(8,128)(2,1)S(1)} custom-call(s32[12]{0:T(128)S(1)} %concatenate.3.meta, bf16[16,112,128]{2,1,0:T(8,128)(2,1)S(1)} %all_to_all.21.received, s32[4,128]{1,0:T(4,128)S(1)} %get-tuple-element.33.down_ids, s32[4,128]{1,0:T(4,128)S(1)} %get-tuple-element.34.up_ids), custom_call_target="tpu_custom_call" | custom-call | tf_op jit(solution)/shard_map/pallas_call | solution.py:435
  46.0 19.6 %all_to_all.22.received = bf16[16,80,128]{2,1,0:T(8,128)(2,1)S(1)} all-to-all(bf16[16,80,128]{2,1,0:T(8,128)(2,1)S(1)} %shard_map.174), channel_id=1, replica_groups=mesh['section'=32,'dp'=16] {'dp'}, dimensions={0} | all-to-all | bytes 655360 | tf_op jit(solution)/shard_map/all_to_all | solution.py:442
  65.6 2.2 %shard_map.175 = (bf16[2,512,512]{2,1,0:T(8,128)(2,1)S(1)}, bf16[2,512,512]{2,1,0:T(8,128)(2,1)S(1)}, f32[64,512]{1,0:T(8,128)S(1)}, bf16[64,512]{1,0:T(8,128)(2,1)S(1)}, f32[32,128]{1,0:T(8,128)S(1)}) custom-call(s32[12]{0:T(128)S(1)} %concatenate.3.meta, bf16[16,80,128]{2,1,0:T(8,128)(2,1)S(1)} %all_to_all.22.received, ...), custom_call_target="tpu_custom_call" | custom-call | tf_op jit(solution)/shard_map/pallas_call | solution.py:444
  67.8 4.9 %collective-permute-start.1 = (bf16[2,512,512]{2,1,0:T(8,128)(2,1)S(1)}, bf16[2,512,512]{2,1,0:T(8,128)(2,1)S(1)}, u32[]{:S(2)}, u32[]{:S(2)}) collective-permute-start(bf16[2,512,512]{2,1,0:T(8,128)(2,1)S(1)} %get-tuple-element.37), channel_id=1, source_target_pairs={{0,16},{16,32},{32,48},{48,64},{64,80},{80,96},{96,112},{112,128},... | collective-permute-start | bytes 3145736 | tf_op jit(solution)/shard_map/ppermute | solution.py:458
  72.7 2.0 %collective-permute-start.2 = (bf16[2,512,512]{2,1,0:T(8,128)(2,1)S(1)}, bf16[2,512,512]{2,1,0:T(8,128)(2,1)S(1)}, u32[]{:S(2)}, u32[]{:S(2)}) collective-permute-start(bf16[2,512,512]{2,1,0:T(8,128)(2,1)S(1)} %get-tuple-element.38), channel_id=1, source_target_pairs={{16,0},{32,16},{48,32},{64,48},{80,64},{96,80},{112,96},{128,112},... | collective-permute-start | bytes 3145736 | tf_op jit(solution)/shard_map/ppermute | solution.py:459
  74.7 6.4 %collective-permute-start.3 = (bf16[64,512]{1,0:T(8,128)(2,1)S(1)}, bf16[64,512]{1,0:T(8,128)(2,1)S(1)}, u32[]{:S(2)}, u32[]{:S(2)}) collective-permute-start(bf16[64,512]{1,0:T(8,128)(2,1)S(1)} %get-tuple-element.40), channel_id=1, source_target_pairs={{0,496},{16,480},{32,464},{48,448},{64,432},{80,416},{96,400},{112... | collective-permute-start | bytes 196616 | tf_op jit(solution)/shard_map/ppermute | solution.py:460
  81.2 14.9 %all_to_all.23 = f32[32,1,128]{2,1,0:T(1,128)S(1)} all-to-all(f32[32,1,128]{2,1,0:T(1,128)S(1)} %bitcast.25), channel_id=1, replica_groups=mesh['section'=32,'dp'=16] {'section'}, dimensions={0} | all-to-all | bytes 32768 | tf_op jit(solution)/shard_map/all_to_all | solution.py:461
  96.1 0.0 collective-permute-done.3.mate
  96.1 0.0 collective-permute-done.1.ahead
  96.1 0.0 collective-permute-done.2.behind
  96.1 2.0 %shard_map.176 = (bf16[512,512]{1,0:T(8,128)(2,1)}, bf16[512,512]{1,0:T(8,128)(2,1)}, bf16[512,512]{1,0:T(8,128)(2,1)}, bf16[512,512]{1,0:T(8,128)(2,1)}, f32[32...) custom-call(bf16[2,512,512]{2,1,0:T(8,128)(2,1)S(1)} %collective-permute-done.1.ahead, ...), custom_call_target="tpu_custom_call" | custom-call | tf_op jit(solution)/shard_map/pallas_call | solution.py:462
Async XLA Ops:
  1.4 13.1 %collective-permute-start = (bf16[64,512]{1,0:T(8,128)(2,1)S(1)}, bf16[64,512]{1,0:T(8,128)(2,1)S(1)}, u32[]{:S(2)}, u32[]{:S(2)}) collective-permute-start(bf16[64,512]{1,0:T(8,128)(2,1)S(1)} %shard_map.171.w_d), channel_id=1, source_target_pairs={{0,496},{16,480},{32,464},{48,448},{64,432},{80,416},{96,400},{112... | collective-permute-start | bytes 196616 | tf_op jit(solution)/shard_map/ppermute | solution.py:399
  10.3 0.7 copy-start
  10.3 0.7 copy-start.1
  67.8 28.3 %collective-permute-start.1 = (bf16[2,512,512]{2,1,0:T(8,128)(2,1)S(1)}, bf16[2,512,512]{2,1,0:T(8,128)(2,1)S(1)}, u32[]{:S(2)}, u32[]{:S(2)}) collective-permute-start(bf16[2,512,512]{2,1,0:T(8,128)(2,1)S(1)} %get-tuple-element.37), channel_id=1, source_target_pairs={{0,16},{16,32},{32,48},{48,64},{64,80},{80,96},{96,112},{112,128},... | collective-permute-start | bytes 3145736 | tf_op jit(solution)/shard_map/ppermute | solution.py:458
  72.7 23.4 %collective-permute-start.2 = (bf16[2,512,512]{2,1,0:T(8,128)(2,1)S(1)}, bf16[2,512,512]{2,1,0:T(8,128)(2,1)S(1)}, u32[]{:S(2)}, u32[]{:S(2)}) collective-permute-start(bf16[2,512,512]{2,1,0:T(8,128)(2,1)S(1)} %get-tuple-element.38), channel_id=1, source_target_pairs={{16,0},{32,16},{48,32},{64,48},{80,64},{96,80},{112,96},{128,112},... | collective-permute-start | bytes 3145736 | tf_op jit(solution)/shard_map/ppermute | solution.py:459
  74.7 21.3 %collective-permute-start.3 = (bf16[64,512]{1,0:T(8,128)(2,1)S(1)}, bf16[64,512]{1,0:T(8,128)(2,1)S(1)}, u32[]{:S(2)}, u32[]{:S(2)}) collective-permute-start(bf16[64,512]{1,0:T(8,128)(2,1)S(1)} %get-tuple-element.40), channel_id=1, source_target_pairs={{0,496},{16,480},{32,464},{48,448},{64,432},{80,416},{96,400},{112... | collective-permute-start | bytes 196616 | tf_op jit(solution)/shard_map/ppermute | solution.py:460

commit v3 on v2

--- a/solution.py
+++ b/solution.py
@@ -9,10 +9,14 @@
 F32 = jnp.float32
 BF16 = jnp.bfloat16
 HIGH = lax.Precision.HIGHEST
-ROWS = 112
-BACK_ROWS = 80
 R = 32
+M = 32
 LANES = 128
+PER = 64
+CROSS = 2 * PER
+EXTRA = CROSS + R
+ROWS = EXTRA + 16
+BACK_ROWS = 2 * PER + 16
 
 
 def nt(a, b, precision=None):
@@ -105,31 +109,31 @@
     zero = jnp.zeros((R, width), BF16)
     wx = jnp.concatenate([a_d, zero, gated(b_d, is_last), zero], axis=0)
     wc = jnp.concatenate([zero, zero, gated(b_d, jnp.logical_not(is_last)), zero], axis=0)
-    out[:, 64:96, :] = jnp.zeros((chunks, R, LANES), BF16)
+    out[:, CROSS:EXTRA, :] = jnp.zeros((chunks, R, LANES), BF16)
     get_x_d.wait()
     get_c_d.wait()
     main = nt(x_d[...], wx) + nt(c_d[...], wc)
-    out[:, 0:R, :] = main.astype(BF16).reshape(chunks, R, LANES)
+    out[:, 0:PER, :] = main.astype(BF16).reshape(chunks, PER, LANES)
     get_x_u.wait()
     rows = []
     for block in (x_d[...], x_u[...]):
         row = squares_row(block)
         high = row.astype(BF16).astype(F32)
         rows += [high, row - high]
-    per = LANES // R
+    per = LANES // PER
     pad = jnp.zeros((8, LANES), F32)
     for j in range(chunks):
         start = (j // per) * LANES
         piece = [row[:, start : start + LANES] for row in rows]
         tail = jnp.concatenate([pad] + piece + [pad[0:4]], axis=0)
-        out[j, 96:ROWS, :] = tail.astype(BF16)
+        out[j, EXTRA:ROWS, :] = tail.astype(BF16)
     get_gain.wait()
     get_cand.wait()
 
     def logits_of(block):
         high, low = halves(columns_of(gain, cand))
         value = nt(block, high) + nt(block, low)
-        out[:, 32:64, :] = value.astype(BF16).reshape(chunks, R, LANES)
+        out[:, PER:CROSS, :] = value.astype(BF16).reshape(chunks, PER, LANES)
 
     @pl.when(is_last)
     def _():
@@ -141,7 +145,7 @@
 
     @pl.when(jnp.logical_not(jnp.logical_or(is_first, is_last)))
     def _():
-        out[:, 32:64, :] = jnp.zeros((chunks, R, LANES), BF16)
+        out[:, PER:CROSS, :] = jnp.zeros((chunks, PER, LANES), BF16)
 
     get_c_u.wait()
     get_ids_d.wait()
@@ -158,9 +162,9 @@
     wx = jnp.concatenate([zero, a_u, zero, gated(b_u, is_first)], axis=0)
     wc = jnp.concatenate([zero, zero, zero, gated(b_u, jnp.logical_not(is_first))], axis=0)
     main = nt(x_u[...], wx) + nt(c_u[...], wc)
-    main = main.reshape(chunks, R, LANES) + partial[:, 0:R, :].astype(F32)
-    out[:, 0:R, :] = main.astype(BF16)
-    out[:, R:ROWS, :] = partial[:, R:ROWS, :]
+    main = main.reshape(chunks, PER, LANES) + partial[:, 0:PER, :].astype(F32)
+    out[:, 0:PER, :] = main.astype(BF16)
+    out[:, PER:ROWS, :] = partial[:, PER:ROWS, :]
 
     @pl.when(jnp.logical_or(is_first, is_last))
     def _():
@@ -171,27 +175,43 @@
         own = nt(b_e, b_e)
         folded = jnp.concatenate([own[8 * r : 8 * r + 8] for r in range(4)], axis=1)
         tail = jnp.concatenate([folded, jnp.zeros((8, LANES), F32)], axis=0)
-        out[:, 64:96, :] = jnp.broadcast_to(cross.astype(BF16)[None], (chunks, R, LANES))
-        held = partial[:, 96:ROWS, :].astype(F32) + tail[None]
-        out[:, 96:ROWS, :] = held.astype(BF16)
+        out[:, CROSS:EXTRA, :] = jnp.broadcast_to(cross.astype(BF16)[None], (chunks, R, LANES))
+        held = partial[:, EXTRA:ROWS, :].astype(F32) + tail[None]
+        out[:, EXTRA:ROWS, :] = held.astype(BF16)
+
+
+def gathered_sum(received, out):
+    total = jnp.sum(received[...].astype(F32), axis=0)
+    folded = total[EXTRA : EXTRA + 8]
+    rows = [folded]
+    for side in range(2):
+        first = EXTRA + 8 + 2 * side
+        row = total[first : first + 1] + total[first + 1 : first + 2]
+        high = row.astype(BF16).astype(F32)
+        rows += [high, row - high]
+    rows += [jnp.zeros((4, LANES), F32)]
+    out[0:EXTRA] = total[0:EXTRA].astype(BF16)
+    out[EXTRA:ROWS] = jnp.concatenate(rows, axis=0).astype(BF16)
 
 
 def middle(meta, received, down_ids, up_ids, out):
-    place = meta[0]
+    chunks = out.shape[0]
+    place = lax.rem(meta[0], chunks)
     is_first = meta[1] == 0
     is_last = meta[1] == meta[2] - 1
     is_end = jnp.logical_or(is_first, is_last)
-    chunks = received.shape[0]
     inverse = 1.0 / meta[3].astype(F32)
     heads = LANES // R
     offsets = [meta[4 + k] for k in range(heads)]
     loss_weights = [meta[4 + heads + k] for k in range(heads)]
-    total = jnp.sum(received[...].astype(F32), axis=0)
-    main, base_logits, cross = total[0:32], total[32:64], total[64:96]
-    folded, square_rows = total[96:104], total[104:108]
-    lane = lax.broadcasted_iota(jnp.int32, (R, LANES), 1)
-    token = lax.broadcasted_iota(jnp.int32, (R, LANES), 0)
-    base = R * lax.rem(place, LANES // R)
+    total = received[0].astype(F32) + received[1].astype(F32)
+    main, base_logits, cross = total[0:PER], total[PER:CROSS], total[CROSS:EXTRA]
+    folded, square_rows = total[EXTRA : EXTRA + 8], total[EXTRA + 8 : EXTRA + 12]
+    lane = lax.broadcasted_iota(jnp.int32, (PER, LANES), 1)
+    token = lax.broadcasted_iota(jnp.int32, (PER, LANES), 0)
+    spot = lax.rem(token, M)
+    sequences = chunks * (PER // M)
+    base = PER * lax.rem(place, LANES // PER)
 
     def column(row):
         return jnp.sum(jnp.where(lane == base + token, row, 0.0), axis=1, keepdims=True)
@@ -219,7 +239,7 @@
     scale_e = lax.rsqrt(jnp.maximum(square_e, 0.0) * inverse + EPS)
     raw = base_logits + nn(act_e, cross, HIGH)
     logits = raw * scale_e
-    block = lax.div(place, LANES // R)
+    block = lax.div(place, LANES // PER)
     ids_d = down_ids[pl.ds(block, 1), :]
     ids_u = up_ids[pl.ds(block, 1), :]
     ids = jnp.where(is_first, ids_u, ids_d).astype(F32)
@@ -228,21 +248,21 @@
     weight_sum = jnp.float32(0.0)
     for k in range(heads):
         weight_sum = weight_sum + loss_weights[k].astype(F32)
-    top = jnp.zeros((R, LANES), F32)
-    target = jnp.zeros((R, LANES), F32)
-    weight = jnp.zeros((R, LANES), F32)
+    top = jnp.zeros((PER, LANES), F32)
+    target = jnp.zeros((PER, LANES), F32)
+    weight = jnp.zeros((PER, LANES), F32)
     for k in range(heads):
         mine = group == k
         shift = offsets[k]
         largest = jnp.max(jnp.where(mine, logits, -jnp.inf), axis=1, keepdims=True)
         wanted = jnp.sum(jnp.where(lane == base + token + shift, ids, 0.0), axis=1, keepdims=True)
-        factor = loss_weights[k].astype(F32) / weight_sum / ((R - shift) * chunks).astype(F32)
-        valid = jnp.where(token + shift < R, factor, 0.0)
+        factor = loss_weights[k].astype(F32) / weight_sum / ((M - shift) * sequences).astype(F32)
+        valid = jnp.where(spot + shift < M, factor, 0.0)
         top = jnp.where(mine, largest, top)
         target = jnp.where(mine, wanted, target)
         weight = jnp.where(mine, valid, weight)
     power = jnp.exp(logits - top)
-    below = jnp.ones((R, LANES), F32)
+    below = jnp.ones((PER, LANES), F32)
     for k in range(heads):
         mine = group == k
         below = jnp.where(mine, jnp.sum(jnp.where(mine, power, 0.0), axis=1, keepdims=True), below)
@@ -285,16 +305,16 @@
 
 def tokens_of(received, first):
     chunks = received.shape[0]
-    return received[:, first : first + R, :].reshape(chunks * R, LANES)
+    return received[:, first : first + PER, :].reshape(chunks * PER, LANES)
 
 
 def coefficient(received, row):
     chunks = received.shape[0]
-    lane = lax.broadcasted_iota(jnp.int32, (R, LANES), 1)
-    token = lax.broadcasted_iota(jnp.int32, (R, LANES), 0)
+    lane = lax.broadcasted_iota(jnp.int32, (PER, LANES), 1)
+    token = lax.broadcasted_iota(jnp.int32, (PER, LANES), 0)
     cols = []
     for j in range(chunks):
-        rows = received[j, 64:BACK_ROWS, :].astype(F32)
+        rows = received[j, CROSS:BACK_ROWS, :].astype(F32)
         both = rows[row : row + 1] + rows[row + 1 : row + 2]
         cols.append(jnp.sum(jnp.where(lane == token, both, 0.0), axis=1, keepdims=True))
     return jnp.concatenate(cols, axis=0)
@@ -305,37 +325,47 @@
     return jnp.concatenate([weights if k == group else zero for k in range(LANES // R)], axis=0)
 
 
-def backward(meta, received, x_d, x_u, c_d, c_u, w_d, w_u, gain, cand, ahead, behind, g_d, g_u, loss, cot):
+def cotangent(received, side, x, c, w, gain, cand, end, cot):
+    cot[...] = c[...].astype(F32)
+
+    @pl.when(end)
+    def _():
+        high, low = halves(columns_of(gain, cand))
+        grad = tokens_of(received, PER)
+        final = x[...].astype(F32) + nn(tokens_of(received, 0), at_rows(w[R : 2 * R], side))
+        cot[...] = nn(grad, high) + nn(grad, low) - coefficient(received, 4) * final
+
+
+def weight_grads(meta, received, x_d, x_u, c_d, c_u, w_d, w_u, gain, cand, g_d, g_u, cot):
     is_first = meta[1] == 0
     is_last = meta[1] == meta[2] - 1
     act = tokens_of(received, 0)
-    work = (
-        (1, x_u, c_u, w_u, behind.at[0], ahead.at[1], g_u, is_first),
-        (0, x_d, c_d, w_d, ahead.at[0], behind.at[1], g_d, is_last),
-    )
-    for side, x, c, w, y, dx, g, end in work:
-        final = x[...].astype(F32) + nn(act, at_rows(w[R : 2 * R], side))
-        y[...] = final.astype(BF16)
-        cot[...] = c[...].astype(F32)
-
-        @pl.when(end)
-        def _():
-            high, low = halves(columns_of(gain, cand))
-            grad = tokens_of(received, 32)
-            again = x[...].astype(F32) + nn(act, at_rows(w[R : 2 * R], side))
-            cot[...] = nn(grad, high) + nn(grad, low) - coefficient(received, 4) * again
-
-        held = cot[...]
-        wide = x[...].astype(F32)
-        back = held + nn(act, at_rows(w[0:R], 2 + side)) - coefficient(received, 2 * side) * wide
-        dx[...] = back.astype(BF16)
-        by_cot = tn(act, held.astype(BF16))
+    work = ((1, x_u, c_u, w_u, g_u, is_first), (0, x_d, c_d, w_d, g_d, is_last))
+    for side, x, c, w, g, end in work:
+        cotangent(received, side, x, c, w, gain, cand, end, cot)
+        by_cot = tn(act, cot[...].astype(BF16))
         by_x = tn(act, x[...])
         grads = jnp.concatenate(
             [by_x[64 + R * side : 64 + R * side + R], by_cot[R * side : R * side + R]], axis=0
         )
         g[...] = grads.astype(g.dtype)
-    rows = jnp.sum(received[:, 64:BACK_ROWS, :].astype(F32), axis=0)
+
+
+def token_grads(meta, received, x_d, x_u, c_d, c_u, w_d, w_u, gain, cand, ahead, behind, loss, cot):
+    is_first = meta[1] == 0
+    is_last = meta[1] == meta[2] - 1
+    act = tokens_of(received, 0)
+    work = (
+        (1, x_u, c_u, w_u, behind.at[0], ahead.at[1], is_first),
+        (0, x_d, c_d, w_d, ahead.at[0], behind.at[1], is_last),
+    )
+    for side, x, c, w, y, dx, end in work:
+        wide = x[...].astype(F32)
+        y[...] = (wide + nn(act, at_rows(w[R : 2 * R], side))).astype(BF16)
+        cotangent(received, side, x, c, w, gain, cand, end, cot)
+        back = cot[...] + nn(act, at_rows(w[0:R], 2 + side)) - coefficient(received, 2 * side) * wide
+        dx[...] = back.astype(BF16)
+    rows = jnp.sum(received[:, CROSS:BACK_ROWS, :].astype(F32), axis=0)
     total = rows[6:7] + rows[7:8] + rows[8:9]
     loss[...] = jnp.broadcast_to(total, loss.shape)
 
@@ -404,7 +434,10 @@
     ids = down_ids.reshape(id_rows), up_ids.reshape(id_rows)
     fetched = (down_in[0], up_in[0], down_cot[0], up_cot[0], head_gain, cand, *ids)
 
-    send = shape((groups, ROWS, LANES), BF16)
+    near = tokens // PER
+    rings = [list(range(first, first + near)) for first in range(0, groups, near)]
+    partners = [list(members) for members in zip(*rings)]
+    send = shape((near, ROWS, LANES), BF16)
     partial, x_d, x_u, c_d, c_u, gain_part, cand_part, ids_d, ids_u = pl.pallas_call(
         first_partial,
         out_shape=(
@@ -430,34 +463,45 @@
         out_specs=vmem,
         compiler_params=params,
     )(meta, partial, x_u, c_u, w_u, w_d, gain_part, cand_part)
-    received = lax.all_to_all(partial, "dp", 0, 0)
+    received = lax.all_to_all(partial, "dp", 0, 0, axis_index_groups=rings)
+    summed = pl.pallas_call(
+        gathered_sum,
+        out_shape=shape((ROWS, LANES), BF16),
+        in_specs=[vmem],
+        out_specs=vmem,
+        compiler_params=params,
+    )(received)
+    received = lax.all_gather(summed, "dp", axis_index_groups=partners)
 
     back = pl.pallas_call(
         middle,
-        out_shape=shape((groups, BACK_ROWS, LANES), BF16),
+        out_shape=shape((near, BACK_ROWS, LANES), BF16),
         in_specs=[smem] + [vmem] * 3,
         out_specs=vmem,
         compiler_params=params,
     )(meta, received, ids_d, ids_u)
-    gathered = lax.all_to_all(back, "dp", 0, 0)
-
-    ahead, behind, g_d, g_u, loss_rows = pl.pallas_call(
-        backward,
-        out_shape=(
-            both,
-            both,
-            shape((2 * R, local_width), F32),
-            shape((2 * R, local_width), BF16),
-            shape((sections, LANES), F32),
-        ),
+    gathered = lax.all_to_all(back, "dp", 0, 0, axis_index_groups=rings)
+
+    held = (meta, gathered, x_d, x_u, c_d, c_u, w_d, w_u, gain_part, cand_part)
+    g_d, g_u = pl.pallas_call(
+        weight_grads,
+        out_shape=(shape((2 * R, local_width), F32), shape((2 * R, local_width), BF16)),
         in_specs=[smem] + [vmem] * 9,
-        out_specs=(vmem,) * 5,
+        out_specs=(vmem,) * 2,
         scratch_shapes=[pltpu.VMEM((tokens, local_width), F32)],
         compiler_params=params,
-    )(meta, gathered, x_d, x_u, c_d, c_u, w_d, w_u, gain_part, cand_part)
+    )(*held)
+    mate = lax.ppermute(g_u, "section", mirror)
+    ahead, behind, loss_rows = pl.pallas_call(
+        token_grads,
+        out_shape=(both, both, shape((sections, LANES), F32)),
+        in_specs=[smem] + [vmem] * 9,
+        out_specs=(vmem,) * 3,
+        scratch_shapes=[pltpu.VMEM((tokens, local_width), F32)],
+        compiler_params=params,
+    )(*held)
     ahead = lax.ppermute(ahead, "section", further)
     behind = lax.ppermute(behind, "section", nearer)
-    mate = lax.ppermute(g_u, "section", mirror)
     losses = lax.all_to_all(loss_rows, "section", 0, 0, tiled=True)
     down_next, up_next, down_back, up_back, grad_a, grad_b, loss = pl.pallas_call(
         finish,

time: 98.5 us -> 92.4 us (0.938)
  blocking collectives: 63.3 us -> 53.6 us
  starting transfers between devices: 22.2 us -> 24.7 us
    all_to_all x2, blocking collectives: 48.3 us -> 35.1 us  [the longest x1 23 us: shards(): received = lax.all_to_all(partial, 'dp', 0, 0, axis_index_groups=rings)]
    all_gather x0 -> x1, blocking collectives: none -> 7.48 us  [shards(): received = lax.all_gather(summed, 'dp', axis_index_groups=partners)]
    all_to_all x1, blocking collectives: 14.9 us -> 11 us  [shards(): losses = lax.all_to_all(loss_rows, 'section', 0, 0, tiled=True)]
    ppermute x1, starting transfers between devices: 4.92 us -> 7.72 us  [shards(): ahead = lax.ppermute(ahead, 'section', further)]
    pallas_call x2 -> x4, Pallas kernels: 3.93 us -> 4.87 us  [the longest x1 1.8 us: shards(): pl.pallas_call(middle, out_shape=shape((near, BACK_ROWS, LANES), BF16), i...]
  transfers between devices with their start and end apart: 4 -> 4, of which waited for: 0 -> 0; matrix products, arithmetic and copies ran while one was open for 0% -> 0% of each run, Pallas kernels for 4% -> 5%
where the time goes in v3:
time: 92.4 us; the launch traced here: 92 us
  blocking collectives  53.6 us (58%)
  starting transfers between devices  24.7 us (27%)
  Pallas kernels  12.1 us (13%)
    all_to_all x1, blocking collectives, shards(): received = lax.all_to_all(partial, 'dp', 0, 0, axis_index_groups=rings)  23 us
    all_to_all x1, blocking collectives, shards(): gathered = lax.all_to_all(back, 'dp', 0, 0, axis_index_groups=rings)  12.1 us
    all_to_all x1, blocking collectives, shards(): losses = lax.all_to_all(loss_rows, 'section', 0, 0, tiled=True)  11 us
    ppermute x1, starting transfers between devices, shards(): w_u = lax.ppermute(w_d, 'section', mirror)  8.81 us
    ppermute x1, starting transfers between devices, shards(): ahead = lax.ppermute(ahead, 'section', further)  7.72 us
    all_gather x1, blocking collectives, shards(): received = lax.all_gather(summed, 'dp', axis_index_groups=partners)  7.48 us
    ppermute x1, starting transfers between devices, shards(): mate = lax.ppermute(g_u, 'section', mirror)  6.3 us
    pallas_call x1, Pallas kernels, shards(): pl.pallas_call(first_partial, out_shape=(send, wide, wide, wide, wide, sh...  3.46 us
  transfers between devices with their start and end apart: 4, of which 0 were waited for; matrix products, arithmetic and copies ran while one was open for 0% of the time, Pallas kernels for 5%

profile of v3, /device:TPU:1, one launch (start us, length us, event | category | flops | bytes accessed | tf_op | source)
XLA Modules:
  0.0 92.0 jit_solution(6088477104812245050)
XLA Ops:
  0.6 0.8 shard_map.171.w_d
  1.4 8.8 %collective-permute-start = (bf16[64,512]{1,0:T(8,128)(2,1)S(1)}, bf16[64,512]{1,0:T(8,128)(2,1)S(1)}, u32[]{:S(2)}, u32[]{:S(2)}) collective-permute-start(bf16[64,512]{1,0:T(8,128)(2,1)S(1)} %shard_map.171.w_d), channel_id=1, source_target_pairs={{0,496},{16,480},{32,464},{48,448},{64,432},{80,416},{96,400},{112... | collective-permute-start | bytes 196616 | tf_op jit(solution)/shard_map/ppermute | solution.py:429
  10.3 0.0 copy-start
  10.3 0.0 copy-start.1
  10.3 0.6 copy-done
  10.9 0.0 copy-done.1
  10.9 0.1 concatenate.3.meta
  11.0 3.5 %shard_map.172 = (bf16[8,176,128]{2,1,0:T(8,128)(2,1)S(1)}, bf16[512,512]{1,0:T(8,128)(2,1)S(1)}, bf16[512,512]{1,0:T(8,128)(2,1)S(1)}, bf16[512,512]{1,0:T(8,12...) custom-call(s32[12]{0:T(128)S(1)} %concatenate.3.meta, ...), custom_call_target="tpu_custom_call" | custom-call | tf_op jit(solution)/shard_map/pallas_call | solution.py:441
  14.5 0.0 collective-permute-done.w_u
  14.5 1.0 %shard_map.173 = bf16[8,176,128]{2,1,0:T(8,128)(2,1)S(1)} custom-call(s32[12]{0:T(128)S(1)} %concatenate.3.meta, bf16[8,176,128]{2,1,0:T(8,128)(2,1)S(1)} %get-tuple-element.28.partial, bf16[512,512]{1,0:T(8,128)(2,1)S(1)} %get-tuple-element.29.x_u, bf16[512,512]{1,0:T(8,128)(2,1)S(1)} %get-tuple-element.30.c_u, ...), custom_call_target="tpu_custom_call" | custom-call | tf_op jit(solution)/shard_map/pallas_call | solution.py:459
  15.5 23.0 %all_to_all.21.received = bf16[8,176,128]{2,1,0:T(8,128)(2,1)S(1)} all-to-all(bf16[8,176,128]{2,1,0:T(8,128)(2,1)S(1)} %shard_map.173), channel_id=1, replica_groups={{0,1,2,3,4,5,6,7},{8,9,10,11,12,13,14,15},{16,17,18,19,20,21,22,23},{24..., dimensions={0} | all-to-all | bytes 720896 | tf_op jit(solution)/shard_map/all_to_all | solution.py:466
  38.5 0.1 shard_map.174
  38.6 7.5 %all-gather = bf16[352,128]{1,0:T(8,128)(2,1)S(1)} all-gather(bf16[176,128]{1,0:T(8,128)(2,1)S(1)} %shard_map.174), channel_id=2, replica_groups={{0,8},{1,9},{2,10},{3,11},{4,12},{5,13},{6,14},{7,15},{16,24},{17,25},{..., dimensions={0}, use_global_device_ids=true | all-gather | bytes 135168 | tf_op jit(solution)/shard_map/all_gather | solution.py:474
  46.0 1.8 %shard_map.175 = bf16[8,144,128]{2,1,0:T(8,128)(2,1)S(1)} custom-call(s32[12]{0:T(128)S(1)} %concatenate.3.meta, bf16[2,176,128]{2,1,0:T(8,128)(2,1)S(1)} %bitcast.25, s32[4,128]{1,0:T(4,128)S(1)} %get-tuple-element.33.down_ids, s32[4,128]{1,0:T(4,128)S(1)} %get-tuple-element.34.up_ids), custom_call_target="tpu_custom_call" | custom-call | tf_op jit(solution)/shard_map/pallas_call | solution.py:476
  47.8 12.1 %all_to_all.22.received = bf16[8,144,128]{2,1,0:T(8,128)(2,1)S(1)} all-to-all(bf16[8,144,128]{2,1,0:T(8,128)(2,1)S(1)} %shard_map.175), channel_id=1, replica_groups={{0,1,2,3,4,5,6,7},{8,9,10,11,12,13,14,15},{16,17,18,19,20,21,22,23},{24..., dimensions={0} | all-to-all | bytes 589824 | tf_op jit(solution)/shard_map/all_to_all | solution.py:483
  59.9 1.7 %shard_map.176 = (bf16[2,512,512]{2,1,0:T(8,128)(2,1)S(1)}, bf16[2,512,512]{2,1,0:T(8,128)(2,1)S(1)}, f32[32,128]{1,0:T(8,128)S(1)}) custom-call(s32[12]{0:T(128)S(1)} %concatenate.3.meta, bf16[8,144,128]{2,1,0:T(8,128)(2,1)S(1)} %all_to_all.22.received, bf16[512,512]{1,0:T(8,128)(2,1)S(1)} %get-tuple-element.35.x_d, ...), custom_call_target="tpu_custom_call" | custom-call | tf_op jit(solution)/shard_map/pallas_call | solution.py:495
  61.6 7.7 %collective-permute-start.1 = (bf16[2,512,512]{2,1,0:T(8,128)(2,1)S(1)}, bf16[2,512,512]{2,1,0:T(8,128)(2,1)S(1)}, u32[]{:S(2)}, u32[]{:S(2)}) collective-permute-start(bf16[2,512,512]{2,1,0:T(8,128)(2,1)S(1)} %get-tuple-element.37), channel_id=1, source_target_pairs={{0,16},{16,32},{32,48},{48,64},{64,80},{80,96},{96,112},{112,128},... | collective-permute-start | bytes 3145736 | tf_op jit(solution)/shard_map/ppermute | solution.py:503
  69.3 1.9 %collective-permute-start.2 = (bf16[2,512,512]{2,1,0:T(8,128)(2,1)S(1)}, bf16[2,512,512]{2,1,0:T(8,128)(2,1)S(1)}, u32[]{:S(2)}, u32[]{:S(2)}) collective-permute-start(bf16[2,512,512]{2,1,0:T(8,128)(2,1)S(1)} %get-tuple-element.38), channel_id=1, source_target_pairs={{16,0},{32,16},{48,32},{64,48},{80,64},{96,80},{112,96},{128,112},... | collective-permute-start | bytes 3145736 | tf_op jit(solution)/shard_map/ppermute | solution.py:504
  71.3 1.3 %shard_map.177 = (f32[64,512]{1,0:T(8,128)S(1)}, bf16[64,512]{1,0:T(8,128)(2,1)S(1)}) custom-call(s32[12]{0:T(128)S(1)} %concatenate.3.meta, bf16[8,144,128]{2,1,0:T(8,128)(2,1)S(1)} %all_to_all.22.received, bf16[512,512]{1,0:T(8,128)(2,1)S(1)} %get-tuple-element.35.x_d, bf16[512,512]{1,0:T(8,128)(2,1)S(1)} %get-tuple-element.29.x_u, ...), custom_call_target="tpu_custom_call" | custom-call | tf_op jit(solution)/shard_map/pallas_call | solution.py:486
  72.6 6.3 %collective-permute-start.3 = (bf16[64,512]{1,0:T(8,128)(2,1)S(1)}, bf16[64,512]{1,0:T(8,128)(2,1)S(1)}, u32[]{:S(2)}, u32[]{:S(2)}) collective-permute-start(bf16[64,512]{1,0:T(8,128)(2,1)S(1)} %get-tuple-element.40), channel_id=1, source_target_pairs={{0,496},{16,480},{32,464},{48,448},{64,432},{80,416},{96,400},{112... | collective-permute-start | bytes 196616 | tf_op jit(solution)/shard_map/ppermute | solution.py:494
  78.9 11.0 %all_to_all.23 = f32[32,1,128]{2,1,0:T(1,128)S(1)} all-to-all(f32[32,1,128]{2,1,0:T(1,128)S(1)} %bitcast.27), channel_id=1, replica_groups=mesh['section'=32,'dp'=16] {'section'}, dimensions={0} | all-to-all | bytes 32768 | tf_op jit(solution)/shard_map/all_to_all | solution.py:505
  89.9 0.0 collective-permute-done.3.mate
  89.9 0.0 collective-permute-done.1.ahead
  89.9 0.0 collective-permute-done.2.behind
  89.9 2.0 %shard_map.178 = (bf16[512,512]{1,0:T(8,128)(2,1)}, bf16[512,512]{1,0:T(8,128)(2,1)}, bf16[512,512]{1,0:T(8,128)(2,1)}, bf16[512,512]{1,0:T(8,128)(2,1)}, f32[32...) custom-call(bf16[2,512,512]{2,1,0:T(8,128)(2,1)S(1)} %collective-permute-done.1.ahead, ...), custom_call_target="tpu_custom_call" | custom-call | tf_op jit(solution)/shard_map/pallas_call | solution.py:506
Async XLA Ops:
  1.4 13.1 %collective-permute-start = (bf16[64,512]{1,0:T(8,128)(2,1)S(1)}, bf16[64,512]{1,0:T(8,128)(2,1)S(1)}, u32[]{:S(2)}, u32[]{:S(2)}) collective-permute-start(bf16[64,512]{1,0:T(8,128)(2,1)S(1)} %shard_map.171.w_d), channel_id=1, source_target_pairs={{0,496},{16,480},{32,464},{48,448},{64,432},{80,416},{96,400},{112... | collective-permute-start | bytes 196616 | tf_op jit(solution)/shard_map/ppermute | solution.py:429
  10.3 0.7 copy-start
  10.3 0.7 copy-start.1
  61.6 28.3 %collective-permute-start.1 = (bf16[2,512,512]{2,1,0:T(8,128)(2,1)S(1)}, bf16[2,512,512]{2,1,0:T(8,128)(2,1)S(1)}, u32[]{:S(2)}, u32[]{:S(2)}) collective-permute-start(bf16[2,512,512]{2,1,0:T(8,128)(2,1)S(1)} %get-tuple-element.37), channel_id=1, source_target_pairs={{0,16},{16,32},{32,48},{48,64},{64,80},{80,96},{96,112},{112,128},... | collective-permute-start | bytes 3145736 | tf_op jit(solution)/shard_map/ppermute | solution.py:503
  69.3 20.6 %collective-permute-start.2 = (bf16[2,512,512]{2,1,0:T(8,128)(2,1)S(1)}, bf16[2,512,512]{2,1,0:T(8,128)(2,1)S(1)}, u32[]{:S(2)}, u32[]{:S(2)}) collective-permute-start(bf16[2,512,512]{2,1,0:T(8,128)(2,1)S(1)} %get-tuple-element.38), channel_id=1, source_target_pairs={{16,0},{32,16},{48,32},{64,48},{80,64},{96,80},{112,96},{128,112},... | collective-permute-start | bytes 3145736 | tf_op jit(solution)/shard_map/ppermute | solution.py:504
  72.6 17.3 %collective-permute-start.3 = (bf16[64,512]{1,0:T(8,128)(2,1)S(1)}, bf16[64,512]{1,0:T(8,128)(2,1)S(1)}, u32[]{:S(2)}, u32[]{:S(2)}) collective-permute-start(bf16[64,512]{1,0:T(8,128)(2,1)S(1)} %get-tuple-element.40), channel_id=1, source_target_pairs={{0,496},{16,480},{32,464},{48,448},{64,432},{80,416},{96,400},{112... | collective-permute-start | bytes 196616 | tf_op jit(solution)/shard_map/ppermute | solution.py:494

commit v4 on v3

--- a/solution.py
+++ b/solution.py
@@ -351,40 +351,65 @@
         g[...] = grads.astype(g.dtype)
 
 
-def token_grads(meta, received, x_d, x_u, c_d, c_u, w_d, w_u, gain, cand, ahead, behind, loss, cot):
+def token_grads(meta, received, x_d, x_u, c_d, c_u, w_d, w_u, gain, cand, outer, inner, loss, cot):
     is_first = meta[1] == 0
     is_last = meta[1] == meta[2] - 1
-    act = tokens_of(received, 0)
-    work = (
-        (1, x_u, c_u, w_u, behind.at[0], ahead.at[1], is_first),
-        (0, x_d, c_d, w_d, ahead.at[0], behind.at[1], is_last),
-    )
-    for side, x, c, w, y, dx, end in work:
-        wide = x[...].astype(F32)
-        y[...] = (wide + nn(act, at_rows(w[R : 2 * R], side))).astype(BF16)
-        cotangent(received, side, x, c, w, gain, cand, end, cot)
-        back = cot[...] + nn(act, at_rows(w[0:R], 2 + side)) - coefficient(received, 2 * side) * wide
-        dx[...] = back.astype(BF16)
+    is_even = lax.rem(meta[1], 2) == 0
+
+    def fill(ahead, behind):
+        act = tokens_of(received, 0)
+        work = (
+            (1, x_u, c_u, w_u, behind.at[0], ahead.at[1], is_first),
+            (0, x_d, c_d, w_d, ahead.at[0], behind.at[1], is_last),
+        )
+        for side, x, c, w, y, dx, end in work:
+            wide = x[...].astype(F32)
+            y[...] = (wide + nn(act, at_rows(w[R : 2 * R], side))).astype(BF16)
+            cotangent(received, side, x, c, w, gain, cand, end, cot)
+            back = cot[...] + nn(act, at_rows(w[0:R], 2 + side)) - coefficient(received, 2 * side) * wide
+            dx[...] = back.astype(BF16)
+
+    @pl.when(is_even)
+    def _():
+        fill(inner, outer)
+
+    @pl.when(jnp.logical_not(is_even))
+    def _():
+        fill(outer, inner)
+
     rows = jnp.sum(received[:, CROSS:BACK_ROWS, :].astype(F32), axis=0)
     total = rows[6:7] + rows[7:8] + rows[8:9]
     loss[...] = jnp.broadcast_to(total, loss.shape)
 
 
-def finish(ahead, behind, g_d, mate, losses, down_next, up_next, down_back, up_back, grad_a, grad_b, loss, sems):
-    copies = [
-        pltpu.make_async_copy(ahead.at[0], down_next, sems.at[0]),
-        pltpu.make_async_copy(behind.at[0], up_next, sems.at[1]),
-        pltpu.make_async_copy(behind.at[1], down_back, sems.at[2]),
-        pltpu.make_async_copy(ahead.at[1], up_back, sems.at[3]),
-    ]
-    for copy in copies:
-        copy.start()
+def finish(
+    meta, outer, inner, g_d, mate, losses, down_next, up_next, down_back, up_back, grad_a, grad_b, loss, sems
+):
+    is_even = lax.rem(meta[1], 2) == 0
     total = g_d[...] + mate[...].astype(F32)
     grad_a[...] = total[0:R]
     grad_b[...] = total[R : 2 * R]
     loss[0] = jnp.sum(losses[:, 0:1])
-    for copy in copies:
-        copy.wait()
+
+    def write(ahead, behind):
+        copies = [
+            pltpu.make_async_copy(ahead.at[0], down_next, sems.at[0]),
+            pltpu.make_async_copy(behind.at[0], up_next, sems.at[1]),
+            pltpu.make_async_copy(behind.at[1], down_back, sems.at[2]),
+            pltpu.make_async_copy(ahead.at[1], up_back, sems.at[3]),
+        ]
+        for copy in copies:
+            copy.start()
+        for copy in copies:
+            copy.wait()
+
+    @pl.when(is_even)
+    def _():
+        write(outer, inner)
+
+    @pl.when(jnp.logical_not(is_even))
+    def _():
+        write(inner, outer)
 
 
 def shards(
@@ -408,8 +433,8 @@
     tokens, local_width = down_in.shape[1:]
     heads, candidates = head_gain.shape[0], cand.shape[0]
     mirror = [(i, sections - 1 - i) for i in range(sections)]
-    further = [(i, i + 1) for i in range(sections - 1)]
-    nearer = [(i + 1, i) for i in range(sections - 1)]
+    inside = [(i, i ^ 1) for i in range(sections)]
+    between = [(i, i + 1 if i % 2 else i - 1) for i in range(1, sections - 1)]
     smem = pl.BlockSpec(memory_space=pltpu.SMEM)
     vmem = pl.BlockSpec(memory_space=pltpu.VMEM)
     hbm = pl.BlockSpec(memory_space=pltpu.HBM)
@@ -492,7 +517,7 @@
         compiler_params=params,
     )(*held)
     mate = lax.ppermute(g_u, "section", mirror)
-    ahead, behind, loss_rows = pl.pallas_call(
+    outer, inner, loss_rows = pl.pallas_call(
         token_grads,
         out_shape=(both, both, shape((sections, LANES), F32)),
         in_specs=[smem] + [vmem] * 9,
@@ -500,8 +525,8 @@
         scratch_shapes=[pltpu.VMEM((tokens, local_width), F32)],
         compiler_params=params,
     )(*held)
-    ahead = lax.ppermute(ahead, "section", further)
-    behind = lax.ppermute(behind, "section", nearer)
+    outer = lax.ppermute(outer, "section", between)
+    inner = lax.ppermute(inner, "section", inside)
     losses = lax.all_to_all(loss_rows, "section", 0, 0, tiled=True)
     down_next, up_next, down_back, up_back, grad_a, grad_b, loss = pl.pallas_call(
         finish,
@@ -514,11 +539,11 @@
             shape((R, local_width), F32),
             shape((1,), F32),
         ),
-        in_specs=[vmem] * 5,
+        in_specs=[smem] + [vmem] * 5,
         out_specs=(hbm,) * 4 + (vmem, vmem, smem),
         scratch_shapes=[pltpu.SemaphoreType.DMA((4,))],
         compiler_params=params,
-    )(ahead, behind, g_d, mate, losses)
+    )(meta, outer, inner, g_d, mate, losses)
     return (
         down_next[None],
         up_next[None],

time: 92.4 us -> 92.9 us (level)
  starting transfers between devices: 24.7 us -> 23 us
  blocking collectives: 53.6 us -> 55.2 us
    ppermute x1, starting transfers between devices: 6.3 us -> 4.56 us  [shards(): mate = lax.ppermute(g_u, 'section', mirror)]
    all_to_all x1, blocking collectives: 11 us -> 12.6 us  [shards(): losses = lax.all_to_all(loss_rows, 'section', 0, 0, tiled=True)]
where the time goes in v4:
time: 92.9 us; the launch traced here: 92.5 us
  blocking collectives  55.2 us (59%)
  starting transfers between devices  23 us (25%)
  Pallas kernels  12.8 us (14%)
    all_to_all x1, blocking collectives, shards(): received = lax.all_to_all(partial, 'dp', 0, 0, axis_index_groups=rings)  23 us
    all_to_all x1, blocking collectives, shards(): losses = lax.all_to_all(loss_rows, 'section', 0, 0, tiled=True)  12.6 us
    all_to_all x1, blocking collectives, shards(): gathered = lax.all_to_all(back, 'dp', 0, 0, axis_index_groups=rings)  12.1 us
    ppermute x1, starting transfers between devices, shards(): w_u = lax.ppermute(w_d, 'section', mirror)  8.81 us
    ppermute x1, starting transfers between devices, shards(): outer = lax.ppermute(outer, 'section', between)  7.72 us
    all_gather x1, blocking collectives, shards(): received = lax.all_gather(summed, 'dp', axis_index_groups=partners)  7.48 us
    ppermute x1, starting transfers between devices, shards(): mate = lax.ppermute(g_u, 'section', mirror)  4.56 us
    pallas_call x1, Pallas kernels, shards(): pl.pallas_call(first_partial, out_shape=(send, wide, wide, wide, wide, sh...  3.46 us
  transfers between devices with their start and end apart: 4, of which 0 were waited for; matrix products, arithmetic and copies ran while one was open for 0% of the time, Pallas kernels for 5%

profile of v4, /device:TPU:1, one launch (start us, length us, event | category | flops | bytes accessed | tf_op | source)
XLA Modules:
  0.0 92.5 jit_solution(6261555579467824145)
XLA Ops:
  0.6 0.8 shard_map.171.w_d
  1.4 8.8 %collective-permute-start = (bf16[64,512]{1,0:T(8,128)(2,1)S(1)}, bf16[64,512]{1,0:T(8,128)(2,1)S(1)}, u32[]{:S(2)}, u32[]{:S(2)}) collective-permute-start(bf16[64,512]{1,0:T(8,128)(2,1)S(1)} %shard_map.171.w_d), channel_id=1, source_target_pairs={{0,496},{16,480},{32,464},{48,448},{64,432},{80,416},{96,400},{112... | collective-permute-start | bytes 196616 | tf_op jit(solution)/shard_map/ppermute | solution.py:454
  10.3 0.0 copy-start
  10.3 0.0 copy-start.1
  10.3 0.6 copy-done
  10.9 0.0 copy-done.1
  10.9 0.1 concatenate.3.meta
  11.0 3.5 %shard_map.172 = (bf16[8,176,128]{2,1,0:T(8,128)(2,1)S(1)}, bf16[512,512]{1,0:T(8,128)(2,1)S(1)}, bf16[512,512]{1,0:T(8,128)(2,1)S(1)}, bf16[512,512]{1,0:T(8,12...) custom-call(s32[12]{0:T(128)S(1)} %concatenate.3.meta, ...), custom_call_target="tpu_custom_call" | custom-call | tf_op jit(solution)/shard_map/pallas_call | solution.py:466
  14.5 0.0 collective-permute-done.w_u
  14.5 1.0 %shard_map.173 = bf16[8,176,128]{2,1,0:T(8,128)(2,1)S(1)} custom-call(s32[12]{0:T(128)S(1)} %concatenate.3.meta, bf16[8,176,128]{2,1,0:T(8,128)(2,1)S(1)} %get-tuple-element.28.partial, bf16[512,512]{1,0:T(8,128)(2,1)S(1)} %get-tuple-element.29.x_u, bf16[512,512]{1,0:T(8,128)(2,1)S(1)} %get-tuple-element.30.c_u, ...), custom_call_target="tpu_custom_call" | custom-call | tf_op jit(solution)/shard_map/pallas_call | solution.py:484
  15.5 23.0 %all_to_all.21.received = bf16[8,176,128]{2,1,0:T(8,128)(2,1)S(1)} all-to-all(bf16[8,176,128]{2,1,0:T(8,128)(2,1)S(1)} %shard_map.173), channel_id=1, replica_groups={{0,1,2,3,4,5,6,7},{8,9,10,11,12,13,14,15},{16,17,18,19,20,21,22,23},{24..., dimensions={0} | all-to-all | bytes 720896 | tf_op jit(solution)/shard_map/all_to_all | solution.py:491
  38.5 0.1 shard_map.174
  38.6 7.5 %all-gather = bf16[352,128]{1,0:T(8,128)(2,1)S(1)} all-gather(bf16[176,128]{1,0:T(8,128)(2,1)S(1)} %shard_map.174), channel_id=2, replica_groups={{0,8},{1,9},{2,10},{3,11},{4,12},{5,13},{6,14},{7,15},{16,24},{17,25},{..., dimensions={0}, use_global_device_ids=true | all-gather | bytes 135168 | tf_op jit(solution)/shard_map/all_gather | solution.py:499
  46.0 1.8 %shard_map.175 = bf16[8,144,128]{2,1,0:T(8,128)(2,1)S(1)} custom-call(s32[12]{0:T(128)S(1)} %concatenate.3.meta, bf16[2,176,128]{2,1,0:T(8,128)(2,1)S(1)} %bitcast.25, s32[4,128]{1,0:T(4,128)S(1)} %get-tuple-element.33.down_ids, s32[4,128]{1,0:T(4,128)S(1)} %get-tuple-element.34.up_ids), custom_call_target="tpu_custom_call" | custom-call | tf_op jit(solution)/shard_map/pallas_call | solution.py:501
  47.8 12.1 %all_to_all.22.received = bf16[8,144,128]{2,1,0:T(8,128)(2,1)S(1)} all-to-all(bf16[8,144,128]{2,1,0:T(8,128)(2,1)S(1)} %shard_map.175), channel_id=1, replica_groups={{0,1,2,3,4,5,6,7},{8,9,10,11,12,13,14,15},{16,17,18,19,20,21,22,23},{24..., dimensions={0} | all-to-all | bytes 589824 | tf_op jit(solution)/shard_map/all_to_all | solution.py:508
  59.9 1.7 %shard_map.176 = (bf16[2,512,512]{2,1,0:T(8,128)(2,1)S(1)}, bf16[2,512,512]{2,1,0:T(8,128)(2,1)S(1)}, f32[32,128]{1,0:T(8,128)S(1)}) custom-call(s32[12]{0:T(128)S(1)} %concatenate.3.meta, bf16[8,144,128]{2,1,0:T(8,128)(2,1)S(1)} %all_to_all.22.received, bf16[512,512]{1,0:T(8,128)(2,1)S(1)} %get-tuple-element.35.x_d, ...), custom_call_target="tpu_custom_call" | custom-call | tf_op jit(solution)/shard_map/pallas_call | solution.py:520
  61.6 7.7 %collective-permute-start.1 = (bf16[2,512,512]{2,1,0:T(8,128)(2,1)S(1)}, bf16[2,512,512]{2,1,0:T(8,128)(2,1)S(1)}, u32[]{:S(2)}, u32[]{:S(2)}) collective-permute-start(bf16[2,512,512]{2,1,0:T(8,128)(2,1)S(1)} %get-tuple-element.37), channel_id=1, source_target_pairs={{16,32},{32,16},{48,64},{64,48},{80,96},{96,80},{112,128},{128,112... | collective-permute-start | bytes 3145736 | tf_op jit(solution)/shard_map/ppermute | solution.py:528
  69.4 1.9 %collective-permute-start.2 = (bf16[2,512,512]{2,1,0:T(8,128)(2,1)S(1)}, bf16[2,512,512]{2,1,0:T(8,128)(2,1)S(1)}, u32[]{:S(2)}, u32[]{:S(2)}) collective-permute-start(bf16[2,512,512]{2,1,0:T(8,128)(2,1)S(1)} %get-tuple-element.38), channel_id=1, source_target_pairs={{0,16},{16,0},{32,48},{48,32},{64,80},{80,64},{96,112},{112,96},{1... | collective-permute-start | bytes 3145736 | tf_op jit(solution)/shard_map/ppermute | solution.py:529
  71.3 1.3 %shard_map.177 = (f32[64,512]{1,0:T(8,128)S(1)}, bf16[64,512]{1,0:T(8,128)(2,1)S(1)}) custom-call(s32[12]{0:T(128)S(1)} %concatenate.3.meta, bf16[8,144,128]{2,1,0:T(8,128)(2,1)S(1)} %all_to_all.22.received, bf16[512,512]{1,0:T(8,128)(2,1)S(1)} %get-tuple-element.35.x_d, bf16[512,512]{1,0:T(8,128)(2,1)S(1)} %get-tuple-element.29.x_u, ...), custom_call_target="tpu_custom_call" | custom-call | tf_op jit(solution)/shard_map/pallas_call | solution.py:511
  72.6 4.6 %collective-permute-start.3 = (bf16[64,512]{1,0:T(8,128)(2,1)S(1)}, bf16[64,512]{1,0:T(8,128)(2,1)S(1)}, u32[]{:S(2)}, u32[]{:S(2)}) collective-permute-start(bf16[64,512]{1,0:T(8,128)(2,1)S(1)} %get-tuple-element.40), channel_id=1, source_target_pairs={{0,496},{16,480},{32,464},{48,448},{64,432},{80,416},{96,400},{112... | collective-permute-start | bytes 196616 | tf_op jit(solution)/shard_map/ppermute | solution.py:519
  77.2 12.6 %all_to_all.23 = f32[32,1,128]{2,1,0:T(1,128)S(1)} all-to-all(f32[32,1,128]{2,1,0:T(1,128)S(1)} %bitcast.27), channel_id=1, replica_groups=mesh['section'=32,'dp'=16] {'section'}, dimensions={0} | all-to-all | bytes 32768 | tf_op jit(solution)/shard_map/all_to_all | solution.py:530
  89.8 0.0 collective-permute-done.3.mate
  89.8 0.0 collective-permute-done.1.outer
  89.8 0.0 collective-permute-done.2.inner
  89.8 2.7 %shard_map.178 = (bf16[512,512]{1,0:T(8,128)(2,1)}, bf16[512,512]{1,0:T(8,128)(2,1)}, bf16[512,512]{1,0:T(8,128)(2,1)}, bf16[512,512]{1,0:T(8,128)(2,1)}, f32[32...) custom-call(s32[12]{0:T(128)S(1)} %concatenate.3.meta, bf16[2,512,512]{2,1,0:T(8,128)(2,1)S(1)} %collective-permute-done.1.outer, ...), custom_call_target="tpu_custom_call" | custom-call | tf_op jit(solution)/shard_map/pallas_call | solution.py:531
Async XLA Ops:
  1.4 13.1 %collective-permute-start = (bf16[64,512]{1,0:T(8,128)(2,1)S(1)}, bf16[64,512]{1,0:T(8,128)(2,1)S(1)}, u32[]{:S(2)}, u32[]{:S(2)}) collective-permute-start(bf16[64,512]{1,0:T(8,128)(2,1)S(1)} %shard_map.171.w_d), channel_id=1, source_target_pairs={{0,496},{16,480},{32,464},{48,448},{64,432},{80,416},{96,400},{112... | collective-permute-start | bytes 196616 | tf_op jit(solution)/shard_map/ppermute | solution.py:454
  10.3 0.7 copy-start
  10.3 0.7 copy-start.1
  61.6 28.2 %collective-permute-start.1 = (bf16[2,512,512]{2,1,0:T(8,128)(2,1)S(1)}, bf16[2,512,512]{2,1,0:T(8,128)(2,1)S(1)}, u32[]{:S(2)}, u32[]{:S(2)}) collective-permute-start(bf16[2,512,512]{2,1,0:T(8,128)(2,1)S(1)} %get-tuple-element.37), channel_id=1, source_target_pairs={{16,32},{32,16},{48,64},{64,48},{80,96},{96,80},{112,128},{128,112... | collective-permute-start | bytes 3145736 | tf_op jit(solution)/shard_map/ppermute | solution.py:528
  69.4 20.5 %collective-permute-start.2 = (bf16[2,512,512]{2,1,0:T(8,128)(2,1)S(1)}, bf16[2,512,512]{2,1,0:T(8,128)(2,1)S(1)}, u32[]{:S(2)}, u32[]{:S(2)}) collective-permute-start(bf16[2,512,512]{2,1,0:T(8,128)(2,1)S(1)} %get-tuple-element.38), channel_id=1, source_target_pairs={{0,16},{16,0},{32,48},{48,32},{64,80},{80,64},{96,112},{112,96},{1... | collective-permute-start | bytes 3145736 | tf_op jit(solution)/shard_map/ppermute | solution.py:529
  72.6 17.2 %collective-permute-start.3 = (bf16[64,512]{1,0:T(8,128)(2,1)S(1)}, bf16[64,512]{1,0:T(8,128)(2,1)S(1)}, u32[]{:S(2)}, u32[]{:S(2)}) collective-permute-start(bf16[64,512]{1,0:T(8,128)(2,1)S(1)} %get-tuple-element.40), channel_id=1, source_target_pairs={{0,496},{16,480},{32,464},{48,448},{64,432},{80,416},{96,400},{112... | collective-permute-start | bytes 196616 | tf_op jit(solution)/shard_map/ppermute | solution.py:519

commit v5 on v4

--- a/solution.py
+++ b/solution.py
@@ -77,6 +77,8 @@
     cand_hbm,
     ids_d_hbm,
     ids_u_hbm,
+    offsets_hbm,
+    weights_hbm,
     w_d,
     out,
     x_d,
@@ -87,6 +89,8 @@
     cand,
     ids_d,
     ids_u,
+    offsets,
+    weights,
     sems,
 ):
     sections = meta[2]
@@ -103,7 +107,10 @@
     get_cand = pltpu.make_async_copy(cand_hbm.at[:, here], cand, sems.at[5])
     get_ids_d = pltpu.make_async_copy(ids_d_hbm, ids_d, sems.at[6])
     get_ids_u = pltpu.make_async_copy(ids_u_hbm, ids_u, sems.at[7])
-    for copy in (get_x_d, get_c_d, get_x_u, get_gain, get_cand, get_c_u, get_ids_d, get_ids_u):
+    get_offsets = pltpu.make_async_copy(offsets_hbm, offsets, sems.at[8])
+    get_weights = pltpu.make_async_copy(weights_hbm, weights, sems.at[9])
+    small = (get_ids_d, get_ids_u, get_offsets, get_weights)
+    for copy in (get_x_d, get_c_d, get_x_u, get_gain, get_cand, get_c_u, *small):
         copy.start()
     a_d, b_d = w_d[0:R], w_d[R : 2 * R]
     zero = jnp.zeros((R, width), BF16)
@@ -148,8 +155,8 @@
         out[:, PER:CROSS, :] = jnp.zeros((chunks, PER, LANES), BF16)
 
     get_c_u.wait()
-    get_ids_d.wait()
-    get_ids_u.wait()
+    for copy in small:
+        copy.wait()
 
 
 def second_partial(meta, partial, x_u, c_u, w_u, w_d, gain, cand, out):
@@ -194,7 +201,7 @@
     out[EXTRA:ROWS] = jnp.concatenate(rows, axis=0).astype(BF16)
 
 
-def middle(meta, received, down_ids, up_ids, out):
+def middle(meta, offsets, loss_weights, received, down_ids, up_ids, out):
     chunks = out.shape[0]
     place = lax.rem(meta[0], chunks)
     is_first = meta[1] == 0
@@ -202,8 +209,6 @@
     is_end = jnp.logical_or(is_first, is_last)
     inverse = 1.0 / meta[3].astype(F32)
     heads = LANES // R
-    offsets = [meta[4 + k] for k in range(heads)]
-    loss_weights = [meta[4 + heads + k] for k in range(heads)]
     total = received[0].astype(F32) + received[1].astype(F32)
     main, base_logits, cross = total[0:PER], total[PER:CROSS], total[CROSS:EXTRA]
     folded, square_rows = total[EXTRA : EXTRA + 8], total[EXTRA + 8 : EXTRA + 12]
@@ -325,33 +330,7 @@
     return jnp.concatenate([weights if k == group else zero for k in range(LANES // R)], axis=0)
 
 
-def cotangent(received, side, x, c, w, gain, cand, end, cot):
-    cot[...] = c[...].astype(F32)
-
-    @pl.when(end)
-    def _():
-        high, low = halves(columns_of(gain, cand))
-        grad = tokens_of(received, PER)
-        final = x[...].astype(F32) + nn(tokens_of(received, 0), at_rows(w[R : 2 * R], side))
-        cot[...] = nn(grad, high) + nn(grad, low) - coefficient(received, 4) * final
-
-
-def weight_grads(meta, received, x_d, x_u, c_d, c_u, w_d, w_u, gain, cand, g_d, g_u, cot):
-    is_first = meta[1] == 0
-    is_last = meta[1] == meta[2] - 1
-    act = tokens_of(received, 0)
-    work = ((1, x_u, c_u, w_u, g_u, is_first), (0, x_d, c_d, w_d, g_d, is_last))
-    for side, x, c, w, g, end in work:
-        cotangent(received, side, x, c, w, gain, cand, end, cot)
-        by_cot = tn(act, cot[...].astype(BF16))
-        by_x = tn(act, x[...])
-        grads = jnp.concatenate(
-            [by_x[64 + R * side : 64 + R * side + R], by_cot[R * side : R * side + R]], axis=0
-        )
-        g[...] = grads.astype(g.dtype)
-
-
-def token_grads(meta, received, x_d, x_u, c_d, c_u, w_d, w_u, gain, cand, outer, inner, loss, cot):
+def backward(meta, received, x_d, x_u, c_d, c_u, w_d, w_u, gain, cand, outer, inner, g_d, g_u, loss, cot):
     is_first = meta[1] == 0
     is_last = meta[1] == meta[2] - 1
     is_even = lax.rem(meta[1], 2) == 0
@@ -359,15 +338,30 @@
     def fill(ahead, behind):
         act = tokens_of(received, 0)
         work = (
-            (1, x_u, c_u, w_u, behind.at[0], ahead.at[1], is_first),
-            (0, x_d, c_d, w_d, ahead.at[0], behind.at[1], is_last),
+            (1, x_u, c_u, w_u, behind.at[0], ahead.at[1], g_u, is_first),
+            (0, x_d, c_d, w_d, ahead.at[0], behind.at[1], g_d, is_last),
         )
-        for side, x, c, w, y, dx, end in work:
+        for side, x, c, w, y, dx, g, end in work:
             wide = x[...].astype(F32)
             y[...] = (wide + nn(act, at_rows(w[R : 2 * R], side))).astype(BF16)
-            cotangent(received, side, x, c, w, gain, cand, end, cot)
-            back = cot[...] + nn(act, at_rows(w[0:R], 2 + side)) - coefficient(received, 2 * side) * wide
+            cot[...] = c[...].astype(F32)
+
+            @pl.when(end)
+            def _():
+                high, low = halves(columns_of(gain, cand))
+                grad = tokens_of(received, PER)
+                final = x[...].astype(F32) + nn(act, at_rows(w[R : 2 * R], side))
+                cot[...] = nn(grad, high) + nn(grad, low) - coefficient(received, 4) * final
+
+            held = cot[...]
+            back = held + nn(act, at_rows(w[0:R], 2 + side)) - coefficient(received, 2 * side) * wide
             dx[...] = back.astype(BF16)
+            by_cot = tn(act, held.astype(BF16))
+            by_x = tn(act, x[...])
+            grads = jnp.concatenate(
+                [by_x[64 + R * side : 64 + R * side + R], by_cot[R * side : R * side + R]], axis=0
+            )
+            g[...] = grads.astype(g.dtype)
 
     @pl.when(is_even)
     def _():
@@ -386,30 +380,39 @@
     meta, outer, inner, g_d, mate, losses, down_next, up_next, down_back, up_back, grad_a, grad_b, loss, sems
 ):
     is_even = lax.rem(meta[1], 2) == 0
-    total = g_d[...] + mate[...].astype(F32)
-    grad_a[...] = total[0:R]
-    grad_b[...] = total[R : 2 * R]
-    loss[0] = jnp.sum(losses[:, 0:1])
-
-    def write(ahead, behind):
-        copies = [
+
+    def copies_of(ahead, behind):
+        return [
             pltpu.make_async_copy(ahead.at[0], down_next, sems.at[0]),
             pltpu.make_async_copy(behind.at[0], up_next, sems.at[1]),
             pltpu.make_async_copy(behind.at[1], down_back, sems.at[2]),
             pltpu.make_async_copy(ahead.at[1], up_back, sems.at[3]),
         ]
-        for copy in copies:
+
+    @pl.when(is_even)
+    def _():
+        for copy in copies_of(outer, inner):
             copy.start()
-        for copy in copies:
+
+    @pl.when(jnp.logical_not(is_even))
+    def _():
+        for copy in copies_of(inner, outer):
+            copy.start()
+
+    total = g_d[...] + mate[...].astype(F32)
+    grad_a[...] = total[0:R]
+    grad_b[...] = total[R : 2 * R]
+    loss[0] = jnp.sum(losses[:, 0:1])
+
+    @pl.when(is_even)
+    def _():
+        for copy in copies_of(outer, inner):
             copy.wait()
 
-    @pl.when(is_even)
-    def _():
-        write(outer, inner)
-
     @pl.when(jnp.logical_not(is_even))
     def _():
-        write(inner, outer)
+        for copy in copies_of(inner, outer):
+            copy.wait()
 
 
 def shards(
@@ -454,16 +457,15 @@
     w_u = lax.ppermute(w_d, "section", mirror)
     sizes = jnp.int32(sections), jnp.int32(head_gain.shape[1])
     meta = jnp.stack([place.astype(jnp.int32), position.astype(jnp.int32), *sizes])
-    meta = jnp.concatenate([meta, offsets, loss_weights])
     id_rows = (tokens // LANES, LANES)
     ids = down_ids.reshape(id_rows), up_ids.reshape(id_rows)
-    fetched = (down_in[0], up_in[0], down_cot[0], up_cot[0], head_gain, cand, *ids)
+    fetched = (down_in[0], up_in[0], down_cot[0], up_cot[0], head_gain, cand, *ids, offsets, loss_weights)
 
     near = tokens // PER
     rings = [list(range(first, first + near)) for first in range(0, groups, near)]
     partners = [list(members) for members in zip(*rings)]
     send = shape((near, ROWS, LANES), BF16)
-    partial, x_d, x_u, c_d, c_u, gain_part, cand_part, ids_d, ids_u = pl.pallas_call(
+    partial, x_d, x_u, c_d, c_u, gain_part, cand_part, ids_d, ids_u, shifts, shares = pl.pallas_call(
         first_partial,
         out_shape=(
             send,
@@ -475,10 +477,12 @@
             shape((candidates, local_width), BF16),
             shape(id_rows, jnp.int32),
             shape(id_rows, jnp.int32),
+            shape(offsets.shape, jnp.int32),
+            shape(loss_weights.shape, jnp.int32),
         ),
-        in_specs=[smem] + [hbm] * 8 + [vmem],
-        out_specs=(vmem,) * 9,
-        scratch_shapes=[pltpu.SemaphoreType.DMA((8,))],
+        in_specs=[smem] + [hbm] * 10 + [vmem],
+        out_specs=(vmem,) * 9 + (smem,) * 2,
+        scratch_shapes=[pltpu.SemaphoreType.DMA((10,))],
         compiler_params=params,
     )(meta, *(in_hbm(held) for held in fetched), w_d)
     partial = pl.pallas_call(
@@ -501,32 +505,29 @@
     back = pl.pallas_call(
         middle,
         out_shape=shape((near, BACK_ROWS, LANES), BF16),
-        in_specs=[smem] + [vmem] * 3,
+        in_specs=[smem] * 3 + [vmem] * 3,
         out_specs=vmem,
         compiler_params=params,
-    )(meta, received, ids_d, ids_u)
+    )(meta, shifts, shares, received, ids_d, ids_u)
     gathered = lax.all_to_all(back, "dp", 0, 0, axis_index_groups=rings)
 
-    held = (meta, gathered, x_d, x_u, c_d, c_u, w_d, w_u, gain_part, cand_part)
-    g_d, g_u = pl.pallas_call(
-        weight_grads,
-        out_shape=(shape((2 * R, local_width), F32), shape((2 * R, local_width), BF16)),
+    outer, inner, g_d, g_u, loss_rows = pl.pallas_call(
+        backward,
+        out_shape=(
+            both,
+            both,
+            shape((2 * R, local_width), F32),
+            shape((2 * R, local_width), BF16),
+            shape((sections, LANES), F32),
+        ),
         in_specs=[smem] + [vmem] * 9,
-        out_specs=(vmem,) * 2,
+        out_specs=(vmem,) * 5,
         scratch_shapes=[pltpu.VMEM((tokens, local_width), F32)],
         compiler_params=params,
-    )(*held)
-    mate = lax.ppermute(g_u, "section", mirror)
-    outer, inner, loss_rows = pl.pallas_call(
-        token_grads,
-        out_shape=(both, both, shape((sections, LANES), F32)),
-        in_specs=[smem] + [vmem] * 9,
-        out_specs=(vmem,) * 3,
-        scratch_shapes=[pltpu.VMEM((tokens, local_width), F32)],
-        compiler_params=params,
-    )(*held)
+    )(meta, gathered, x_d, x_u, c_d, c_u, w_d, w_u, gain_part, cand_part)
     outer = lax.ppermute(outer, "section", between)
     inner = lax.ppermute(inner, "section", inside)
+    mate = lax.ppermute(g_u, "section", mirror)
     losses = lax.all_to_all(loss_rows, "section", 0, 0, tiled=True)
     down_next, up_next, down_back, up_back, grad_a, grad_b, loss = pl.pallas_call(
         finish,

time: 92.9 us -> 91.4 us (0.984)
    pallas_call x2 -> x1, Pallas kernels: 3.04 us -> 2.22 us  [shards(): pl.pallas_call(backward, out_shape=(both, both, shape((2 * R, local_width...]
where the time goes in v5:
time: 91.4 us; the launch traced here: 91 us
  blocking collectives  54.6 us (60%)
  starting transfers between devices  23.1 us (25%)
  Pallas kernels  12.5 us (14%)
    all_to_all x1, blocking collectives, shards(): received = lax.all_to_all(partial, 'dp', 0, 0, axis_index_groups=rings)  23 us
    all_to_all x1, blocking collectives, shards(): gathered = lax.all_to_all(back, 'dp', 0, 0, axis_index_groups=rings)  12.1 us
    all_to_all x1, blocking collectives, shards(): losses = lax.all_to_all(loss_rows, 'section', 0, 0, tiled=True)  12 us
    ppermute x1, starting transfers between devices, shards(): w_u = lax.ppermute(w_d, 'section', mirror)  8.81 us
    ppermute x1, starting transfers between devices, shards(): outer = lax.ppermute(outer, 'section', between)  7.78 us
    all_gather x1, blocking collectives, shards(): received = lax.all_gather(summed, 'dp', axis_index_groups=partners)  7.48 us
    ppermute x1, starting transfers between devices, shards(): mate = lax.ppermute(g_u, 'section', mirror)  4.56 us
    pallas_call x1, Pallas kernels, shards(): pl.pallas_call(first_partial, out_shape=(send, wide, wide, wide, wide, sh...  4.1 us
  transfers between devices with their start and end apart: 4, of which 0 were waited for; matrix products, arithmetic and copies ran while one was open for 0% of the time, Pallas kernels for 5%

profile of v5, /device:TPU:1, one launch (start us, length us, event | category | flops | bytes accessed | tf_op | source)
XLA Modules:
  0.0 91.0 jit_solution(9215184657570985445)
XLA Ops:
  0.6 0.8 shard_map.171.w_d
  1.4 8.8 %collective-permute-start = (bf16[64,512]{1,0:T(8,128)(2,1)S(1)}, bf16[64,512]{1,0:T(8,128)(2,1)S(1)}, u32[]{:S(2)}, u32[]{:S(2)}) collective-permute-start(bf16[64,512]{1,0:T(8,128)(2,1)S(1)} %shard_map.171.w_d), channel_id=1, source_target_pairs={{0,496},{16,480},{32,464},{48,448},{64,432},{80,416},{96,400},{112... | collective-permute-start | bytes 196616 | tf_op jit(solution)/shard_map/ppermute | solution.py:457
  10.3 0.1 pad_add_fusion.meta
  10.3 4.1 %shard_map.172 = (bf16[8,176,128]{2,1,0:T(8,128)(2,1)S(1)}, bf16[512,512]{1,0:T(8,128)(2,1)S(1)}, bf16[512,512]{1,0:T(8,128)(2,1)S(1)}, bf16[512,512]{1,0:T(8,12...) custom-call(s32[4]{0:T(128)S(1)} %pad_add_fusion.meta, ...), custom_call_target="tpu_custom_call" | custom-call | tf_op jit(solution)/shard_map/pallas_call | solution.py:468
  14.4 0.0 collective-permute-done.w_u
  14.5 1.0 %shard_map.173 = bf16[8,176,128]{2,1,0:T(8,128)(2,1)S(1)} custom-call(s32[4]{0:T(128)S(1)} %pad_add_fusion.meta, bf16[8,176,128]{2,1,0:T(8,128)(2,1)S(1)} %get-tuple-element.32.partial, bf16[512,512]{1,0:T(8,128)(2,1)S(1)} %get-tuple-element.33.x_u, bf16[512,512]{1,0:T(8,128)(2,1)S(1)} %get-tuple-element.34.c_u, ...), custom_call_target="tpu_custom_call" | custom-call | tf_op jit(solution)/shard_map/pallas_call | solution.py:488
  15.4 23.0 %all_to_all.21.received = bf16[8,176,128]{2,1,0:T(8,128)(2,1)S(1)} all-to-all(bf16[8,176,128]{2,1,0:T(8,128)(2,1)S(1)} %shard_map.173), channel_id=1, replica_groups={{0,1,2,3,4,5,6,7},{8,9,10,11,12,13,14,15},{16,17,18,19,20,21,22,23},{24..., dimensions={0} | all-to-all | bytes 720896 | tf_op jit(solution)/shard_map/all_to_all | solution.py:495
  38.4 0.1 shard_map.174
  38.5 7.5 %all-gather = bf16[352,128]{1,0:T(8,128)(2,1)S(1)} all-gather(bf16[176,128]{1,0:T(8,128)(2,1)S(1)} %shard_map.174), channel_id=2, replica_groups={{0,8},{1,9},{2,10},{3,11},{4,12},{5,13},{6,14},{7,15},{16,24},{17,25},{..., dimensions={0}, use_global_device_ids=true | all-gather | bytes 135168 | tf_op jit(solution)/shard_map/all_gather | solution.py:503
  46.0 1.8 %shard_map.175 = bf16[8,144,128]{2,1,0:T(8,128)(2,1)S(1)} custom-call(s32[4]{0:T(128)S(1)} %pad_add_fusion.meta, s32[4]{0:T(128)S(1)} %get-tuple-element.30.offsets, s32[4]{0:T(128)S(1)} %get-tuple-element.31.loss_weights, bf16[2,176,128]{2,1,0:T(8,128)(2,1)S(1)} %bitcast.25, s32[4,128]{1,0:T(4,128)S(1)} %get-tuple-element.37.down_ids, ...), custom_call_target="tpu_custom_call" | custom-call | tf_op jit(solution)/shard_map/pallas_call | solution.py:505
  47.8 12.1 %all_to_all.22.received = bf16[8,144,128]{2,1,0:T(8,128)(2,1)S(1)} all-to-all(bf16[8,144,128]{2,1,0:T(8,128)(2,1)S(1)} %shard_map.175), channel_id=1, replica_groups={{0,1,2,3,4,5,6,7},{8,9,10,11,12,13,14,15},{16,17,18,19,20,21,22,23},{24..., dimensions={0} | all-to-all | bytes 589824 | tf_op jit(solution)/shard_map/all_to_all | solution.py:512
  59.9 2.2 %shard_map.176 = (bf16[2,512,512]{2,1,0:T(8,128)(2,1)S(1)}, bf16[2,512,512]{2,1,0:T(8,128)(2,1)S(1)}, f32[64,512]{1,0:T(8,128)S(1)}, bf16[64,512]{1,0:T(8,128)(2,1)S(1)}, f32[32,128]{1,0:T(8,128)S(1)}) custom-call(s32[4]{0:T(128)S(1)} %pad_add_fusion.meta, bf16[8,144,128]{2,1,0:T(8,128)(2,1)S(1)} %all_to_all.22.received, ...), custom_call_target="tpu_custom_call" | custom-call | tf_op jit(solution)/shard_map/pallas_call | solution.py:514
  62.1 7.8 %collective-permute-start.1 = (bf16[2,512,512]{2,1,0:T(8,128)(2,1)S(1)}, bf16[2,512,512]{2,1,0:T(8,128)(2,1)S(1)}, u32[]{:S(2)}, u32[]{:S(2)}) collective-permute-start(bf16[2,512,512]{2,1,0:T(8,128)(2,1)S(1)} %get-tuple-element.41), channel_id=1, source_target_pairs={{16,32},{32,16},{48,64},{64,48},{80,96},{96,80},{112,128},{128,112... | collective-permute-start | bytes 3145736 | tf_op jit(solution)/shard_map/ppermute | solution.py:528
  69.9 1.9 %collective-permute-start.2 = (bf16[2,512,512]{2,1,0:T(8,128)(2,1)S(1)}, bf16[2,512,512]{2,1,0:T(8,128)(2,1)S(1)}, u32[]{:S(2)}, u32[]{:S(2)}) collective-permute-start(bf16[2,512,512]{2,1,0:T(8,128)(2,1)S(1)} %get-tuple-element.42), channel_id=1, source_target_pairs={{0,16},{16,0},{32,48},{48,32},{64,80},{80,64},{96,112},{112,96},{1... | collective-permute-start | bytes 3145736 | tf_op jit(solution)/shard_map/ppermute | solution.py:529
  71.8 4.6 %collective-permute-start.3 = (bf16[64,512]{1,0:T(8,128)(2,1)S(1)}, bf16[64,512]{1,0:T(8,128)(2,1)S(1)}, u32[]{:S(2)}, u32[]{:S(2)}) collective-permute-start(bf16[64,512]{1,0:T(8,128)(2,1)S(1)} %get-tuple-element.44), channel_id=1, source_target_pairs={{0,496},{16,480},{32,464},{48,448},{64,432},{80,416},{96,400},{112... | collective-permute-start | bytes 196616 | tf_op jit(solution)/shard_map/ppermute | solution.py:530
  76.4 12.0 %all_to_all.23 = f32[32,1,128]{2,1,0:T(1,128)S(1)} all-to-all(f32[32,1,128]{2,1,0:T(1,128)S(1)} %bitcast.27), channel_id=1, replica_groups=mesh['section'=32,'dp'=16] {'section'}, dimensions={0} | all-to-all | bytes 32768 | tf_op jit(solution)/shard_map/all_to_all | solution.py:531
  88.4 0.0 collective-permute-done.3.mate
  88.4 0.0 collective-permute-done.1.outer
  88.4 0.0 collective-permute-done.2.inner
  88.4 2.6 %shard_map.177 = (bf16[512,512]{1,0:T(8,128)(2,1)}, bf16[512,512]{1,0:T(8,128)(2,1)}, bf16[512,512]{1,0:T(8,128)(2,1)}, bf16[512,512]{1,0:T(8,128)(2,1)}, f32[32...) custom-call(s32[4]{0:T(128)S(1)} %pad_add_fusion.meta, bf16[2,512,512]{2,1,0:T(8,128)(2,1)S(1)} %collective-permute-done.1.outer, ...), custom_call_target="tpu_custom_call" | custom-call | tf_op jit(solution)/shard_map/pallas_call | solution.py:532
Async XLA Ops:
  1.4 13.0 %collective-permute-start = (bf16[64,512]{1,0:T(8,128)(2,1)S(1)}, bf16[64,512]{1,0:T(8,128)(2,1)S(1)}, u32[]{:S(2)}, u32[]{:S(2)}) collective-permute-start(bf16[64,512]{1,0:T(8,128)(2,1)S(1)} %shard_map.171.w_d), channel_id=1, source_target_pairs={{0,496},{16,480},{32,464},{48,448},{64,432},{80,416},{96,400},{112... | collective-permute-start | bytes 196616 | tf_op jit(solution)/shard_map/ppermute | solution.py:457
  62.1 26.3 %collective-permute-start.1 = (bf16[2,512,512]{2,1,0:T(8,128)(2,1)S(1)}, bf16[2,512,512]{2,1,0:T(8,128)(2,1)S(1)}, u32[]{:S(2)}, u32[]{:S(2)}) collective-permute-start(bf16[2,512,512]{2,1,0:T(8,128)(2,1)S(1)} %get-tuple-element.41), channel_id=1, source_target_pairs={{16,32},{32,16},{48,64},{64,48},{80,96},{96,80},{112,128},{128,112... | collective-permute-start | bytes 3145736 | tf_op jit(solution)/shard_map/ppermute | solution.py:528
  69.9 18.5 %collective-permute-start.2 = (bf16[2,512,512]{2,1,0:T(8,128)(2,1)S(1)}, bf16[2,512,512]{2,1,0:T(8,128)(2,1)S(1)}, u32[]{:S(2)}, u32[]{:S(2)}) collective-permute-start(bf16[2,512,512]{2,1,0:T(8,128)(2,1)S(1)} %get-tuple-element.42), channel_id=1, source_target_pairs={{0,16},{16,0},{32,48},{48,32},{64,80},{80,64},{96,112},{112,96},{1... | collective-permute-start | bytes 3145736 | tf_op jit(solution)/shard_map/ppermute | solution.py:529
  71.8 16.6 %collective-permute-start.3 = (bf16[64,512]{1,0:T(8,128)(2,1)S(1)}, bf16[64,512]{1,0:T(8,128)(2,1)S(1)}, u32[]{:S(2)}, u32[]{:S(2)}) collective-permute-start(bf16[64,512]{1,0:T(8,128)(2,1)S(1)} %get-tuple-element.44), channel_id=1, source_target_pairs={{0,496},{16,480},{32,464},{48,448},{64,432},{80,416},{96,400},{112... | collective-permute-start | bytes 196616 | tf_op jit(solution)/shard_map/ppermute | solution.py:530

commit v6 on v5

--- a/solution.py
+++ b/solution.py
@@ -13,10 +13,10 @@
 M = 32
 LANES = 128
 PER = 64
-CROSS = 2 * PER
-EXTRA = CROSS + R
-ROWS = EXTRA + 16
-BACK_ROWS = 2 * PER + 16
+PLAIN = PER + 16
+CROSS = PLAIN + PER
+ROWS = CROSS + R
+BACK_ROWS = PLAIN + PER
 
 
 def nt(a, b, precision=None):
@@ -116,7 +116,7 @@
     zero = jnp.zeros((R, width), BF16)
     wx = jnp.concatenate([a_d, zero, gated(b_d, is_last), zero], axis=0)
     wc = jnp.concatenate([zero, zero, gated(b_d, jnp.logical_not(is_last)), zero], axis=0)
-    out[:, CROSS:EXTRA, :] = jnp.zeros((chunks, R, LANES), BF16)
+    out[:, CROSS:ROWS, :] = jnp.zeros((chunks, R, LANES), BF16)
     get_x_d.wait()
     get_c_d.wait()
     main = nt(x_d[...], wx) + nt(c_d[...], wc)
@@ -133,14 +133,14 @@
         start = (j // per) * LANES
         piece = [row[:, start : start + LANES] for row in rows]
         tail = jnp.concatenate([pad] + piece + [pad[0:4]], axis=0)
-        out[j, EXTRA:ROWS, :] = tail.astype(BF16)
+        out[j, PER:PLAIN, :] = tail.astype(BF16)
     get_gain.wait()
     get_cand.wait()
 
     def logits_of(block):
         high, low = halves(columns_of(gain, cand))
         value = nt(block, high) + nt(block, low)
-        out[:, PER:CROSS, :] = value.astype(BF16).reshape(chunks, PER, LANES)
+        out[:, PLAIN:CROSS, :] = value.astype(BF16).reshape(chunks, PER, LANES)
 
     @pl.when(is_last)
     def _():
@@ -152,7 +152,7 @@
 
     @pl.when(jnp.logical_not(jnp.logical_or(is_first, is_last)))
     def _():
-        out[:, PER:CROSS, :] = jnp.zeros((chunks, PER, LANES), BF16)
+        out[:, PLAIN:CROSS, :] = jnp.zeros((chunks, PER, LANES), BF16)
 
     get_c_u.wait()
     for copy in small:
@@ -171,10 +171,9 @@
     main = nt(x_u[...], wx) + nt(c_u[...], wc)
     main = main.reshape(chunks, PER, LANES) + partial[:, 0:PER, :].astype(F32)
     out[:, 0:PER, :] = main.astype(BF16)
-    out[:, PER:ROWS, :] = partial[:, PER:ROWS, :]
-
-    @pl.when(jnp.logical_or(is_first, is_last))
-    def _():
+    rows = out.shape[1]
+    out[:, PER:rows, :] = partial[:, PER:rows, :]
+    if rows > PLAIN:
         b_d = w_d[R : 2 * R]
         b_e = jnp.where(is_last, b_d.astype(F32), b_u.astype(F32)).astype(BF16)
         high, low = halves(columns_of(gain, cand))
@@ -182,23 +181,25 @@
         own = nt(b_e, b_e)
         folded = jnp.concatenate([own[8 * r : 8 * r + 8] for r in range(4)], axis=1)
         tail = jnp.concatenate([folded, jnp.zeros((8, LANES), F32)], axis=0)
-        out[:, CROSS:EXTRA, :] = jnp.broadcast_to(cross.astype(BF16)[None], (chunks, R, LANES))
-        held = partial[:, EXTRA:ROWS, :].astype(F32) + tail[None]
-        out[:, EXTRA:ROWS, :] = held.astype(BF16)
+        out[:, CROSS:ROWS, :] = jnp.broadcast_to(cross.astype(BF16)[None], (chunks, R, LANES))
+        held = partial[:, PER:PLAIN, :].astype(F32) + tail[None]
+        out[:, PER:PLAIN, :] = held.astype(BF16)
 
 
 def gathered_sum(received, out):
     total = jnp.sum(received[...].astype(F32), axis=0)
-    folded = total[EXTRA : EXTRA + 8]
+    folded = total[PER : PER + 8]
     rows = [folded]
     for side in range(2):
-        first = EXTRA + 8 + 2 * side
+        first = PER + 8 + 2 * side
         row = total[first : first + 1] + total[first + 1 : first + 2]
         high = row.astype(BF16).astype(F32)
         rows += [high, row - high]
     rows += [jnp.zeros((4, LANES), F32)]
-    out[0:EXTRA] = total[0:EXTRA].astype(BF16)
-    out[EXTRA:ROWS] = jnp.concatenate(rows, axis=0).astype(BF16)
+    out[0:PER] = total[0:PER].astype(BF16)
+    out[PER:PLAIN] = jnp.concatenate(rows, axis=0).astype(BF16)
+    if total.shape[0] > PLAIN:
+        out[PLAIN:] = total[PLAIN:].astype(BF16)
 
 
 def middle(meta, offsets, loss_weights, received, down_ids, up_ids, out):
@@ -206,12 +207,11 @@
     place = lax.rem(meta[0], chunks)
     is_first = meta[1] == 0
     is_last = meta[1] == meta[2] - 1
-    is_end = jnp.logical_or(is_first, is_last)
+    ends = out.shape[1] > PLAIN
     inverse = 1.0 / meta[3].astype(F32)
     heads = LANES // R
     total = received[0].astype(F32) + received[1].astype(F32)
-    main, base_logits, cross = total[0:PER], total[PER:CROSS], total[CROSS:EXTRA]
-    folded, square_rows = total[EXTRA : EXTRA + 8], total[EXTRA + 8 : EXTRA + 12]
+    main, folded, square_rows = total[0:PER], total[PER : PER + 8], total[PER + 8 : PER + 12]
     lane = lax.broadcasted_iota(jnp.int32, (PER, LANES), 1)
     token = lax.broadcasted_iota(jnp.int32, (PER, LANES), 0)
     spot = lax.rem(token, M)
@@ -234,55 +234,58 @@
     sigma = jax.nn.sigmoid(pre)
     act = pre * sigma
 
-    act_e = jnp.where(is_first, act[:, R : 2 * R], act[:, 0:R])
-    cot_e = jnp.where(is_first, main[:, 3 * R :], main[:, 2 * R : 3 * R])
-    own = jnp.concatenate([folded[:, R * r : R * r + R] for r in range(4)], axis=0)
-    act_own = nn(act_e, own, HIGH)
-    out_b = cot_e + act_own
-    square_e = jnp.where(is_first, square_u, square_d)
-    square_e = square_e + jnp.sum(act_e * (cot_e + out_b), axis=1, keepdims=True)
-    scale_e = lax.rsqrt(jnp.maximum(square_e, 0.0) * inverse + EPS)
-    raw = base_logits + nn(act_e, cross, HIGH)
-    logits = raw * scale_e
-    block = lax.div(place, LANES // PER)
-    ids_d = down_ids[pl.ds(block, 1), :]
-    ids_u = up_ids[pl.ds(block, 1), :]
-    ids = jnp.where(is_first, ids_u, ids_d).astype(F32)
-    group = lax.div(lane, R)
-    within = lax.rem(lane, R)
-    weight_sum = jnp.float32(0.0)
-    for k in range(heads):
-        weight_sum = weight_sum + loss_weights[k].astype(F32)
-    top = jnp.zeros((PER, LANES), F32)
-    target = jnp.zeros((PER, LANES), F32)
-    weight = jnp.zeros((PER, LANES), F32)
-    for k in range(heads):
-        mine = group == k
-        shift = offsets[k]
-        largest = jnp.max(jnp.where(mine, logits, -jnp.inf), axis=1, keepdims=True)
-        wanted = jnp.sum(jnp.where(lane == base + token + shift, ids, 0.0), axis=1, keepdims=True)
-        factor = loss_weights[k].astype(F32) / weight_sum / ((M - shift) * sequences).astype(F32)
-        valid = jnp.where(spot + shift < M, factor, 0.0)
-        top = jnp.where(mine, largest, top)
-        target = jnp.where(mine, wanted, target)
-        weight = jnp.where(mine, valid, weight)
-    power = jnp.exp(logits - top)
-    below = jnp.ones((PER, LANES), F32)
-    for k in range(heads):
-        mine = group == k
-        below = jnp.where(mine, jnp.sum(jnp.where(mine, power, 0.0), axis=1, keepdims=True), below)
-    hit = jnp.where(within == target.astype(jnp.int32), 1.0, 0.0)
-    per_lane = hit * (top + jnp.log(below) - logits) * weight
-    loss = jnp.sum(jnp.sum(per_lane, axis=1, keepdims=True), axis=0, keepdims=True)
-    grad = weight * (power / below - hit)
-    grad_cols = grad * scale_e
-    coef_e = jnp.sum(grad * raw, axis=1, keepdims=True) * scale_e * scale_e * scale_e * inverse
-    dg_e = nt(grad_cols, cross, HIGH) - coef_e * out_b
-
     dg = pltpu.roll(main, 2 * R, axis=1)
-    dg_wide = jnp.concatenate([dg_e] * 4, axis=1)
-    replace = jnp.logical_or(jnp.logical_and(is_last, down_lane), jnp.logical_and(is_first, up_lane))
-    dg = jnp.where(replace, dg_wide, dg)
+    columns = []
+    if ends:
+        act_e = jnp.where(is_first, act[:, R : 2 * R], act[:, 0:R])
+        cot_e = jnp.where(is_first, main[:, 3 * R :], main[:, 2 * R : 3 * R])
+        own = jnp.concatenate([folded[:, R * r : R * r + R] for r in range(4)], axis=0)
+        act_own = nn(act_e, own, HIGH)
+        out_b = cot_e + act_own
+        square_e = jnp.where(is_first, square_u, square_d)
+        square_e = square_e + jnp.sum(act_e * (cot_e + out_b), axis=1, keepdims=True)
+        scale_e = lax.rsqrt(jnp.maximum(square_e, 0.0) * inverse + EPS)
+        cross = total[CROSS:ROWS]
+        raw = total[PLAIN:CROSS] + nn(act_e, cross, HIGH)
+        logits = raw * scale_e
+        block = lax.div(place, LANES // PER)
+        ids_d = down_ids[pl.ds(block, 1), :]
+        ids_u = up_ids[pl.ds(block, 1), :]
+        ids = jnp.where(is_first, ids_u, ids_d).astype(F32)
+        group = lax.div(lane, R)
+        within = lax.rem(lane, R)
+        weight_sum = jnp.float32(0.0)
+        for k in range(heads):
+            weight_sum = weight_sum + loss_weights[k].astype(F32)
+        top = jnp.zeros((PER, LANES), F32)
+        target = jnp.zeros((PER, LANES), F32)
+        weight = jnp.zeros((PER, LANES), F32)
+        for k in range(heads):
+            mine = group == k
+            shift = offsets[k]
+            largest = jnp.max(jnp.where(mine, logits, -jnp.inf), axis=1, keepdims=True)
+            wanted = jnp.sum(jnp.where(lane == base + token + shift, ids, 0.0), axis=1, keepdims=True)
+            factor = loss_weights[k].astype(F32) / weight_sum / ((M - shift) * sequences).astype(F32)
+            valid = jnp.where(spot + shift < M, factor, 0.0)
+            top = jnp.where(mine, largest, top)
+            target = jnp.where(mine, wanted, target)
+            weight = jnp.where(mine, valid, weight)
+        power = jnp.exp(logits - top)
+        below = jnp.ones((PER, LANES), F32)
+        for k in range(heads):
+            mine = group == k
+            below = jnp.where(mine, jnp.sum(jnp.where(mine, power, 0.0), axis=1, keepdims=True), below)
+        hit = jnp.where(within == target.astype(jnp.int32), 1.0, 0.0)
+        per_lane = hit * (top + jnp.log(below) - logits) * weight
+        loss = jnp.sum(jnp.sum(per_lane, axis=1, keepdims=True), axis=0, keepdims=True)
+        grad = weight * (power / below - hit)
+        grad_cols = grad * scale_e
+        coef_e = jnp.sum(grad * raw, axis=1, keepdims=True) * scale_e * scale_e * scale_e * inverse
+        dg_e = nt(grad_cols, cross, HIGH) - coef_e * out_b
+        dg_wide = jnp.concatenate([dg_e] * 4, axis=1)
+        replace = jnp.logical_or(jnp.logical_and(is_last, down_lane), jnp.logical_and(is_first, up_lane))
+        dg = jnp.where(replace, dg_wide, dg)
+        columns = [coef_e]
     d_pre = jnp.where(low_lane, dg * sigma * (1.0 + pre * (1.0 - sigma)), 0.0)
     d_scaled = d_pre * scale
     moved = d_pre * projected
@@ -291,7 +294,6 @@
     coef_d = coef_d * scale_d * scale_d * scale_d * inverse
     coef_u = coef_u * scale_u * scale_u * scale_u * inverse
     both = jnp.where(low_lane, act, pltpu.roll(d_scaled, 2 * R, axis=1))
-    head = jnp.where(is_end, grad_cols, 0.0)
 
     def parts_of(row):
         high = row.astype(BF16).astype(F32)
@@ -299,12 +301,13 @@
         return [high, low, row - high - low]
 
     rows = []
-    for col in (coef_d, coef_u, coef_e):
+    for col in (coef_d, coef_u, *columns):
         row = jnp.sum(jnp.where(lane == token, col, 0.0), axis=0, keepdims=True)
         rows += parts_of(row)[0:2]
-    rows += parts_of(jnp.broadcast_to(jnp.where(is_end, loss, 0.0), (1, LANES)))
-    rows += [jnp.zeros((7, LANES), F32)]
-    chunk = jnp.concatenate([both, head, jnp.concatenate(rows, axis=0)], axis=0)
+    if ends:
+        rows += parts_of(jnp.broadcast_to(loss, (1, LANES)))
+    rows += [jnp.zeros((16 - len(rows), LANES), F32)]
+    chunk = jnp.concatenate([both] + rows + ([grad_cols] if ends else []), axis=0)
     out[...] = jnp.broadcast_to(chunk.astype(BF16)[None], out.shape)
 
 
@@ -319,7 +322,7 @@
     token = lax.broadcasted_iota(jnp.int32, (PER, LANES), 0)
     cols = []
     for j in range(chunks):
-        rows = received[j, CROSS:BACK_ROWS, :].astype(F32)
+        rows = received[j, PER:PLAIN, :].astype(F32)
         both = rows[row : row + 1] + rows[row + 1 : row + 2]
         cols.append(jnp.sum(jnp.where(lane == token, both, 0.0), axis=1, keepdims=True))
     return jnp.concatenate(cols, axis=0)
@@ -346,12 +349,14 @@
             y[...] = (wide + nn(act, at_rows(w[R : 2 * R], side))).astype(BF16)
             cot[...] = c[...].astype(F32)
 
-            @pl.when(end)
-            def _():
-                high, low = halves(columns_of(gain, cand))
-                grad = tokens_of(received, PER)
-                final = x[...].astype(F32) + nn(act, at_rows(w[R : 2 * R], side))
-                cot[...] = nn(grad, high) + nn(grad, low) - coefficient(received, 4) * final
+            if received.shape[1] > PLAIN:
+
+                @pl.when(end)
+                def _():
+                    high, low = halves(columns_of(gain, cand))
+                    grad = tokens_of(received, PLAIN)
+                    final = x[...].astype(F32) + nn(act, at_rows(w[R : 2 * R], side))
+                    cot[...] = nn(grad, high) + nn(grad, low) - coefficient(received, 4) * final
 
             held = cot[...]
             back = held + nn(act, at_rows(w[0:R], 2 + side)) - coefficient(received, 2 * side) * wide
@@ -371,8 +376,10 @@
     def _():
         fill(outer, inner)
 
-    rows = jnp.sum(received[:, CROSS:BACK_ROWS, :].astype(F32), axis=0)
-    total = rows[6:7] + rows[7:8] + rows[8:9]
+    total = jnp.zeros((1, LANES), F32)
+    if received.shape[1] > PLAIN:
+        rows = jnp.sum(received[:, PER:PLAIN, :].astype(F32), axis=0)
+        total = rows[6:7] + rows[7:8] + rows[8:9]
     loss[...] = jnp.broadcast_to(total, loss.shape)
 
 
@@ -485,46 +492,55 @@
         scratch_shapes=[pltpu.SemaphoreType.DMA((10,))],
         compiler_params=params,
     )(meta, *(in_hbm(held) for held in fetched), w_d)
-    partial = pl.pallas_call(
-        second_partial,
-        out_shape=send,
-        in_specs=[smem] + [vmem] * 7,
-        out_specs=vmem,
-        compiler_params=params,
-    )(meta, partial, x_u, c_u, w_u, w_d, gain_part, cand_part)
-    received = lax.all_to_all(partial, "dp", 0, 0, axis_index_groups=rings)
-    summed = pl.pallas_call(
-        gathered_sum,
-        out_shape=shape((ROWS, LANES), BF16),
-        in_specs=[vmem],
-        out_specs=vmem,
-        compiler_params=params,
-    )(received)
-    received = lax.all_gather(summed, "dp", axis_index_groups=partners)
-
-    back = pl.pallas_call(
-        middle,
-        out_shape=shape((near, BACK_ROWS, LANES), BF16),
-        in_specs=[smem] * 3 + [vmem] * 3,
-        out_specs=vmem,
-        compiler_params=params,
-    )(meta, shifts, shares, received, ids_d, ids_u)
-    gathered = lax.all_to_all(back, "dp", 0, 0, axis_index_groups=rings)
-
-    outer, inner, g_d, g_u, loss_rows = pl.pallas_call(
-        backward,
-        out_shape=(
-            both,
-            both,
-            shape((2 * R, local_width), F32),
-            shape((2 * R, local_width), BF16),
-            shape((sections, LANES), F32),
-        ),
-        in_specs=[smem] + [vmem] * 9,
-        out_specs=(vmem,) * 5,
-        scratch_shapes=[pltpu.VMEM((tokens, local_width), F32)],
-        compiler_params=params,
-    )(meta, gathered, x_d, x_u, c_d, c_u, w_d, w_u, gain_part, cand_part)
+
+    def over_dp(rows, back_rows):
+        def run(meta, partial, x_d, x_u, c_d, c_u, w_d, w_u, gain_part, cand_part, shifts, shares, ids_d, ids_u):
+            chunk = pl.pallas_call(
+                second_partial,
+                out_shape=shape((near, rows, LANES), BF16),
+                in_specs=[smem] + [vmem] * 7,
+                out_specs=vmem,
+                compiler_params=params,
+            )(meta, partial, x_u, c_u, w_u, w_d, gain_part, cand_part)
+            received = lax.all_to_all(chunk, "dp", 0, 0, axis_index_groups=rings)
+            summed = pl.pallas_call(
+                gathered_sum,
+                out_shape=shape((rows, LANES), BF16),
+                in_specs=[vmem],
+                out_specs=vmem,
+                compiler_params=params,
+            )(received)
+            received = lax.all_gather(summed, "dp", axis_index_groups=partners)
+            back = pl.pallas_call(
+                middle,
+                out_shape=shape((near, back_rows, LANES), BF16),
+                in_specs=[smem] * 3 + [vmem] * 3,
+                out_specs=vmem,
+                compiler_params=params,
+            )(meta, shifts, shares, received, ids_d, ids_u)
+            gathered = lax.all_to_all(back, "dp", 0, 0, axis_index_groups=rings)
+            return pl.pallas_call(
+                backward,
+                out_shape=(
+                    both,
+                    both,
+                    shape((2 * R, local_width), F32),
+                    shape((2 * R, local_width), BF16),
+                    shape((sections, LANES), F32),
+                ),
+                in_specs=[smem] + [vmem] * 9,
+                out_specs=(vmem,) * 5,
+                scratch_shapes=[pltpu.VMEM((tokens, local_width), F32)],
+                compiler_params=params,
+            )(meta, gathered, x_d, x_u, c_d, c_u, w_d, w_u, gain_part, cand_part)
+
+        return run
+
+    held = (meta, partial, x_d, x_u, c_d, c_u, w_d, w_u, gain_part, cand_part, shifts, shares, ids_d, ids_u)
+    is_end = jnp.logical_or(position == 0, position == sections - 1)
+    outer, inner, g_d, g_u, loss_rows = lax.cond(
+        is_end, over_dp(ROWS, BACK_ROWS), over_dp(PLAIN, PLAIN), *held
+    )
     outer = lax.ppermute(outer, "section", between)
     inner = lax.ppermute(inner, "section", inside)
     mate = lax.ppermute(g_u, "section", mirror)

time: 91.4 us -> 87.7 us (0.960)
  blocking collectives: 54.6 us -> 48.5 us
  starting transfers between devices: 23.1 us -> 26 us
    all_to_all x2, blocking collectives: 35.1 us -> 29.7 us  [the longest x1 18.3 us: run(): received = lax.all_to_all(chunk, 'dp', 0, 0, axis_index_groups=rings)]
    ppermute x1, starting transfers between devices: 1.92 us -> 6.69 us  [shards(): inner = lax.ppermute(inner, 'section', inside)]
    ppermute x1, starting transfers between devices: 7.78 us -> 5.54 us  [shards(): outer = lax.ppermute(outer, 'section', between)]
where the time goes in v6:
time: 87.7 us; the launch traced here: 87.3 us
  blocking collectives  48.5 us (55%)
  starting transfers between devices  26 us (30%)
  Pallas kernels  12 us (14%)
    all_to_all x1, blocking collectives, run(): received = lax.all_to_all(chunk, 'dp', 0, 0, axis_index_groups=rings)  18.3 us
    all_to_all x1, blocking collectives, shards(): losses = lax.all_to_all(loss_rows, 'section', 0, 0, tiled=True)  11.6 us
    all_to_all x1, blocking collectives, run(): gathered = lax.all_to_all(back, 'dp', 0, 0, axis_index_groups=rings)  11.4 us
    ppermute x1, starting transfers between devices, shards(): w_u = lax.ppermute(w_d, 'section', mirror)  8.81 us
    all_gather x1, blocking collectives, run(): received = lax.all_gather(summed, 'dp', axis_index_groups=partners)  7.22 us
    ppermute x1, starting transfers between devices, shards(): inner = lax.ppermute(inner, 'section', inside)  6.69 us
    ppermute x1, starting transfers between devices, shards(): outer = lax.ppermute(outer, 'section', between)  5.54 us
    ppermute x1, starting transfers between devices, shards(): mate = lax.ppermute(g_u, 'section', mirror)  4.93 us
  transfers between devices with their start and end apart: 4, of which 0 were waited for; matrix products, arithmetic and copies ran while one was open for 0% of the time, Pallas kernels for 5%

profile of v6, /device:TPU:1, one launch (start us, length us, event | category | flops | bytes accessed | tf_op | source)
XLA Modules:
  0.0 87.3 jit_solution(7135387353362498058)
XLA Ops:
  0.6 0.8 shard_map.171.w_d
  1.4 8.8 %collective-permute-start = (bf16[64,512]{1,0:T(8,128)(2,1)S(1)}, bf16[64,512]{1,0:T(8,128)(2,1)S(1)}, u32[]{:S(2)}, u32[]{:S(2)}) collective-permute-start(bf16[64,512]{1,0:T(8,128)(2,1)S(1)} %shard_map.171.w_d), channel_id=1, source_target_pairs={{0,496},{16,480},{32,464},{48,448},{64,432},{80,416},{96,400},{112... | collective-permute-start | bytes 196616 | tf_op jit(solution)/shard_map/ppermute | solution.py:464
  10.3 0.1 pad_add_fusion.meta
  10.3 4.1 %shard_map.172 = (bf16[8,176,128]{2,1,0:T(8,128)(2,1)S(1)}, bf16[512,512]{1,0:T(8,128)(2,1)S(1)}, bf16[512,512]{1,0:T(8,128)(2,1)S(1)}, bf16[512,512]{1,0:T(8,12...) custom-call(s32[4]{0:T(128)S(1)} %pad_add_fusion.meta, ...), custom_call_target="tpu_custom_call" | custom-call | tf_op jit(solution)/shard_map/pallas_call | solution.py:475
  14.4 0.0 collective-permute-done
  14.5 41.5 %conditional.1 = ((bf16[2,512,512]{2,1,0:T(8,128)(2,1)S(1)}, bf16[2,512,512]{2,1,0:T(8,128)(2,1)}, f32[64,512]{1,0:T(8,128)S(1)}, bf16[64,512]{1,0:T(8,128)(2,1)S(1)}, f32[32,128]{1,0:T(8,128)S(1)})) conditional(s32[]{:T(128)} %convert_element_type.3, (s32[4]{0:T(128)S(1)}, bf16[8,176,128]{2,1,0:T(8,128)(2,1)S(1)}, bf16[512,512]{1,0:T(8,128)(2,1)S(1)}, ...), branch_computations={%region_0.0_spmd, %region_1.0_spmd} | conditional | bytes 1445896 | solution.py:541
  14.5 1.0 %branch_0_fun.4 = bf16[8,80,128]{2,1,0:T(8,128)(2,1)S(1)} custom-call(s32[4]{0:T(128)S(1)} %get-tuple-element.56.meta, bf16[8,176,128]{2,1,0:T(8,128)(2,1)S(1)} %get-tuple-element.59.partial, bf16[512,512]{1,0:T(8,128)(2,1)S(1)} %get-tuple-element.60.x_u, bf16[512,512]{1,0:T(8,128)(2,1)S(1)} %get-tuple-element.61.c_u, ...), custom_call_target="tpu_custom_call" | custom-call | tf_op jit(solution)/shard_map/cond/branch_0_fun/pallas_call | solution.py:498
  15.5 18.3 %all_to_all.27.received = bf16[8,80,128]{2,1,0:T(8,128)(2,1)S(1)} all-to-all(bf16[8,80,128]{2,1,0:T(8,128)(2,1)S(1)} %branch_0_fun.4), channel_id=1, replica_groups={{0,1,2,3,4,5,6,7},{8,9,10,11,12,13,14,15},{16,17,18,19,20,21,22,23},{24..., dimensions={0} | all-to-all | bytes 327680 | tf_op jit(solution)/shard_map/cond/branch_0_fun/all_to_all | solution.py:505
  33.8 7.2 %all-gather = bf16[160,128]{1,0:T(8,128)(2,1)S(1)} all-gather(bf16[80,128]{1,0:T(8,128)(2,1)S(1)} %branch_0_fun.5), channel_id=2, replica_groups={{0,8},{1,9},{2,10},{3,11},{4,12},{5,13},{6,14},{7,15},{16,24},{17,25},{..., dimensions={0}, use_global_device_ids=true | all-gather | bytes 61440 | tf_op jit(solution)/shard_map/cond/branch_0_fun/all_gather | solution.py:513
  41.0 0.8 branch_0_fun.6
  41.9 11.4 %all_to_all.28.received = bf16[8,80,128]{2,1,0:T(8,128)(2,1)S(1)} all-to-all(bf16[8,80,128]{2,1,0:T(8,128)(2,1)S(1)} %branch_0_fun.6), channel_id=1, replica_groups={{0,1,2,3,4,5,6,7},{8,9,10,11,12,13,14,15},{16,17,18,19,20,21,22,23},{24..., dimensions={0} | all-to-all | bytes 327680 | tf_op jit(solution)/shard_map/cond/branch_0_fun/all_to_all | solution.py:521
  53.2 2.7 %branch_0_fun.7 = (bf16[2,512,512]{2,1,0:T(8,128)(2,1)S(1)}, bf16[2,512,512]{2,1,0:T(8,128)(2,1)}, f32[64,512]{1,0:T(8,128)S(1)}, bf16[64,512]{1,0:T(8,128)(2,1)S(1)}, f32[32,128]{1,0:T(8,128)S(1)}) custom-call(s32[4]{0:T(128)S(1)} %get-tuple-element.56.meta, bf16[8,80,128]{2,1,0:T(8,128)(2,1)S(1)} %all_to_all.28.received, ...), custom_call_target="tpu_custom_call" | custom-call | tf_op jit(solution)/shard_map/cond/branch_0_fun/pallas_call | solution.py:522
  56.0 5.5 %collective-permute-start.1 = (bf16[2,512,512]{2,1,0:T(8,128)(2,1)S(1)}, bf16[2,512,512]{2,1,0:T(8,128)(2,1)S(1)}, u32[]{:S(2)}, u32[]{:S(2)}) collective-permute-start(bf16[2,512,512]{2,1,0:T(8,128)(2,1)S(1)} %get-tuple-element.125), channel_id=1, source_target_pairs={{16,32},{32,16},{48,64},{64,48},{80,96},{96,80},{112,128},{128,112... | collective-permute-start | bytes 3145736 | tf_op jit(solution)/shard_map/ppermute | solution.py:544
  61.5 6.7 %collective-permute-start.2 = (bf16[2,512,512]{2,1,0:T(8,128)(2,1)}, bf16[2,512,512]{2,1,0:T(8,128)(2,1)S(1)}, u32[]{:S(2)}, u32[]{:S(2)}) collective-permute-start(bf16[2,512,512]{2,1,0:T(8,128)(2,1)} %get-tuple-element.126), channel_id=1, source_target_pairs={{0,16},{16,0},{32,48},{48,32},{64,80},{80,64},{96,112},{112,96},{1... | collective-permute-start | bytes 3145736 | tf_op jit(solution)/shard_map/ppermute | solution.py:545
  68.2 4.9 %collective-permute-start.3 = (bf16[64,512]{1,0:T(8,128)(2,1)S(1)}, bf16[64,512]{1,0:T(8,128)(2,1)S(1)}, u32[]{:S(2)}, u32[]{:S(2)}) collective-permute-start(bf16[64,512]{1,0:T(8,128)(2,1)S(1)} %get-tuple-element.128), channel_id=1, source_target_pairs={{0,496},{16,480},{32,464},{48,448},{64,432},{80,416},{96,400},{112... | collective-permute-start | bytes 196616 | tf_op jit(solution)/shard_map/ppermute | solution.py:546
  73.2 11.6 %all_to_all.31 = f32[32,1,128]{2,1,0:T(1,128)S(1)} all-to-all(f32[32,1,128]{2,1,0:T(1,128)S(1)} %bitcast.33), channel_id=1, replica_groups=mesh['section'=32,'dp'=16] {'section'}, dimensions={0} | all-to-all | bytes 32768 | tf_op jit(solution)/shard_map/all_to_all | solution.py:547
  84.7 0.0 collective-permute-done.3.mate
  84.7 0.0 collective-permute-done.1.outer
  84.7 0.0 collective-permute-done.2.inner
  84.7 2.6 %shard_map.173 = (bf16[512,512]{1,0:T(8,128)(2,1)}, bf16[512,512]{1,0:T(8,128)(2,1)}, bf16[512,512]{1,0:T(8,128)(2,1)}, bf16[512,512]{1,0:T(8,128)(2,1)}, f32[32...) custom-call(s32[4]{0:T(128)S(1)} %pad_add_fusion.meta, bf16[2,512,512]{2,1,0:T(8,128)(2,1)S(1)} %collective-permute-done.1.outer, ...), custom_call_target="tpu_custom_call" | custom-call | tf_op jit(solution)/shard_map/pallas_call | solution.py:548
  (1 shorter events, 0.0 us)
Async XLA Ops:
  1.4 13.0 %collective-permute-start = (bf16[64,512]{1,0:T(8,128)(2,1)S(1)}, bf16[64,512]{1,0:T(8,128)(2,1)S(1)}, u32[]{:S(2)}, u32[]{:S(2)}) collective-permute-start(bf16[64,512]{1,0:T(8,128)(2,1)S(1)} %shard_map.171.w_d), channel_id=1, source_target_pairs={{0,496},{16,480},{32,464},{48,448},{64,432},{80,416},{96,400},{112... | collective-permute-start | bytes 196616 | tf_op jit(solution)/shard_map/ppermute | solution.py:464
  56.0 28.8 %collective-permute-start.1 = (bf16[2,512,512]{2,1,0:T(8,128)(2,1)S(1)}, bf16[2,512,512]{2,1,0:T(8,128)(2,1)S(1)}, u32[]{:S(2)}, u32[]{:S(2)}) collective-permute-start(bf16[2,512,512]{2,1,0:T(8,128)(2,1)S(1)} %get-tuple-element.125), channel_id=1, source_target_pairs={{16,32},{32,16},{48,64},{64,48},{80,96},{96,80},{112,128},{128,112... | collective-permute-start | bytes 3145736 | tf_op jit(solution)/shard_map/ppermute | solution.py:544
  61.5 23.2 %collective-permute-start.2 = (bf16[2,512,512]{2,1,0:T(8,128)(2,1)}, bf16[2,512,512]{2,1,0:T(8,128)(2,1)S(1)}, u32[]{:S(2)}, u32[]{:S(2)}) collective-permute-start(bf16[2,512,512]{2,1,0:T(8,128)(2,1)} %get-tuple-element.126), channel_id=1, source_target_pairs={{0,16},{16,0},{32,48},{48,32},{64,80},{80,64},{96,112},{112,96},{1... | collective-permute-start | bytes 3145736 | tf_op jit(solution)/shard_map/ppermute | solution.py:545
  68.2 16.5 %collective-permute-start.3 = (bf16[64,512]{1,0:T(8,128)(2,1)S(1)}, bf16[64,512]{1,0:T(8,128)(2,1)S(1)}, u32[]{:S(2)}, u32[]{:S(2)}) collective-permute-start(bf16[64,512]{1,0:T(8,128)(2,1)S(1)} %get-tuple-element.128), channel_id=1, source_target_pairs={{0,496},{16,480},{32,464},{48,448},{64,432},{80,416},{96,400},{112... | collective-permute-start | bytes 196616 | tf_op jit(solution)/shard_map/ppermute | solution.py:546

commit v7 on v6

--- a/solution.py
+++ b/solution.py
@@ -349,14 +349,12 @@
             y[...] = (wide + nn(act, at_rows(w[R : 2 * R], side))).astype(BF16)
             cot[...] = c[...].astype(F32)
 
-            if received.shape[1] > PLAIN:
-
-                @pl.when(end)
-                def _():
-                    high, low = halves(columns_of(gain, cand))
-                    grad = tokens_of(received, PLAIN)
-                    final = x[...].astype(F32) + nn(act, at_rows(w[R : 2 * R], side))
-                    cot[...] = nn(grad, high) + nn(grad, low) - coefficient(received, 4) * final
+            @pl.when(end)
+            def _():
+                high, low = halves(columns_of(gain, cand))
+                grad = tokens_of(received, PLAIN)
+                final = x[...].astype(F32) + nn(act, at_rows(w[R : 2 * R], side))
+                cot[...] = nn(grad, high) + nn(grad, low) - coefficient(received, 4) * final
 
             held = cot[...]
             back = held + nn(act, at_rows(w[0:R], 2 + side)) - coefficient(received, 2 * side) * wide
@@ -376,10 +374,8 @@
     def _():
         fill(outer, inner)
 
-    total = jnp.zeros((1, LANES), F32)
-    if received.shape[1] > PLAIN:
-        rows = jnp.sum(received[:, PER:PLAIN, :].astype(F32), axis=0)
-        total = rows[6:7] + rows[7:8] + rows[8:9]
+    rows = jnp.sum(received[:, PER:PLAIN, :].astype(F32), axis=0)
+    total = rows[6:7] + rows[7:8] + rows[8:9]
     loss[...] = jnp.broadcast_to(total, loss.shape)
 
 
@@ -494,7 +490,7 @@
     )(meta, *(in_hbm(held) for held in fetched), w_d)
 
     def over_dp(rows, back_rows):
-        def run(meta, partial, x_d, x_u, c_d, c_u, w_d, w_u, gain_part, cand_part, shifts, shares, ids_d, ids_u):
+        def run(meta, partial, x_u, c_u, w_d, w_u, gain_part, cand_part, shifts, shares, ids_d, ids_u):
             chunk = pl.pallas_call(
                 second_partial,
                 out_shape=shape((near, rows, LANES), BF16),
@@ -519,28 +515,27 @@
                 compiler_params=params,
             )(meta, shifts, shares, received, ids_d, ids_u)
             gathered = lax.all_to_all(back, "dp", 0, 0, axis_index_groups=rings)
-            return pl.pallas_call(
-                backward,
-                out_shape=(
-                    both,
-                    both,
-                    shape((2 * R, local_width), F32),
-                    shape((2 * R, local_width), BF16),
-                    shape((sections, LANES), F32),
-                ),
-                in_specs=[smem] + [vmem] * 9,
-                out_specs=(vmem,) * 5,
-                scratch_shapes=[pltpu.VMEM((tokens, local_width), F32)],
-                compiler_params=params,
-            )(meta, gathered, x_d, x_u, c_d, c_u, w_d, w_u, gain_part, cand_part)
+            return jnp.pad(gathered, ((0, 0), (0, BACK_ROWS - back_rows), (0, 0)))
 
         return run
 
-    held = (meta, partial, x_d, x_u, c_d, c_u, w_d, w_u, gain_part, cand_part, shifts, shares, ids_d, ids_u)
+    held = (meta, partial, x_u, c_u, w_d, w_u, gain_part, cand_part, shifts, shares, ids_d, ids_u)
     is_end = jnp.logical_or(position == 0, position == sections - 1)
-    outer, inner, g_d, g_u, loss_rows = lax.cond(
-        is_end, over_dp(ROWS, BACK_ROWS), over_dp(PLAIN, PLAIN), *held
-    )
+    gathered = lax.cond(is_end, over_dp(ROWS, BACK_ROWS), over_dp(PLAIN, PLAIN), *held)
+    outer, inner, g_d, g_u, loss_rows = pl.pallas_call(
+        backward,
+        out_shape=(
+            both,
+            both,
+            shape((2 * R, local_width), F32),
+            shape((2 * R, local_width), BF16),
+            shape((sections, LANES), F32),
+        ),
+        in_specs=[smem] + [vmem] * 9,
+        out_specs=(vmem,) * 5,
+        scratch_shapes=[pltpu.VMEM((tokens, local_width), F32)],
+        compiler_params=params,
+    )(meta, gathered, x_d, x_u, c_d, c_u, w_d, w_u, gain_part, cand_part)
     outer = lax.ppermute(outer, "section", between)
     inner = lax.ppermute(inner, "section", inside)
     mate = lax.ppermute(g_u, "section", mirror)

time: 87.7 us -> 86.7 us (0.989)
  no operation moved by 1% of the time
where the time goes in v7:
time: 86.7 us; the launch traced here: 86.3 us
  blocking collectives  48.5 us (56%)
  starting transfers between devices  25.5 us (29%)
  Pallas kernels  11.4 us (13%)
    all_to_all x1, blocking collectives, run(): received = lax.all_to_all(chunk, 'dp', 0, 0, axis_index_groups=rings)  18.4 us
    all_to_all x1, blocking collectives, shards(): losses = lax.all_to_all(loss_rows, 'section', 0, 0, tiled=True)  11.5 us
    all_to_all x1, blocking collectives, run(): gathered = lax.all_to_all(back, 'dp', 0, 0, axis_index_groups=rings)  11.4 us
    ppermute x1, starting transfers between devices, shards(): w_u = lax.ppermute(w_d, 'section', mirror)  8.81 us
    all_gather x1, blocking collectives, run(): received = lax.all_gather(summed, 'dp', axis_index_groups=partners)  7.22 us
    ppermute x1, starting transfers between devices, shards(): inner = lax.ppermute(inner, 'section', inside)  6.18 us
    ppermute x1, starting transfers between devices, shards(): outer = lax.ppermute(outer, 'section', between)  5.55 us
    ppermute x1, starting transfers between devices, shards(): mate = lax.ppermute(g_u, 'section', mirror)  4.96 us
  transfers between devices with their start and end apart: 4, of which 0 were waited for; matrix products, arithmetic and copies ran while one was open for 0% of the time, Pallas kernels for 5%

profile of v7, /device:TPU:1, one launch (start us, length us, event | category | flops | bytes accessed | tf_op | source)
XLA Modules:
  0.0 86.3 jit_solution(13182157902149944987)
XLA Ops:
  0.6 0.8 shard_map.171.w_d
  1.4 8.8 %collective-permute-start = (bf16[64,512]{1,0:T(8,128)(2,1)S(1)}, bf16[64,512]{1,0:T(8,128)(2,1)S(1)}, u32[]{:S(2)}, u32[]{:S(2)}) collective-permute-start(bf16[64,512]{1,0:T(8,128)(2,1)S(1)} %shard_map.171.w_d), channel_id=1, source_target_pairs={{0,496},{16,480},{32,464},{48,448},{64,432},{80,416},{96,400},{112... | collective-permute-start | bytes 196616 | tf_op jit(solution)/shard_map/ppermute | solution.py:460
  10.3 0.1 pad_add_fusion.meta
  10.3 4.1 %shard_map.172 = (bf16[8,176,128]{2,1,0:T(8,128)(2,1)S(1)}, bf16[512,512]{1,0:T(8,128)(2,1)S(1)}, bf16[512,512]{1,0:T(8,128)(2,1)S(1)}, bf16[512,512]{1,0:T(8,12...) custom-call(s32[4]{0:T(128)S(1)} %pad_add_fusion.meta, ...), custom_call_target="tpu_custom_call" | custom-call | tf_op jit(solution)/shard_map/pallas_call | solution.py:471
  14.4 0.0 collective-permute-done.w_u
  14.5 38.8 %conditional.1 = (bf16[8,144,128]{2,1,0:T(8,128)(2,1)S(1)}) conditional(s32[]{:T(128)} %convert_element_type.5, (s32[4]{0:T(128)S(1)}, bf16[8,176,128]{2,1,0:T(8,128)(2,1)S(1)}, bf16[512,512]{1,0:T(8,128)(2,1)S(1)}, bf16[512,512]{1,0:T(8,128)(2,1)S(1)}, bf16[64,512]{1,0:T(8,128)(2,1)S(1)}, /*index=5*/bf16[64,512]{1,0:T(8,128)(2,1)S(1)}, ...), branch_computations={%region_0.1_spmd, %region_1.2_spmd} | conditional | bytes 1445896 | solution.py:524
  14.5 1.0 %branch_0_fun.3 = bf16[8,80,128]{2,1,0:T(8,128)(2,1)S(1)} custom-call(s32[4]{0:T(128)S(1)} %get-tuple-element.35.meta, bf16[8,176,128]{2,1,0:T(8,128)(2,1)S(1)} %get-tuple-element.54.partial, bf16[512,512]{1,0:T(8,128)(2,1)S(1)} %get-tuple-element.55.x_u, bf16[512,512]{1,0:T(8,128)(2,1)S(1)} %get-tuple-element.56.c_u, ...), custom_call_target="tpu_custom_call" | custom-call | tf_op jit(solution)/shard_map/cond/branch_0_fun/pallas_call | solution.py:494
  15.5 18.4 %all_to_all.27.received = bf16[8,80,128]{2,1,0:T(8,128)(2,1)S(1)} all-to-all(bf16[8,80,128]{2,1,0:T(8,128)(2,1)S(1)} %branch_0_fun.3), channel_id=1, replica_groups={{0,1,2,3,4,5,6,7},{8,9,10,11,12,13,14,15},{16,17,18,19,20,21,22,23},{24..., dimensions={0} | all-to-all | bytes 327680 | tf_op jit(solution)/shard_map/cond/branch_0_fun/all_to_all | solution.py:501
  33.9 7.2 %all-gather = bf16[160,128]{1,0:T(8,128)(2,1)S(1)} all-gather(bf16[80,128]{1,0:T(8,128)(2,1)S(1)} %branch_0_fun.4), channel_id=2, replica_groups={{0,8},{1,9},{2,10},{3,11},{4,12},{5,13},{6,14},{7,15},{16,24},{17,25},{..., dimensions={0}, use_global_device_ids=true | all-gather | bytes 61440 | tf_op jit(solution)/shard_map/cond/branch_0_fun/all_gather | solution.py:509
  41.1 0.8 branch_0_fun.5
  41.9 11.4 %all_to_all.28 = bf16[8,80,128]{2,1,0:T(8,128)(2,1)S(1)} all-to-all(bf16[8,80,128]{2,1,0:T(8,128)(2,1)S(1)} %branch_0_fun.5), channel_id=1, replica_groups={{0,1,2,3,4,5,6,7},{8,9,10,11,12,13,14,15},{16,17,18,19,20,21,22,23},{24..., dimensions={0} | all-to-all | bytes 327680 | tf_op jit(solution)/shard_map/cond/branch_0_fun/all_to_all | solution.py:517
  53.3 2.1 %shard_map.173 = (bf16[2,512,512]{2,1,0:T(8,128)(2,1)S(1)}, bf16[2,512,512]{2,1,0:T(8,128)(2,1)S(1)}, f32[64,512]{1,0:T(8,128)S(1)}, bf16[64,512]{1,0:T(8,128)(2,1)S(1)}, f32[32,128]{1,0:T(8,128)S(1)}) custom-call(s32[4]{0:T(128)S(1)} %pad_add_fusion.meta, bf16[8,144,128]{2,1,0:T(8,128)(2,1)S(1)} %get-tuple-element.128.received, ...), custom_call_target="tpu_custom_call" | custom-call | tf_op jit(solution)/shard_map/pallas_call | solution.py:525
  55.4 5.5 %collective-permute-start.1 = (bf16[2,512,512]{2,1,0:T(8,128)(2,1)S(1)}, bf16[2,512,512]{2,1,0:T(8,128)(2,1)S(1)}, u32[]{:S(2)}, u32[]{:S(2)}) collective-permute-start(bf16[2,512,512]{2,1,0:T(8,128)(2,1)S(1)} %get-tuple-element.116), channel_id=1, source_target_pairs={{16,32},{32,16},{48,64},{64,48},{80,96},{96,80},{112,128},{128,112... | collective-permute-start | bytes 3145736 | tf_op jit(solution)/shard_map/ppermute | solution.py:539
  61.0 6.2 %collective-permute-start.2 = (bf16[2,512,512]{2,1,0:T(8,128)(2,1)S(1)}, bf16[2,512,512]{2,1,0:T(8,128)(2,1)S(1)}, u32[]{:S(2)}, u32[]{:S(2)}) collective-permute-start(bf16[2,512,512]{2,1,0:T(8,128)(2,1)S(1)} %get-tuple-element.117), channel_id=1, source_target_pairs={{0,16},{16,0},{32,48},{48,32},{64,80},{80,64},{96,112},{112,96},{1... | collective-permute-start | bytes 3145736 | tf_op jit(solution)/shard_map/ppermute | solution.py:540
  67.2 5.0 %collective-permute-start.3 = (bf16[64,512]{1,0:T(8,128)(2,1)S(1)}, bf16[64,512]{1,0:T(8,128)(2,1)S(1)}, u32[]{:S(2)}, u32[]{:S(2)}) collective-permute-start(bf16[64,512]{1,0:T(8,128)(2,1)S(1)} %get-tuple-element.119), channel_id=1, source_target_pairs={{0,496},{16,480},{32,464},{48,448},{64,432},{80,416},{96,400},{112... | collective-permute-start | bytes 196616 | tf_op jit(solution)/shard_map/ppermute | solution.py:541
  72.1 11.5 %all_to_all.31 = f32[32,1,128]{2,1,0:T(1,128)S(1)} all-to-all(f32[32,1,128]{2,1,0:T(1,128)S(1)} %bitcast.29), channel_id=1, replica_groups=mesh['section'=32,'dp'=16] {'section'}, dimensions={0} | all-to-all | bytes 32768 | tf_op jit(solution)/shard_map/all_to_all | solution.py:542
  83.7 0.0 collective-permute-done.3.mate
  83.7 0.0 collective-permute-done.1.outer
  83.7 0.0 collective-permute-done.2.inner
  83.7 2.6 %shard_map.174 = (bf16[512,512]{1,0:T(8,128)(2,1)}, bf16[512,512]{1,0:T(8,128)(2,1)}, bf16[512,512]{1,0:T(8,128)(2,1)}, bf16[512,512]{1,0:T(8,128)(2,1)}, f32[32...) custom-call(s32[4]{0:T(128)S(1)} %pad_add_fusion.meta, bf16[2,512,512]{2,1,0:T(8,128)(2,1)S(1)} %collective-permute-done.1.outer, ...), custom_call_target="tpu_custom_call" | custom-call | tf_op jit(solution)/shard_map/pallas_call | solution.py:543
  (2 shorter events, 0.1 us)
Async XLA Ops:
  1.4 13.0 %collective-permute-start = (bf16[64,512]{1,0:T(8,128)(2,1)S(1)}, bf16[64,512]{1,0:T(8,128)(2,1)S(1)}, u32[]{:S(2)}, u32[]{:S(2)}) collective-permute-start(bf16[64,512]{1,0:T(8,128)(2,1)S(1)} %shard_map.171.w_d), channel_id=1, source_target_pairs={{0,496},{16,480},{32,464},{48,448},{64,432},{80,416},{96,400},{112... | collective-permute-start | bytes 196616 | tf_op jit(solution)/shard_map/ppermute | solution.py:460
  55.4 28.3 %collective-permute-start.1 = (bf16[2,512,512]{2,1,0:T(8,128)(2,1)S(1)}, bf16[2,512,512]{2,1,0:T(8,128)(2,1)S(1)}, u32[]{:S(2)}, u32[]{:S(2)}) collective-permute-start(bf16[2,512,512]{2,1,0:T(8,128)(2,1)S(1)} %get-tuple-element.116), channel_id=1, source_target_pairs={{16,32},{32,16},{48,64},{64,48},{80,96},{96,80},{112,128},{128,112... | collective-permute-start | bytes 3145736 | tf_op jit(solution)/shard_map/ppermute | solution.py:539
  61.0 22.7 %collective-permute-start.2 = (bf16[2,512,512]{2,1,0:T(8,128)(2,1)S(1)}, bf16[2,512,512]{2,1,0:T(8,128)(2,1)S(1)}, u32[]{:S(2)}, u32[]{:S(2)}) collective-permute-start(bf16[2,512,512]{2,1,0:T(8,128)(2,1)S(1)} %get-tuple-element.117), channel_id=1, source_target_pairs={{0,16},{16,0},{32,48},{48,32},{64,80},{80,64},{96,112},{112,96},{1... | collective-permute-start | bytes 3145736 | tf_op jit(solution)/shard_map/ppermute | solution.py:540
  67.2 16.5 %collective-permute-start.3 = (bf16[64,512]{1,0:T(8,128)(2,1)S(1)}, bf16[64,512]{1,0:T(8,128)(2,1)S(1)}, u32[]{:S(2)}, u32[]{:S(2)}) collective-permute-start(bf16[64,512]{1,0:T(8,128)(2,1)S(1)} %get-tuple-element.119), channel_id=1, source_target_pairs={{0,496},{16,480},{32,464},{48,448},{64,432},{80,416},{96,400},{112... | collective-permute-start | bytes 196616 | tf_op jit(solution)/shard_map/ppermute | solution.py:541
